TPU v7x, 512 devices: a whole 4x8x8 slice. The times are simulated.
512 devices in a mesh: dp: 64 (over y, z), tower: 2 (over x_hi), tensor: 4 (over x_lo, core).
Axes of the slice: x: 4 (x_hi: 2, x_lo: 2; x = x_hi * 2 + x_lo), y: 8, z: 8, core: 2. Of those that a mesh axis runs over, the one named last changes fastest.
Arguments:
- image_feats: bfloat16 [16384, 3200], P('dp', ('tower', 'tensor')), may hold values from -200 to 200
- text_feats: bfloat16 [16384, 4096], P('dp', ('tower', 'tensor')), may hold values from -200 to 200
- image_proj: bfloat16 [3200, 768], P(('tower', 'tensor')), may hold values from -0.109375 to 0.109375
- text_proj: bfloat16 [4096, 768], P(('tower', 'tensor')), may hold values from -0.09375 to 0.09375
- labels: int32 [16384], P('dp'), may hold values from 0 to 16383, as said below
- logit_scale: float32 [1], replicated, may hold values from 2 to 8
- logit_bias: float32 [1], replicated, may hold values from -4 to -1
Outputs:
- image_grad: bfloat16 [16384, 3200], P('dp', ('tower', 'tensor'))
- text_grad: bfloat16 [16384, 4096], P('dp', ('tower', 'tensor'))
- image_proj_grad: float32 [3200, 768], P(('tower', 'tensor'), 'dp')
- text_proj_grad: float32 [4096, 768], P(('tower', 'tensor'), 'dp')
Inputs may be any that keep to these rules, and one draw needn't show every extreme that they name: `labels`: an image row of block j (rows j * 256 to (j + 1) * 256 - 1) has its positive text row in block (j - k) mod 64 for some 0 <= k < 4.
All inputs are finite; a program needn't handle non-finite values.
Results may differ from a plain program's by a relative error of at most 0.03.
Values may be sent and summed in bfloat16 or wider, within the bound.
No kernel may reach another device: no remote copies, remote signals or barrier semaphores. Data moves between devices by JAX's collectives and lax.ppermute only.
A program may use at most 64 MiB of HBM per device.

v0:
```python
import jax
import jax.numpy as jnp
from jax import lax
from jax.sharding import PartitionSpec as P

STEPS = 4


norm_eps = 1e-06


def passed_along(value, axis, steps):
    count = lax.axis_size(axis)
    pairs = [(source, (source + steps) % count) for source in range(count)]
    return lax.ppermute(value, axis, pairs)


def unit_rows(summed):
    length = jnp.sqrt(jnp.sum(summed * summed, axis=1, keepdims=True) + norm_eps)
    return (summed / length, length)


def local_backward(feats, weights, unit, length, grad_embed):
    grad_summed = (
        (grad_embed - unit * jnp.sum(unit * grad_embed, axis=1, keepdims=True)) / length
    ).astype(jnp.bfloat16)
    weight_grad = lax.dot_general(
        feats, grad_summed, (((0,), (0,)), ((), ())), preferred_element_type=jnp.float32
    )
    feats_grad = lax.dot_general(
        grad_summed, weights, (((1,), (1,)), ((), ())), preferred_element_type=jnp.float32
    )
    return (weight_grad, feats_grad.astype(jnp.bfloat16))


def on_device(image_feats, text_feats, image_proj, text_proj, labels, logit_scale, logit_bias):
    groups = lax.axis_size(("tower", "tensor"))
    member = lax.axis_index(("tower", "tensor"))
    blocks = lax.axis_size("dp")
    anchor = lax.axis_index("dp")
    row_count = image_feats.shape[0]
    row_share = row_count // groups
    img_part = jnp.dot(image_feats, image_proj, preferred_element_type=jnp.float32).astype(
        jnp.bfloat16
    )
    txt_part = jnp.dot(text_feats, text_proj, preferred_element_type=jnp.float32).astype(
        jnp.bfloat16
    )
    img_summed, txt_summed = (
        lax.psum(img_part.astype(jnp.float32).astype(jnp.bfloat16), ("tower", "tensor")).astype(
            jnp.float32
        ),
        lax.psum(txt_part.astype(jnp.float32).astype(jnp.bfloat16), ("tower", "tensor")).astype(
            jnp.float32
        ),
    )
    img_unit, img_length = unit_rows(img_summed)
    txt_unit, txt_length = unit_rows(txt_summed)
    img_embed = img_unit.astype(jnp.bfloat16)
    txt_embed = txt_unit.astype(jnp.bfloat16)
    row_embed = lax.dynamic_slice_in_dim(img_embed, member * row_share, row_share, 0)
    row_labels = lax.dynamic_slice_in_dim(labels, member * row_share, row_share, 0)
    col_total = txt_embed.shape[0]
    col_ids = lax.iota(jnp.int32, col_total)
    scale_value = logit_scale[0]
    bias_value = logit_bias[0]
    row_grad = jnp.zeros((row_embed.shape[0], row_embed.shape[1]), jnp.float32)
    moving = txt_embed
    returned = jnp.zeros((col_total, txt_embed.shape[1]), jnp.float32)
    for offset in range(STEPS):
        if offset > 0:
            moving = passed_along(moving, "dp", 1)
        source = jnp.mod(anchor - offset, blocks)
        global_cols = source * row_count + col_ids
        polarity = jnp.where(row_labels[:, None] == global_cols[None, :], 1.0, -1.0).astype(
            jnp.float32
        )
        logits = (
            scale_value
            * lax.dot_general(
                row_embed, moving, (((1,), (1,)), ((), ())), preferred_element_type=jnp.float32
            )
            + bias_value
        )
        weights = (-scale_value * polarity * jax.nn.sigmoid(-polarity * logits) / row_count).astype(
            jnp.bfloat16
        )
        row_grad = row_grad + jnp.dot(weights, moving, preferred_element_type=jnp.float32)
        partial_value = lax.dot_general(
            weights, row_embed, (((0,), (0,)), ((), ())), preferred_element_type=jnp.float32
        )
        if offset == 0:
            returned = partial_value
        else:
            returned = returned + passed_along(
                partial_value.astype(jnp.bfloat16), "dp", -offset
            ).astype(partial_value.dtype)
    complete, spread = (row_grad, returned)
    whole = lax.all_gather(
        complete.astype(jnp.bfloat16), ("tower", "tensor"), axis=0, tiled=True
    ).astype(complete.dtype)
    summed_terms = lax.psum(spread.astype(jnp.bfloat16), ("tower", "tensor")).astype(jnp.float32)
    grad_img, grad_txt = (whole, summed_terms)
    img_wgrad, image_grad = local_backward(image_feats, image_proj, img_unit, img_length, grad_img)
    txt_wgrad, text_grad = local_backward(text_feats, text_proj, txt_unit, txt_length, grad_txt)
    image_proj_grad, text_proj_grad = (
        lax.psum_scatter(img_wgrad, "dp", scatter_dimension=1, tiled=True),
        lax.psum_scatter(txt_wgrad, "dp", scatter_dimension=1, tiled=True),
    )
    return (image_grad, text_grad, image_proj_grad, text_proj_grad)


def solution(mesh):
    placed = (
        P("dp", ("tower", "tensor")),
        P("dp", ("tower", "tensor")),
        P(("tower", "tensor"), None),
        P(("tower", "tensor"), None),
        P("dp"),
        P(),
        P(),
    )
    return jax.shard_map(
        on_device,
        mesh=mesh,
        in_specs=placed,
        out_specs=(
            P("dp", ("tower", "tensor")),
            P("dp", ("tower", "tensor")),
            P(("tower", "tensor"), "dp"),
            P(("tower", "tensor"), "dp"),
        ),
        check_vma=False,
    )
```

profile of v0, /device:TPU:6, one launch (start us, length us, event | category | flops | bytes accessed | tf_op | source)
XLA Modules:
  0.0 427.8 jit_solution(14043663975278347616)
XLA Ops:
  7.2 2.4 convolution_convert_fusion.4
  9.6 2.1 convolution_convert_fusion.3
  13.2 73.4 %all-reduce.12.cloned.1.call-done = (bf16[256,768]{1,0:T(8,128)(2,1)}, bf16[256,768]{1,0:T(8,128)(2,1)}) async-done(((bf16[256,768]{1,0:T(8,128)(2,1)}, bf16[256,768]{1,0:T(8,128)(2,1)}), (bf16[256,768]{1,0:T(8,128)(2,1)}, bf16[256,768]{1,0:T(8,128)(2,1)})) %all-reduce.12.cloned.1.call-update) | async-done | bytes 786448 | tf_op jit(solution)/shard_map/psum | solution.py:50
  90.3 3.6 collective-permute-start
  94.3 13.8 %collective-permute-done = bf16[256,768]{1,0:T(8,128)(2,1)S(1)} collective-permute-done((bf16[256,768]{1,0:T(8,128)(2,1)S(1)}, bf16[256,768]{1,0:T(8,128)(2,1)S(1)}, u32[]{:S(2)}, u32[]{:S(2)}) %collective-permute-start) | collective-permute-done | bytes 393248 | tf_op jit(solution)/shard_map/ppermute | solution.py:15
  108.1 1.9 collective-permute-start.1
  110.6 7.2 %collective-permute-start.3 = (bf16[256,768]{1,0:T(8,128)(2,1)S(1)}, bf16[256,768]{1,0:T(8,128)(2,1)S(1)}, u32[]{:S(2)}, u32[]{:S(2)}) collective-permute-start(bf16[256,768]{1,0:T(8,128)(2,1)S(1)} %convolution_convert_fusion.2), channel_id=1, source_target_pairs={{0,504},{8,0},{16,8},{24,16},{32,24},{40,32},{48,40},{56,48},{64,5... | collective-permute-start | bytes 1179656 | tf_op jit(solution)/shard_map/ppermute | solution.py:15
  118.1 6.4 %collective-permute-done.1 = bf16[256,768]{1,0:T(8,128)(2,1)S(1)} collective-permute-done((bf16[256,768]{1,0:T(8,128)(2,1)S(1)}, bf16[256,768]{1,0:T(8,128)(2,1)S(1)}, u32[]{:S(2)}, u32[]{:S(2)}) %collective-permute-start.1) | collective-permute-done | bytes 393248 | tf_op jit(solution)/shard_map/ppermute | solution.py:15
  124.5 1.9 collective-permute-start.2
  127.0 2.9 collective-permute-start.4
  130.1 9.9 %collective-permute-done.2 = bf16[256,768]{1,0:T(8,128)(2,1)S(1)} collective-permute-done((bf16[256,768]{1,0:T(8,128)(2,1)S(1)}, bf16[256,768]{1,0:T(8,128)(2,1)S(1)}, u32[]{:S(2)}, u32[]{:S(2)}) %collective-permute-start.2) | collective-permute-done | bytes 393248 | tf_op jit(solution)/shard_map/ppermute | solution.py:15
  140.7 13.0 %all_gather.3 = bf16[256,768]{1,0:T(8,128)(2,1)S(1)} all-gather(bf16[32,768]{1,0:T(8,128)(2,1)S(1)} %fusion.1), channel_id=1, replica_groups=mesh['dp'=64,'tower'=2,'tensor'=4] {'tower','tensor'}, dimensions={0}, use_global_device_ids=true | all-gather | bytes 442368 | tf_op jit(solution)/shard_map/all_gather | solution.py:99
  153.7 1.9 collective-permute-start.5
  156.2 32.0 %collective-permute-done.5 = bf16[256,768]{1,0:T(8,128)(2,1)S(1)} collective-permute-done((bf16[256,768]{1,0:T(8,128)(2,1)S(1)}, bf16[256,768]{1,0:T(8,128)(2,1)S(1)}, u32[]{:S(2)}, u32[]{:S(2)}) %collective-permute-start.5) | collective-permute-done | bytes 393248 | tf_op jit(solution)/shard_map/ppermute | solution.py:15
  190.7 63.6 %all-reduce.8.cloned.1.call-done = bf16[256,768]{1,0:T(8,128)(2,1)} async-done(((bf16[256,768]{1,0:T(8,128)(2,1)}), bf16[256,768]{1,0:T(8,128)(2,1)}) %all-reduce.8.cloned.1.call-update) | async-done | bytes 393232 | tf_op jit(solution)/shard_map/psum | solution.py:102
  257.3 73.8 %fusion = f32[512,16]{0,1:T(8,128)S(1)} fusion(f32[512,768]{0,1:T(8,128)S(1)} %convolution_bitcast_fusion), kind=kCustom, calls=%all-reduce-scatter | all-reduce-scatter fusion | flops 524289 | bytes 1607680
  331.1 4.0 collective-permute-start.21
  335.1 3.7 collective-permute-start.20
  338.8 5.7 %collective-permute-start.19 = (f32[512,16]{0,1:T(8,128)S(1)}, f32[512,16]{0,1:T(8,128)S(1)}, u32[]{:S(2)}, u32[]{:S(2)}) collective-permute-start(f32[512,16]{0,1:T(8,128)S(1)} %fusion), channel_id=1, source_target_pairs={{0,112},{8,120},{16,128},{24,136},{32,144},{40,152},{48,160},{56,1... | collective-permute-start | bytes 98312
  344.5 3.4 collective-permute-start.18
  348.0 4.9 %collective-permute-start.17 = (f32[512,16]{0,1:T(8,128)S(1)}, f32[512,16]{0,1:T(8,128)S(1)}, u32[]{:S(2)}, u32[]{:S(2)}) collective-permute-start(f32[512,16]{0,1:T(8,128)S(1)} %fusion), channel_id=1, source_target_pairs={{0,96},{8,104},{16,112},{24,120},{32,128},{40,136},{48,144},{56,15... | collective-permute-start | bytes 98312
  356.1 4.6 %collective-permute-start.15 = (f32[512,16]{0,1:T(8,128)S(1)}, f32[512,16]{0,1:T(8,128)S(1)}, u32[]{:S(2)}, u32[]{:S(2)}) collective-permute-start(f32[512,16]{0,1:T(8,128)S(1)} %fusion), channel_id=1, source_target_pairs={{0,80},{8,88},{16,96},{24,104},{32,112},{40,120},{48,128},{56,136}... | collective-permute-start | bytes 98312
  363.3 3.0 collective-permute-start.12
  366.3 3.1 collective-permute-start.11
  369.4 2.1 convolution_convert_fusion.6
  371.5 4.0 collective-permute-start.10
  375.5 4.0 collective-permute-start.9
  379.6 2.2 collective-permute-start.8
  381.8 4.4 %collective-permute-start.7 = (f32[512,16]{0,1:T(8,128)S(1)}, f32[512,16]{0,1:T(8,128)S(1)}, u32[]{:S(2)}, u32[]{:S(2)}) collective-permute-start(f32[512,16]{0,1:T(8,128)S(1)} %fusion), channel_id=1, source_target_pairs={{0,16},{8,24},{16,32},{24,40},{32,48},{40,56},{48,64},{56,72},{64,... | collective-permute-start | bytes 98312
  386.2 2.3 collective-permute-start.6
  390.1 1.9 concatenate
  392.6 26.7 %all-reduce.10.cloned.1.call-done = f32[400,768]{1,0:T(8,128)} async-done(((f32[400,768]{1,0:T(8,128)}), f32[400,768]{1,0:T(8,128)}) %all-reduce.10.cloned.1.call-update) | async-done | bytes 1228816
  (76 shorter events, 21.1 us)
Async XLA Ops:
  7.2 2.4 copy-start
  7.2 5.9 %copy-start.6 = (s32[256]{0:T(256)S(1)}, s32[256]{0:T(256)}, u32[]{:S(2)}) copy-start(s32[256]{0:T(256)} %param.11) | copy-start | bytes 3076
  7.2 79.4 %all-reduce.12.cloned.1.call-start = ((), (), s32[]{:S(2)}) async-start(), calls=%async_computation.2 | async-start | bytes 1572864 | tf_op jit(solution)/shard_map/psum | solution.py:50
  11.7 242.6 %all-reduce.8.cloned.1.call-start = ((), (), s32[]{:S(2)}) async-start(), calls=%async_computation | async-start | bytes 786432 | tf_op jit(solution)/shard_map/psum | solution.py:102
  86.6 3.5 copy-start.2
  90.3 17.8 %collective-permute-start = (bf16[256,768]{1,0:T(8,128)(2,1)S(1)}, bf16[256,768]{1,0:T(8,128)(2,1)S(1)}, u32[]{:S(2)}, u32[]{:S(2)}) collective-permute-start(bf16[256,768]{1,0:T(8,128)(2,1)S(1)} %fusion.46), channel_id=1, source_target_pairs={{0,8},{8,16},{16,24},{24,32},{32,40},{40,48},{48,56},{56,64},{64,7... | collective-permute-start | bytes 1179656 | tf_op jit(solution)/shard_map/ppermute | solution.py:15
  108.1 16.3 %collective-permute-start.1 = (bf16[256,768]{1,0:T(8,128)(2,1)S(1)}, bf16[256,768]{1,0:T(8,128)(2,1)S(1)}, u32[]{:S(2)}, u32[]{:S(2)}) collective-permute-start(bf16[256,768]{1,0:T(8,128)(2,1)S(1)} %collective-permute-done), channel_id=1, source_target_pairs={{0,8},{8,16},{16,24},{24,32},{32,40},{40,48},{48,56},{56,64},{64,7... | collective-permute-start | bytes 1179656 | tf_op jit(solution)/shard_map/ppermute | solution.py:15
  110.6 45.5 %collective-permute-start.3 = (bf16[256,768]{1,0:T(8,128)(2,1)S(1)}, bf16[256,768]{1,0:T(8,128)(2,1)S(1)}, u32[]{:S(2)}, u32[]{:S(2)}) collective-permute-start(bf16[256,768]{1,0:T(8,128)(2,1)S(1)} %convolution_convert_fusion.2), channel_id=1, source_target_pairs={{0,504},{8,0},{16,8},{24,16},{32,24},{40,32},{48,40},{56,48},{64,5... | collective-permute-start | bytes 1179656 | tf_op jit(solution)/shard_map/ppermute | solution.py:15
  124.5 15.5 %collective-permute-start.2 = (bf16[256,768]{1,0:T(8,128)(2,1)S(1)}, bf16[256,768]{1,0:T(8,128)(2,1)S(1)}, u32[]{:S(2)}, u32[]{:S(2)}) collective-permute-start(bf16[256,768]{1,0:T(8,128)(2,1)S(1)} %collective-permute-done.1), channel_id=1, source_target_pairs={{0,8},{8,16},{16,24},{24,32},{32,40},{40,48},{48,56},{56,64},{64,7... | collective-permute-start | bytes 1179656 | tf_op jit(solution)/shard_map/ppermute | solution.py:15
  127.0 29.2 %collective-permute-start.4 = (bf16[256,768]{1,0:T(8,128)(2,1)S(1)}, bf16[256,768]{1,0:T(8,128)(2,1)S(1)}, u32[]{:S(2)}, u32[]{:S(2)}) collective-permute-start(bf16[256,768]{1,0:T(8,128)(2,1)S(1)} %convolution_convert_fusion.1), channel_id=1, source_target_pairs={{0,496},{8,504},{16,0},{24,8},{32,16},{40,24},{48,32},{56,40},{64,... | collective-permute-start | bytes 1179656 | tf_op jit(solution)/shard_map/ppermute | solution.py:15
  153.7 34.4 %collective-permute-start.5 = (bf16[256,768]{1,0:T(8,128)(2,1)S(1)}, bf16[256,768]{1,0:T(8,128)(2,1)S(1)}, u32[]{:S(2)}, u32[]{:S(2)}) collective-permute-start(bf16[256,768]{1,0:T(8,128)(2,1)S(1)} %convolution_convert_fusion), channel_id=1, source_target_pairs={{0,488},{8,496},{16,504},{24,0},{32,8},{40,16},{48,24},{56,32},{64... | collective-permute-start | bytes 1179656 | tf_op jit(solution)/shard_map/ppermute | solution.py:15
  155.9 33.4 %copy-start.4 = (bf16[256,400]{0,1:T(8,128)(2,1)S(1)}, bf16[256,400]{0,1:T(8,128)(2,1)}, u32[]{:S(2)}) copy-start(bf16[256,400]{0,1:T(8,128)(2,1)} %param.7) | copy-start | bytes 614404
  189.3 65.1 %copy-start.1 = (bf16[256,768]{1,0:T(8,128)(2,1)S(1)}, bf16[256,768]{1,0:T(8,128)(2,1)}, u32[]{:S(2)}) copy-start(bf16[256,768]{1,0:T(8,128)(2,1)} %get-tuple-element.13) | copy-start | bytes 1179652
  189.3 230.1 %all-reduce.10.cloned.1.call-start = ((), (), s32[]{:S(2)}) async-start(), calls=%async_computation.1 | async-start | bytes 2457600
  190.7 66.2 %copy-start.3 = (bf16[256,512]{1,0:T(8,128)(2,1)S(1)}, bf16[256,512]{1,0:T(8,128)(2,1)}, u32[]{:S(2)}) copy-start(bf16[256,512]{1,0:T(8,128)(2,1)} %param.8) | copy-start | bytes 786436
  256.9 97.3 %copy-start.5 = (u32[512]{0:T(512)S(1)}, u32[512]{0:T(512)}, u32[]{:S(2)}) copy-start(u32[512]{0:T(512)} %constant.72) | copy-start | bytes 6148
  331.1 21.8 %collective-permute-start.21 = (f32[512,12]{0,1:T(8,128)S(1)}, f32[512,12]{0,1:T(8,128)S(1)}, u32[]{:S(2)}, u32[]{:S(2)}) collective-permute-start(f32[512,12]{0,1:T(8,128)S(1)} %slice), channel_id=1, source_target_pairs={{0,128},{8,136},{16,144},{24,152},{32,160},{40,168},{48,176},{56,1... | collective-permute-start | bytes 73736
  335.1 21.0 %collective-permute-start.20 = (f32[512,16]{0,1:T(8,128)S(1)}, f32[512,16]{0,1:T(8,128)S(1)}, u32[]{:S(2)}, u32[]{:S(2)}) collective-permute-start(f32[512,16]{0,1:T(8,128)S(1)} %fusion), channel_id=1, source_target_pairs={{0,120},{8,128},{16,136},{24,144},{32,152},{40,160},{48,168},{56,1... | collective-permute-start | bytes 98312
  338.8 21.9 %collective-permute-start.19 = (f32[512,16]{0,1:T(8,128)S(1)}, f32[512,16]{0,1:T(8,128)S(1)}, u32[]{:S(2)}, u32[]{:S(2)}) collective-permute-start(f32[512,16]{0,1:T(8,128)S(1)} %fusion), channel_id=1, source_target_pairs={{0,112},{8,120},{16,128},{24,136},{32,144},{40,152},{48,160},{56,1... | collective-permute-start | bytes 98312
  344.5 17.5 %collective-permute-start.18 = (f32[512,16]{0,1:T(8,128)S(1)}, f32[512,16]{0,1:T(8,128)S(1)}, u32[]{:S(2)}, u32[]{:S(2)}) collective-permute-start(f32[512,16]{0,1:T(8,128)S(1)} %fusion), channel_id=1, source_target_pairs={{0,104},{8,112},{16,120},{24,128},{32,136},{40,144},{48,152},{56,1... | collective-permute-start | bytes 98312
  348.0 15.3 %collective-permute-start.17 = (f32[512,16]{0,1:T(8,128)S(1)}, f32[512,16]{0,1:T(8,128)S(1)}, u32[]{:S(2)}, u32[]{:S(2)}) collective-permute-start(f32[512,16]{0,1:T(8,128)S(1)} %fusion), channel_id=1, source_target_pairs={{0,96},{8,104},{16,112},{24,120},{32,128},{40,136},{48,144},{56,15... | collective-permute-start | bytes 98312
  352.9 13.4 %collective-permute-start.16 = (f32[512,16]{0,1:T(8,128)S(1)}, f32[512,16]{0,1:T(8,128)S(1)}, u32[]{:S(2)}, u32[]{:S(2)}) collective-permute-start(f32[512,16]{0,1:T(8,128)S(1)} %fusion), channel_id=1, source_target_pairs={{0,88},{8,96},{16,104},{24,112},{32,120},{40,128},{48,136},{56,144... | collective-permute-start | bytes 98312
  356.1 15.4 %collective-permute-start.15 = (f32[512,16]{0,1:T(8,128)S(1)}, f32[512,16]{0,1:T(8,128)S(1)}, u32[]{:S(2)}, u32[]{:S(2)}) collective-permute-start(f32[512,16]{0,1:T(8,128)S(1)} %fusion), channel_id=1, source_target_pairs={{0,80},{8,88},{16,96},{24,104},{32,112},{40,120},{48,128},{56,136}... | collective-permute-start | bytes 98312
  360.7 14.8 %collective-permute-start.14 = (f32[512,16]{0,1:T(8,128)S(1)}, f32[512,16]{0,1:T(8,128)S(1)}, u32[]{:S(2)}, u32[]{:S(2)}) collective-permute-start(f32[512,16]{0,1:T(8,128)S(1)} %fusion), channel_id=1, source_target_pairs={{0,72},{8,80},{16,88},{24,96},{32,104},{40,112},{48,120},{56,128},... | collective-permute-start | bytes 98312
  362.0 17.6 %collective-permute-start.13 = (f32[512,16]{0,1:T(8,128)S(1)}, f32[512,16]{0,1:T(8,128)S(1)}, u32[]{:S(2)}, u32[]{:S(2)}) collective-permute-start(f32[512,16]{0,1:T(8,128)S(1)} %fusion), channel_id=1, source_target_pairs={{0,64},{8,72},{16,80},{24,88},{32,96},{40,104},{48,112},{56,120},{... | collective-permute-start | bytes 98312
  363.3 18.4 %collective-permute-start.12 = (f32[512,16]{0,1:T(8,128)S(1)}, f32[512,16]{0,1:T(8,128)S(1)}, u32[]{:S(2)}, u32[]{:S(2)}) collective-permute-start(f32[512,16]{0,1:T(8,128)S(1)} %fusion), channel_id=1, source_target_pairs={{0,56},{8,64},{16,72},{24,80},{32,88},{40,96},{48,104},{56,112},{6... | collective-permute-start | bytes 98312
  366.3 19.9 %collective-permute-start.11 = (f32[512,16]{0,1:T(8,128)S(1)}, f32[512,16]{0,1:T(8,128)S(1)}, u32[]{:S(2)}, u32[]{:S(2)}) collective-permute-start(f32[512,16]{0,1:T(8,128)S(1)} %fusion), channel_id=1, source_target_pairs={{0,48},{8,56},{16,64},{24,72},{32,80},{40,88},{48,96},{56,104},{64... | collective-permute-start | bytes 98312
  371.5 18.1 %collective-permute-start.10 = (f32[512,16]{0,1:T(8,128)S(1)}, f32[512,16]{0,1:T(8,128)S(1)}, u32[]{:S(2)}, u32[]{:S(2)}) collective-permute-start(f32[512,16]{0,1:T(8,128)S(1)} %fusion), channel_id=1, source_target_pairs={{0,40},{8,48},{16,56},{24,64},{32,72},{40,80},{48,88},{56,96},{64,... | collective-permute-start | bytes 98312
  375.5 14.1 %collective-permute-start.9 = (f32[512,16]{0,1:T(8,128)S(1)}, f32[512,16]{0,1:T(8,128)S(1)}, u32[]{:S(2)}, u32[]{:S(2)}) collective-permute-start(f32[512,16]{0,1:T(8,128)S(1)} %fusion), channel_id=1, source_target_pairs={{0,32},{8,40},{16,48},{24,56},{32,64},{40,72},{48,80},{56,88},{64,... | collective-permute-start | bytes 98312
  379.6 10.0 %collective-permute-start.8 = (f32[512,16]{0,1:T(8,128)S(1)}, f32[512,16]{0,1:T(8,128)S(1)}, u32[]{:S(2)}, u32[]{:S(2)}) collective-permute-start(f32[512,16]{0,1:T(8,128)S(1)} %fusion), channel_id=1, source_target_pairs={{0,24},{8,32},{16,40},{24,48},{32,56},{40,64},{48,72},{56,80},{64,... | collective-permute-start | bytes 98312
  381.8 7.9 %collective-permute-start.7 = (f32[512,16]{0,1:T(8,128)S(1)}, f32[512,16]{0,1:T(8,128)S(1)}, u32[]{:S(2)}, u32[]{:S(2)}) collective-permute-start(f32[512,16]{0,1:T(8,128)S(1)} %fusion), channel_id=1, source_target_pairs={{0,16},{8,24},{16,32},{24,40},{32,48},{40,56},{48,64},{56,72},{64,... | collective-permute-start | bytes 98312
  386.2 3.9 collective-permute-start.6
Sparse Core Ops, SparseCore 0:
  11.8 74.7 all-reduce.11
  189.4 64.8 all-reduce.7
  257.6 161.6 all-reduce.9
where the time goes:
time: 429 us; the launch traced here: 428 us
  waiting for transfers between devices  226 us (53%)
  blocking collectives  86.8 us (20%)
  starting transfers between devices  72.7 us (17%)
  between operations  16.9 us (4%)
  matrix products  13.2 us (3%)
  other arithmetic  6.73 us (2%)
  local copies, waits for them, and re-layouts  5.08 us (1%)
    unnamed x1, blocking collectives  73.8 us
    psum x1, waiting for transfers between devices, on_device(): lax.psum(img_part.astype(jnp.float32).astype(jnp.bfloat16), ('tower', 'te...  73.4 us
    psum x1, waiting for transfers between devices, on_device(): lax.psum(spread.astype(jnp.bfloat16), ('tower', 'tensor'))  63.6 us
    ppermute x6, waiting for transfers between devices, passed_along(): return lax.ppermute(value, axis, pairs)  62.1 us
    unnamed x17, starting transfers between devices  53.2 us
    unnamed x20, waiting for transfers between devices  27.3 us
    ppermute x6, starting transfers between devices, passed_along(): return lax.ppermute(value, axis, pairs)  19.4 us
    all_gather x1, blocking collectives, on_device(): lax.all_gather(complete.astype(jnp.bfloat16), ('tower', 'tensor'), axis=0...  13 us
  transfers between devices with their start and end apart: 25, of which 8 were waited for; matrix products, arithmetic and copies ran while one was open for 21% of the time, Pallas kernels for 0%

commit v1 on v0

v1 whole, which is shorter than its diff:
```python
import jax
import jax.numpy as jnp
from jax import lax
from jax.sharding import Mesh, PartitionSpec as P

STEPS = 4
NORM_EPS = 1e-06
X = ("xh", "xl", "core")
DP = ("y", "z")


def shifted(value, steps):
    count = lax.axis_size(DP)
    pairs = [(source, (source + steps) % count) for source in range(count)]
    return lax.ppermute(value, DP, pairs)


def on_device(image_feats, text_feats, image_proj, text_proj, labels, logit_scale, logit_bias):
    bf16, f32 = jnp.bfloat16, jnp.float32
    groups = lax.axis_size(X)
    member = lax.axis_index(X)
    anchor = lax.axis_index(DP)
    blocks = lax.axis_size(DP)
    ny, nz = lax.axis_size("y"), lax.axis_size("z")
    rows = image_feats.shape[0]
    share = rows // groups
    d_img, d_txt = image_feats.shape[1], text_feats.shape[1]
    embed = image_proj.shape[1]
    img_line = lax.all_gather(image_feats, "y", axis=0, tiled=True)
    txt_line = lax.all_gather(text_feats, "y", axis=0, tiled=True)
    img_part = jnp.dot(image_feats, image_proj, preferred_element_type=f32).astype(bf16)
    txt_part = jnp.dot(text_feats, text_proj, preferred_element_type=f32).astype(bf16)
    parts = jnp.concatenate(
        [img_part.reshape(groups, share, embed), txt_part.reshape(groups, share, embed)], axis=1
    )
    parts = lax.all_to_all(parts, X, 0, 0, tiled=True)
    summed = jnp.sum(parts.astype(f32), axis=0)
    length = jnp.sqrt(jnp.sum(summed * summed, axis=1, keepdims=True) + NORM_EPS)
    unit = summed / length
    emb = unit.astype(bf16)
    img_own, txt_own = emb[:share], emb[share:]
    near = shifted(txt_own, 1)
    img_all = lax.all_gather(img_own, X, axis=0, tiled=True)
    pair = jnp.concatenate([txt_own, near])
    far = shifted(pair, 2)
    cols = jnp.concatenate([pair, far])
    offsets = jnp.arange(STEPS, dtype=jnp.int32)
    col_ids = (
        jnp.mod(anchor - offsets, blocks)[:, None] * rows
        + member * share
        + jnp.arange(share, dtype=jnp.int32)[None, :]
    ).reshape(-1)
    scale_value, bias_value = logit_scale[0], logit_bias[0]
    polarity = jnp.where(labels[:, None] == col_ids[None, :], 1.0, -1.0).astype(f32)
    logits = (
        scale_value
        * lax.dot_general(img_all, cols, (((1,), (1,)), ((), ())), preferred_element_type=f32)
        + bias_value
    )
    weights = (-scale_value * polarity * jax.nn.sigmoid(-polarity * logits) / rows).astype(bf16)
    txt_terms = lax.dot_general(weights, img_all, (((0,), (0,)), ((), ())), preferred_element_type=f32)
    img_terms = jnp.dot(weights, cols, preferred_element_type=f32).astype(bf16)
    back = shifted(txt_terms[2 * share :].astype(bf16), -2)
    img_terms = lax.all_to_all(img_terms.reshape(groups, share, embed), X, 0, 0, tiled=True)
    two = txt_terms[: 2 * share] + back.astype(f32)
    last = shifted(two[share:].astype(bf16), -1)
    grad_txt = two[:share] + last.astype(f32)
    grad_img = jnp.sum(img_terms.astype(f32), axis=0)
    grad = jnp.concatenate([grad_img, grad_txt])
    grad_summed = ((grad - unit * jnp.sum(unit * grad, axis=1, keepdims=True)) / length).astype(bf16)
    wide = embed // ny
    by_cols = grad_summed.reshape(2 * share, ny, wide).transpose(1, 0, 2)
    by_cols = lax.all_to_all(by_cols, "y", 0, 0, tiled=True)
    by_cols = by_cols.transpose(1, 0, 2).reshape(2 * share, embed)
    both = lax.all_gather(jnp.concatenate([grad_summed, by_cols]), X, axis=0, tiled=False)
    img_rows = both[:, :share].reshape(rows, embed)
    txt_rows = both[:, share : 2 * share].reshape(rows, embed)

    def line(part):
        return part.reshape(groups * share, ny, wide).transpose(1, 0, 2).reshape(ny * rows, wide)

    img_cols = line(both[:, 2 * share : 3 * share])
    txt_cols = line(both[:, 3 * share :])
    down = (((0,), (0,)), ((), ()))
    img_wgrad = lax.dot_general(img_cols, img_line, down, preferred_element_type=f32)
    txt_wgrad = lax.dot_general(txt_cols, txt_line, down, preferred_element_type=f32)
    wgrad = jnp.concatenate([img_wgrad, txt_wgrad], axis=1).astype(bf16)
    wgrad = lax.all_to_all(wgrad.reshape(nz, wide // nz, d_img + d_txt), "z", 0, 0, tiled=True)
    wgrad = jnp.sum(wgrad.astype(f32), axis=0)
    across = (((1,), (1,)), ((), ()))
    image_grad = lax.dot_general(img_rows, image_proj, across, preferred_element_type=f32).astype(bf16)
    text_grad = lax.dot_general(txt_rows, text_proj, across, preferred_element_type=f32).astype(bf16)
    return (image_grad, text_grad, wgrad[:, :d_img].T, wgrad[:, d_img:].T)


def solution(mesh):
    fine = Mesh(mesh.devices.reshape(8, 8, 2, 2, 2), ("y", "z", "xh", "xl", "core"))
    placed = (P(DP, X), P(DP, X), P(X, None), P(X, None), P(DP), P(), P())
    return jax.shard_map(
        on_device,
        mesh=fine,
        in_specs=placed,
        out_specs=(P(DP, X), P(DP, X), P(X, DP), P(X, DP)),
        check_vma=False,
    )
```

time: 429 us -> 241 us (0.56)
  waiting for transfers between devices: 226 us -> 150 us
  blocking collectives: 86.8 us -> 13 us
  starting transfers between devices: 72.7 us -> 40.4 us
    psum x2 -> x0, waiting for transfers between devices: 137 us -> none  [the longest x1 73.4 us: on_device(): lax.psum(img_part.astype(jnp.float32).astype(jnp.bfloat16), ('tower', 'te...]
    all_gather x0 -> x3, waiting for transfers between devices: none -> 108 us  [the longest x1 46 us: on_device(): img_line = lax.all_gather(image_feats, 'y', axis=0, tiled=True)]
    unnamed x1 -> x0, blocking collectives: 73.8 us -> none
    unnamed x17 -> x0, starting transfers between devices: 53.2 us -> none
    ppermute x6 -> x4, waiting for transfers between devices: 62.1 us -> 11.9 us  [shifted(): return lax.ppermute(value, DP, pairs)]
    all_to_all x0 -> x4, waiting for transfers between devices: none -> 29 us  [the longest x1 11.1 us: on_device(): parts = lax.all_to_all(parts, X, 0, 0, tiled=True)]
    all_to_all x0 -> x4, starting transfers between devices: none -> 26.4 us  [the longest x1 9.46 us: on_device(): parts = lax.all_to_all(parts, X, 0, 0, tiled=True)]
    unnamed x20 -> x3, waiting for transfers between devices: 27.3 us -> 1.39 us
  transfers between devices with their start and end apart: 25 -> 11, of which waited for: 8 -> 9; matrix products, arithmetic and copies ran while one was open for 21% -> 4% of each run, Pallas kernels for 0% -> 0%
where the time goes in v1:
time: 241 us; the launch traced here: 240 us
  waiting for transfers between devices  150 us (62%)
  starting transfers between devices  40.4 us (17%)
  between operations  15.3 us (6%)
  blocking collectives  13 us (5%)
  matrix products  10.6 us (4%)
  local copies, waits for them, and re-layouts  7.11 us (3%)
  other arithmetic  4.09 us (2%)
    all_gather x1, waiting for transfers between devices, on_device(): img_line = lax.all_gather(image_feats, 'y', axis=0, tiled=True)  46 us
    all_gather x1, waiting for transfers between devices, on_device(): txt_line = lax.all_gather(text_feats, 'y', axis=0, tiled=True)  43.5 us
    all_gather x1, waiting for transfers between devices, on_device(): lax.all_gather(jnp.concatenate([grad_summed, by_cols]), X, axis=0, tiled=...  18.2 us
    ppermute x4, starting transfers between devices, shifted(): return lax.ppermute(value, DP, pairs)  13.9 us
    all_gather x1, blocking collectives, on_device(): img_all = lax.all_gather(img_own, X, axis=0, tiled=True)  13 us
    ppermute x4, waiting for transfers between devices, shifted(): return lax.ppermute(value, DP, pairs)  11.9 us
    all_to_all x1, waiting for transfers between devices, on_device(): parts = lax.all_to_all(parts, X, 0, 0, tiled=True)  11.1 us
    all_to_all x1, starting transfers between devices, on_device(): parts = lax.all_to_all(parts, X, 0, 0, tiled=True)  9.46 us
  transfers between devices with their start and end apart: 11, of which 9 were waited for; matrix products, arithmetic and copies ran while one was open for 4% of the time, Pallas kernels for 0%

profile of v1, /device:TPU:6, one launch (start us, length us, event | category | flops | bytes accessed | tf_op | source)
XLA Modules:
  0.0 240.4 jit_solution(3432211264541536633)
XLA Ops:
  7.2 1.1 copy-done
  8.3 1.3 convolution_convert_fusion.1
  9.6 1.6 convolution_convert_fusion.2
  11.2 0.9 pad_maximum_fusion
  12.2 9.5 %all-to-all-start = ((bf16[8,64,768]{2,1,0:T(8,128)(2,1)}), bf16[8,64,768]{2,1,0:T(8,128)(2,1)S(1)}, u32[]{:S(2)}, u32[]{:S(2)}) async-start(bf16[8,64,768]{2,1,0:T(8,128)(2,1)} %pad_maximum_fusion), calls=%async_computation | async-start | bytes 1572864 | tf_op jit(solution)/shard_map/all_to_all | solution.py:36
  21.6 11.1 %all-to-all-done = bf16[8,64,768]{2,1,0:T(8,128)(2,1)S(1)} async-done(((bf16[8,64,768]{2,1,0:T(8,128)(2,1)}), bf16[8,64,768]{2,1,0:T(8,128)(2,1)S(1)}, u32[]{:S(2)}, u32[]{:S(2)}) %all-to-all-start) | async-done | bytes 786464 | tf_op jit(solution)/shard_map/all_to_all | solution.py:36
  33.0 1.9 collective-permute-start
  36.4 8.0 %collective-permute-done = bf16[32,768]{1,0:T(8,128)(2,1)S(1)} collective-permute-done((bf16[32,768]{1,0:T(8,128)(2,1)S(1)}, bf16[32,768]{1,0:T(8,128)(2,1)S(1)}, u32[]{:S(2)}, u32[]{:S(2)}) %collective-permute-start) | collective-permute-done | bytes 49184 | tf_op jit(solution)/shard_map/ppermute | solution.py:15
  44.4 1.9 collective-permute-start.1
  46.4 13.0 %all_gather.15 = bf16[256,768]{1,0:T(8,128)(2,1)S(1)} all-gather(bf16[32,768]{1,0:T(8,128)(2,1)S(1)} %get-tuple-element.9), channel_id=1, replica_groups=mesh['y'=8,'z'=8,'xh'=2,'xl'=2,'core'=2] {'xh','xl','core'}, dimensions={0}, use_global_device_ids=true | all-gather | bytes 442368 | tf_op jit(solution)/shard_map/all_gather | solution.py:43
  59.9 8.1 %collective-permute-start.2 = (bf16[64,768]{1,0:T(8,128)(2,1)S(1)}, bf16[64,768]{1,0:T(8,128)(2,1)S(1)}, u32[]{:S(2)}, u32[]{:S(2)}) collective-permute-start(bf16[64,768]{1,0:T(8,128)(2,1)S(1)} %slice.68), channel_id=1, source_target_pairs={{0,496},{8,504},{16,0},{24,8},{32,16},{40,24},{48,32},{56,40},{64,... | collective-permute-start | bytes 294920 | tf_op jit(solution)/shard_map/ppermute | solution.py:15
  68.0 1.0 convolution_convert_fusion
  69.0 5.5 %all-to-all-start.1 = ((bf16[8,32,768]{2,1,0:T(8,128)(2,1)}), bf16[8,32,768]{2,1,0:T(8,128)(2,1)S(1)}, u32[]{:S(2)}, u32[]{:S(2)}) async-start(bf16[8,32,768]{2,1,0:T(8,128)(2,1)} %bitcast.4), calls=%async_computation.1 | async-start | bytes 786432 | tf_op jit(solution)/shard_map/all_to_all | solution.py:64
  74.5 1.9 collective-permute-start.3
  76.6 3.9 %collective-permute-done.3 = bf16[32,768]{1,0:T(8,128)(2,1)S(1)} collective-permute-done((bf16[32,768]{1,0:T(8,128)(2,1)S(1)}, bf16[32,768]{1,0:T(8,128)(2,1)S(1)}, u32[]{:S(2)}, u32[]{:S(2)}) %collective-permute-start.3) | collective-permute-done | bytes 49184 | tf_op jit(solution)/shard_map/ppermute | solution.py:15
  81.7 0.8 fusion.22
  82.5 4.1 %all-to-all-start.2 = ((bf16[8,64,96]{2,1,0:T(8,128)(2,1)}), bf16[8,64,96]{2,1,0:T(8,128)(2,1)S(1)}, u32[]{:S(2)}, u32[]{:S(2)}) async-start(bf16[8,64,96]{2,1,0:T(8,128)(2,1)} %fusion.22), calls=%async_computation.2 | async-start | bytes 262144 | tf_op jit(solution)/shard_map/all_to_all | solution.py:73
  86.8 8.9 %all-to-all-done.2 = bf16[8,64,96]{2,1,0:T(8,128)(2,1)S(1)} async-done(((bf16[8,64,96]{2,1,0:T(8,128)(2,1)}), bf16[8,64,96]{2,1,0:T(8,128)(2,1)S(1)}, u32[]{:S(2)}, u32[]{:S(2)}) %all-to-all-start.2) | async-done | bytes 98336 | tf_op jit(solution)/shard_map/all_to_all | solution.py:73
  95.9 0.7 pad_maximum_fusion.4
  96.7 0.7 all-gather.7.cloned.1.call-update
  98.1 18.2 %all-gather.9.cloned.1.call-done = bf16[1024,768]{1,0:T(8,128)(2,1)} async-done(((bf16[128,768]{1,0:T(8,128)(2,1)}), bf16[1024,768]{1,0:T(8,128)(2,1)}) %all-gather.9.cloned.1.call-update) | async-done | bytes 1572880 | tf_op jit(solution)/shard_map/all_gather | solution.py:75
  116.3 1.5 fusion.29
  120.3 43.5 %all-gather.7.cloned.1.call-done = bf16[2048,512]{1,0:T(8,128)(2,1)} async-done(((bf16[256,512]{1,0:T(8,128)(2,1)}), bf16[2048,512]{1,0:T(8,128)(2,1)}) %all-gather.7.cloned.1.call-update) | async-done | bytes 2097168 | tf_op jit(solution)/shard_map/all_gather | solution.py:30
  163.8 2.0 fusion.4
  165.8 46.0 %all-gather.5.cloned.1.call-done = bf16[2048,400]{0,1:T(8,128)(2,1)} async-done(((bf16[256,400]{0,1:T(8,128)(2,1)}), bf16[2048,400]{0,1:T(8,128)(2,1)}) %all-gather.5.cloned.1.call-update) | async-done | bytes 1638416 | tf_op jit(solution)/shard_map/all_gather | solution.py:29
  211.8 2.0 fusion.7
  213.9 0.8 pad_maximum_fusion.1
  214.7 7.4 %all-to-all-start.3 = ((bf16[8,12,912]{2,1,0:T(8,128)(2,1)}), bf16[8,12,912]{2,1,0:T(8,128)(2,1)S(1)}, u32[]{:S(2)}, u32[]{:S(2)}) async-start(bf16[8,12,912]{2,1,0:T(8,128)(2,1)} %pad_maximum_fusion.1), calls=%async_computation.3 | async-start | bytes 524288 | tf_op jit(solution)/shard_map/all_to_all | solution.py:88
  222.1 1.0 convolution_convert_fusion.4
  223.1 1.1 convolution_convert_fusion.3
  224.2 8.3 %all-to-all-done.3 = bf16[8,12,912]{2,1,0:T(8,128)(2,1)S(1)} async-done(((bf16[8,12,912]{2,1,0:T(8,128)(2,1)}), bf16[8,12,912]{2,1,0:T(8,128)(2,1)S(1)}, u32[]{:S(2)}, u32[]{:S(2)}) %all-to-all-start.3) | async-done | bytes 175136 | tf_op jit(solution)/shard_map/all_to_all | solution.py:88
  233.2 0.7 slice_bitcast_fusion
  (48 shorter events, 6.7 us)
Async XLA Ops:
  7.2 1.1 copy-start
  12.2 47.2 %copy-start.2 = (s32[256]{0:T(256)S(1)}, s32[256]{0:T(256)}, u32[]{:S(2)}) copy-start(s32[256]{0:T(256)} %param.11) | copy-start | bytes 3076
  12.2 20.5 %all-to-all-start = ((bf16[8,64,768]{2,1,0:T(8,128)(2,1)}), bf16[8,64,768]{2,1,0:T(8,128)(2,1)S(1)}, u32[]{:S(2)}, u32[]{:S(2)}) async-start(bf16[8,64,768]{2,1,0:T(8,128)(2,1)} %pad_maximum_fusion), calls=%async_computation | async-start | bytes 1572864 | tf_op jit(solution)/shard_map/all_to_all | solution.py:36
  33.0 11.4 %collective-permute-start = (bf16[32,768]{1,0:T(8,128)(2,1)S(1)}, bf16[32,768]{1,0:T(8,128)(2,1)S(1)}, u32[]{:S(2)}, u32[]{:S(2)}) collective-permute-start(bf16[32,768]{1,0:T(8,128)(2,1)S(1)} %get-tuple-element.8), channel_id=1, source_target_pairs={{0,8},{8,16},{16,24},{24,32},{32,40},{40,48},{48,56},{56,64},{64,7... | collective-permute-start | bytes 147464 | tf_op jit(solution)/shard_map/ppermute | solution.py:15
  44.4 14.9 %collective-permute-start.1 = (bf16[64,768]{1,0:T(8,128)(2,1)S(1)}, bf16[64,768]{1,0:T(8,128)(2,1)S(1)}, u32[]{:S(2)}, u32[]{:S(2)}) collective-permute-start(bf16[64,768]{1,0:T(8,128)(2,1)S(1)} %pad_maximum_fusion.5), channel_id=1, source_target_pairs={{0,16},{8,24},{16,32},{24,40},{32,48},{40,56},{48,64},{56,72},{64,... | collective-permute-start | bytes 294920 | tf_op jit(solution)/shard_map/ppermute | solution.py:15
  59.9 14.6 %collective-permute-start.2 = (bf16[64,768]{1,0:T(8,128)(2,1)S(1)}, bf16[64,768]{1,0:T(8,128)(2,1)S(1)}, u32[]{:S(2)}, u32[]{:S(2)}) collective-permute-start(bf16[64,768]{1,0:T(8,128)(2,1)S(1)} %slice.68), channel_id=1, source_target_pairs={{0,496},{8,504},{16,0},{24,8},{32,16},{40,24},{48,32},{56,40},{64,... | collective-permute-start | bytes 294920 | tf_op jit(solution)/shard_map/ppermute | solution.py:15
  69.0 12.3 %all-to-all-start.1 = ((bf16[8,32,768]{2,1,0:T(8,128)(2,1)}), bf16[8,32,768]{2,1,0:T(8,128)(2,1)S(1)}, u32[]{:S(2)}, u32[]{:S(2)}) async-start(bf16[8,32,768]{2,1,0:T(8,128)(2,1)} %bitcast.4), calls=%async_computation.1 | async-start | bytes 786432 | tf_op jit(solution)/shard_map/all_to_all | solution.py:64
  74.5 6.0 %collective-permute-start.3 = (bf16[32,768]{1,0:T(8,128)(2,1)S(1)}, bf16[32,768]{1,0:T(8,128)(2,1)S(1)}, u32[]{:S(2)}, u32[]{:S(2)}) collective-permute-start(bf16[32,768]{1,0:T(8,128)(2,1)S(1)} %slice.69), channel_id=1, source_target_pairs={{0,504},{8,0},{16,8},{24,16},{32,24},{40,32},{48,40},{56,48},{64,5... | collective-permute-start | bytes 147464 | tf_op jit(solution)/shard_map/ppermute | solution.py:15
  82.5 13.2 %all-to-all-start.2 = ((bf16[8,64,96]{2,1,0:T(8,128)(2,1)}), bf16[8,64,96]{2,1,0:T(8,128)(2,1)S(1)}, u32[]{:S(2)}, u32[]{:S(2)}) async-start(bf16[8,64,96]{2,1,0:T(8,128)(2,1)} %fusion.22), calls=%async_computation.2 | async-start | bytes 262144 | tf_op jit(solution)/shard_map/all_to_all | solution.py:73
  86.6 29.7 %all-gather.9.cloned.1.call-start = ((), (), s32[]{:S(2)}) async-start(), calls=%async_computation.6 | async-start | bytes 1769472 | tf_op jit(solution)/shard_map/all_gather | solution.py:75
  96.6 67.1 %all-gather.7.cloned.1.call-start = ((), (), s32[]{:S(2)}) async-start(), calls=%async_computation.5 | async-start | bytes 2359296 | tf_op jit(solution)/shard_map/all_gather | solution.py:30
  97.4 114.4 %all-gather.5.cloned.1.call-start = ((), (), s32[]{:S(2)}) async-start(), calls=%async_computation.4 | async-start | bytes 1843200 | tf_op jit(solution)/shard_map/all_gather | solution.py:29
  165.8 56.3 %copy-start.1 = (bf16[400,768]{1,0:T(8,128)(2,1)S(1)}, bf16[400,768]{1,0:T(8,128)(2,1)}, u32[]{:S(2)}) copy-start(bf16[400,768]{1,0:T(8,128)(2,1)} %param.9) | copy-start | bytes 1843204
  214.7 17.9 %all-to-all-start.3 = ((bf16[8,12,912]{2,1,0:T(8,128)(2,1)}), bf16[8,12,912]{2,1,0:T(8,128)(2,1)S(1)}, u32[]{:S(2)}, u32[]{:S(2)}) async-start(bf16[8,12,912]{2,1,0:T(8,128)(2,1)} %pad_maximum_fusion.1), calls=%async_computation.3 | async-start | bytes 524288 | tf_op jit(solution)/shard_map/all_to_all | solution.py:88
Sparse Core Ops, SparseCore 0:
  96.8 19.4 all-gather.8
  118.4 45.3 all-gather.6
  165.8 45.9 all-gather.4

commit v2 on v1

v2 whole, which is shorter than its diff:
```python
import jax
import jax.numpy as jnp
from jax import lax
from jax.experimental import pallas as pl
from jax.experimental.pallas import tpu as pltpu
from jax.sharding import Mesh, PartitionSpec as P

STEPS = 4
NORM_EPS = 1e-06
X = ("xh", "xl", "core")
DP = ("y", "z")
ACROSS = (((1,), (1,)), ((), ()))
DOWN = (((0,), (0,)), ((), ()))
HALF = 256


def shifted(value, steps):
    count = lax.axis_size(DP)
    pairs = [(source, (source + steps) % count) for source in range(count)]
    return lax.ppermute(value, DP, pairs)


def project_kernel(img_t_ref, txt_ref, img_proj_ref, txt_proj_ref, parts_ref, pack_ref):
    f32, bf16 = jnp.float32, jnp.bfloat16
    groups, share = parts_ref.shape[0], parts_ref.shape[1] // 2
    d_txt, d_img = txt_ref.shape[1], img_t_ref.shape[0]
    for half in range(d_txt // HALF):
        pack_ref[half * HALF : (half + 1) * HALF] = txt_ref[:, half * HALF : (half + 1) * HALF]
    pack_ref[d_txt:] = img_t_ref[...]
    txt = jnp.dot(txt_ref[...], txt_proj_ref[...], preferred_element_type=f32).astype(bf16)
    img = lax.dot_general(img_t_ref[...], img_proj_ref[...], DOWN, preferred_element_type=f32)
    img = img.astype(bf16)
    for member in range(groups):
        rows = slice(member * share, (member + 1) * share)
        parts_ref[member, :share] = img[rows]
        parts_ref[member, share:] = txt[rows]


def project(image_feats_t, text_feats, image_proj, text_proj, groups):
    rows, d_txt = text_feats.shape
    d_img, embed = image_proj.shape
    return pl.pallas_call(
        project_kernel,
        out_shape=(
            jax.ShapeDtypeStruct((groups, 2 * rows // groups, embed), jnp.bfloat16),
            jax.ShapeDtypeStruct((d_txt + d_img, HALF), jnp.bfloat16),
        ),
        compiler_params=pltpu.CompilerParams(vmem_limit_bytes=58 * 1024 * 1024),
        cost_estimate=pl.CostEstimate(
            flops=2 * rows * (d_img + d_txt) * embed, bytes_accessed=4_000_000, transcendentals=0
        ),
        name="project",
    )(image_feats_t, text_feats, image_proj, text_proj)


def wgrad_kernel(cols_ref, line_ref, out_ref, total_ref):
    f32 = jnp.float32
    step = pl.program_id(0)
    groups, _, both, wide = cols_ref.shape
    share = both // 2
    d_all = total_ref.shape[1]
    d_txt = 2 * HALF

    @pl.when(step == 0)
    def _():
        total_ref[...] = jnp.zeros_like(total_ref)

    for k in range(line_ref.shape[0]):
        img_cols = cols_ref[:, k, :share].reshape(groups * share, wide)
        txt_cols = cols_ref[:, k, share:].reshape(groups * share, wide)
        total_ref[:, d_txt:] += lax.dot_general(
            img_cols, line_ref[k, d_txt:], (((0,), (1,)), ((), ())), preferred_element_type=f32
        )
        for half in range(d_txt // HALF):
            lanes = slice(half * HALF, (half + 1) * HALF)
            total_ref[:, lanes] += lax.dot_general(
                txt_cols,
                line_ref[k, half * HALF : (half + 1) * HALF],
                DOWN,
                preferred_element_type=f32,
            )

    @pl.when(step == pl.num_programs(0) - 1)
    def _():
        parts, padded, _ = out_ref.shape
        take = wide // parts
        for part in range(parts):
            out_ref[part, :take] = total_ref[part * take : (part + 1) * take].astype(out_ref.dtype)
            out_ref[part, take:] = jnp.zeros((padded - take, d_all), out_ref.dtype)


def project_grads(cols, line, parts):
    groups, ny, both, wide = cols.shape
    d_all = line.shape[1]
    padded = 16
    per = 2
    return pl.pallas_call(
        wgrad_kernel,
        grid=(ny // per,),
        in_specs=[
            pl.BlockSpec((groups, per, both, wide), lambda i: (0, i, 0, 0)),
            pl.BlockSpec((per, d_all, HALF), lambda i: (i, 0, 0)),
        ],
        out_specs=pl.BlockSpec((parts, padded, d_all), lambda i: (0, 0, 0)),
        out_shape=jax.ShapeDtypeStruct((parts, padded, d_all), jnp.bfloat16),
        scratch_shapes=[pltpu.VMEM((wide, d_all), jnp.float32)],
        compiler_params=pltpu.CompilerParams(vmem_limit_bytes=58 * 1024 * 1024),
        cost_estimate=pl.CostEstimate(
            flops=4 * ny * HALF * wide * d_all, bytes_accessed=5_000_000, transcendentals=0
        ),
        name="project_grads",
    )(cols, line)


def on_device(image_feats, text_feats, image_proj, text_proj, labels, logit_scale, logit_bias):
    bf16, f32 = jnp.bfloat16, jnp.float32
    groups = lax.axis_size(X)
    member = lax.axis_index(X)
    anchor = lax.axis_index(DP)
    blocks = lax.axis_size(DP)
    ny, nz = lax.axis_size("y"), lax.axis_size("z")
    rows = image_feats.shape[0]
    share = rows // groups
    d_img, d_txt = image_feats.shape[1], text_feats.shape[1]
    embed = image_proj.shape[1]
    parts, pack = project(image_feats.T, text_feats, image_proj, text_proj, groups)
    line = lax.all_gather(pack, "y", axis=0, tiled=False)
    parts = lax.all_to_all(parts, X, 0, 0, tiled=True)
    summed = jnp.sum(parts.astype(f32), axis=0)
    length = jnp.sqrt(jnp.sum(summed * summed, axis=1, keepdims=True) + NORM_EPS)
    unit = summed / length
    emb = unit.astype(bf16)
    img_own, txt_own = emb[:share], emb[share:]
    img_all = jnp.broadcast_to(img_own[None], (groups, share, embed))
    img_all = lax.all_to_all(img_all, X, 0, 0, tiled=True).reshape(rows, embed)
    near = shifted(txt_own, 1)
    pair = jnp.concatenate([txt_own, near])
    far = shifted(pair, 2)
    cols = jnp.concatenate([pair, far])
    offsets = jnp.arange(STEPS, dtype=jnp.int32)
    col_ids = (
        jnp.mod(anchor - offsets, blocks)[:, None] * rows
        + member * share
        + jnp.arange(share, dtype=jnp.int32)[None, :]
    ).reshape(-1)
    scale_value, bias_value = logit_scale[0], logit_bias[0]
    polarity = jnp.where(labels[:, None] == col_ids[None, :], 1.0, -1.0).astype(f32)
    logits = (
        scale_value * lax.dot_general(img_all, cols, ACROSS, preferred_element_type=f32)
        + bias_value
    )
    weights = (-scale_value * polarity * jax.nn.sigmoid(-polarity * logits) / rows).astype(bf16)
    txt_terms = lax.dot_general(weights, img_all, DOWN, preferred_element_type=f32)
    img_terms = jnp.dot(weights, cols, preferred_element_type=f32).astype(bf16)
    back = shifted(txt_terms[2 * share :].astype(bf16), -2)
    img_terms = lax.all_to_all(img_terms.reshape(groups, share, embed), X, 0, 0, tiled=True)
    two = txt_terms[: 2 * share] + back.astype(f32)
    last = shifted(two[share:].astype(bf16), -1)
    grad_txt = two[:share] + last.astype(f32)
    grad_img = jnp.sum(img_terms.astype(f32), axis=0)
    grad = jnp.concatenate([grad_img, grad_txt])
    grad_summed = ((grad - unit * jnp.sum(unit * grad, axis=1, keepdims=True)) / length).astype(bf16)
    wide = embed // ny
    by_cols = grad_summed.reshape(2 * share, ny, wide).transpose(1, 0, 2)
    by_cols = lax.all_to_all(by_cols, "y", 0, 0, tiled=True)
    padded = jnp.pad(grad_summed, ((0, share), (0, 0)))
    by_cols, padded, line = lax.optimization_barrier((by_cols, padded, line))
    cols_all = lax.all_gather(by_cols, X, axis=0, tiled=False)
    wgrad = project_grads(cols_all, line, nz)
    wgrad = lax.all_to_all(wgrad, "z", 0, 0, tiled=True)
    wgrad = jnp.sum(wgrad[:, : wide // nz].astype(f32), axis=0)
    rows_all = lax.all_gather(padded, X, axis=0, tiled=False)
    img_rows = rows_all[:, :share].reshape(rows, embed)
    txt_rows = rows_all[:, share : 2 * share].reshape(rows, embed)
    image_grad = lax.dot_general(img_rows, image_proj, ACROSS, preferred_element_type=f32).astype(bf16)
    text_grad = lax.dot_general(txt_rows, text_proj, ACROSS, preferred_element_type=f32).astype(bf16)
    return (image_grad, text_grad, wgrad[:, d_txt:].T, wgrad[:, :d_txt].T)


def solution(mesh):
    fine = Mesh(mesh.devices.reshape(8, 8, 2, 2, 2), ("y", "z", "xh", "xl", "core"))
    placed = (P(DP, X), P(DP, X), P(X, None), P(X, None), P(DP), P(), P())
    return jax.shard_map(
        on_device,
        mesh=fine,
        in_specs=placed,
        out_specs=(P(DP, X), P(DP, X), P(X, DP), P(X, DP)),
        check_vma=False,
    )
```

time: 241 us -> 139 us (0.58)
  the two profiles are of different devices: /device:TPU:6 before, /device:TPU:1 now
where the time goes in v2:
time: 139 us
  waiting for transfers between devices  37.5 us (27%)
  blocking collectives  34.4 us (25%)
  starting transfers between devices  34 us (24%)
  between operations  15.5 us (11%)
  Pallas kernels  7.55 us (5%)
  local copies, waits for them, and re-layouts  4.39 us (3%)
  matrix products  3.67 us (3%)
  other arithmetic  1.64 us (1%)
    all_gather x1, blocking collectives, on_device(): cols_all = lax.all_gather(by_cols, X, axis=0, tiled=False)  17.4 us
    all_to_all x1, blocking collectives, on_device(): wgrad = lax.all_to_all(wgrad, 'z', 0, 0, tiled=True)  17 us
    ppermute x4, waiting for transfers between devices, shifted(): return lax.ppermute(value, DP, pairs)  15.4 us
    all_to_all x1, waiting for transfers between devices, on_device(): parts = lax.all_to_all(parts, X, 0, 0, tiled=True)  12.3 us
    all_to_all x1, starting transfers between devices, on_device(): parts = lax.all_to_all(parts, X, 0, 0, tiled=True)  10.3 us
    ppermute x4, starting transfers between devices, shifted(): return lax.ppermute(value, DP, pairs)  9.42 us
    all_to_all x1, waiting for transfers between devices, on_device(): by_cols = lax.all_to_all(by_cols, 'y', 0, 0, tiled=True)  7.02 us
    all_to_all x1, starting transfers between devices, on_device(): lax.all_to_all(img_terms.reshape(groups, share, embed), X, 0, 0, tiled=True)  6.05 us
  transfers between devices with their start and end apart: 10, of which 6 were waited for; matrix products, arithmetic and copies ran while one was open for 5% of the time, Pallas kernels for 3%

profile of v2, /device:TPU:1, one launch (start us, length us, event | category | flops | bytes accessed | tf_op | source)
XLA Modules:
  0.0 138.6 jit_solution(5686917936263344454)
XLA Ops:
  7.2 3.1 %project.1 = (bf16[8,64,768]{2,1,0:T(8,128)(2,1)}, bf16[912,256]{1,0:T(8,128)(2,1)}) custom-call(bf16[400,256]{1,0:T(8,128)(2,1)} %bitcast.34, bf16[256,512]{1,0:T(8,128)(2,1)} %txt_ref.1, bf16[400,768]{1,0:T(8,128)(2,1)} %img_proj_ref.1, bf16[512,768]{1,0:T(8,128)(2,1)} %txt_proj_ref.1), custom_call_target="tpu_custom_call" | custom-call | flops 358612992 | bytes 4000000 | tf_op jit(solution)/shard_map/project/pallas_call | solution.py:42
  10.3 10.3 %all-to-all-start = ((bf16[8,64,768]{2,1,0:T(8,128)(2,1)}), bf16[8,64,768]{2,1,0:T(8,128)(2,1)S(1)}, u32[]{:S(2)}, u32[]{:S(2)}) async-start(bf16[8,64,768]{2,1,0:T(8,128)(2,1)} %get-tuple-element.9), calls=%async_computation | async-start | bytes 1572864 | tf_op jit(solution)/shard_map/all_to_all | solution.py:128
  20.7 12.3 %all-to-all-done = bf16[8,64,768]{2,1,0:T(8,128)(2,1)S(1)} async-done(((bf16[8,64,768]{2,1,0:T(8,128)(2,1)}), bf16[8,64,768]{2,1,0:T(8,128)(2,1)S(1)}, u32[]{:S(2)}, u32[]{:S(2)}) %all-to-all-start) | async-done | bytes 786464 | tf_op jit(solution)/shard_map/all_to_all | solution.py:128
  33.1 0.1 multiply_reduce_fusion.1
  33.3 1.9 %collective-permute-start = (bf16[32,768]{1,0:T(8,128)(2,1)S(1)}, bf16[32,768]{1,0:T(8,128)(2,1)S(1)}, u32[]{:S(2)}, u32[]{:S(2)}) collective-permute-start(bf16[32,768]{1,0:T(8,128)(2,1)S(1)} %get-tuple-element.16), channel_id=1, source_target_pairs={{0,8},{8,16},{16,24},{24,32},{32,40},{40,48},{48,56},{56,64},{64,7... | collective-permute-start | bytes 147464 | tf_op jit(solution)/shard_map/ppermute | solution.py:20
  35.2 0.8 broadcast_in_dim.12
  36.0 4.2 %all-to-all-start.1 = ((bf16[8,32,768]{2,1,0:T(8,128)(2,1)}), bf16[8,32,768]{2,1,0:T(8,128)(2,1)S(1)}, u32[]{:S(2)}, u32[]{:S(2)}) async-start(bf16[8,32,768]{2,1,0:T(8,128)(2,1)} %broadcast_in_dim.12), calls=%async_computation.1 | async-start | bytes 786432 | tf_op jit(solution)/shard_map/all_to_all | solution.py:135
  40.3 5.0 %collective-permute-done = bf16[32,768]{1,0:T(8,128)(2,1)S(1)} collective-permute-done((bf16[32,768]{1,0:T(8,128)(2,1)S(1)}, bf16[32,768]{1,0:T(8,128)(2,1)S(1)}, u32[]{:S(2)}, u32[]{:S(2)}) %collective-permute-start) | collective-permute-done | bytes 49184 | tf_op jit(solution)/shard_map/ppermute | solution.py:20
  45.3 1.9 %collective-permute-start.1 = (bf16[64,768]{1,0:T(8,128)(2,1)S(1)}, bf16[64,768]{1,0:T(8,128)(2,1)S(1)}, u32[]{:S(2)}, u32[]{:S(2)}) collective-permute-start(bf16[64,768]{1,0:T(8,128)(2,1)S(1)} %pad_maximum_fusion.2), channel_id=1, source_target_pairs={{0,16},{8,24},{16,32},{24,40},{32,48},{40,56},{48,64},{56,72},{64,... | collective-permute-start | bytes 294920 | tf_op jit(solution)/shard_map/ppermute | solution.py:20
  48.7 9.0 %collective-permute-done.1 = bf16[64,768]{1,0:T(8,128)(2,1)S(1)} collective-permute-done((bf16[64,768]{1,0:T(8,128)(2,1)S(1)}, bf16[64,768]{1,0:T(8,128)(2,1)S(1)}, u32[]{:S(2)}, u32[]{:S(2)}) %collective-permute-start.1) | collective-permute-done | bytes 98336 | tf_op jit(solution)/shard_map/ppermute | solution.py:20
  57.7 0.3 fusion.8
  58.0 0.2 fusion.21
  58.2 1.9 %collective-permute-start.2 = (bf16[64,768]{1,0:T(8,128)(2,1)S(1)}, bf16[64,768]{1,0:T(8,128)(2,1)S(1)}, u32[]{:S(2)}, u32[]{:S(2)}) collective-permute-start(bf16[64,768]{1,0:T(8,128)(2,1)S(1)} %slice.64), channel_id=1, source_target_pairs={{0,496},{8,504},{16,0},{24,8},{32,16},{40,24},{48,32},{56,40},{64,... | collective-permute-start | bytes 294920 | tf_op jit(solution)/shard_map/ppermute | solution.py:20
  60.2 1.0 convolution_convert_fusion
  61.2 6.1 %all-to-all-start.2 = ((bf16[8,32,768]{2,1,0:T(8,128)(2,1)}), bf16[8,32,768]{2,1,0:T(8,128)(2,1)S(1)}, u32[]{:S(2)}, u32[]{:S(2)}) async-start(bf16[8,32,768]{2,1,0:T(8,128)(2,1)} %bitcast.4), calls=%async_computation.2 | async-start | bytes 786432 | tf_op jit(solution)/shard_map/all_to_all | solution.py:156
  67.3 3.7 %collective-permute-start.3 = (bf16[32,768]{1,0:T(8,128)(2,1)S(1)}, bf16[32,768]{1,0:T(8,128)(2,1)S(1)}, u32[]{:S(2)}, u32[]{:S(2)}) collective-permute-start(bf16[32,768]{1,0:T(8,128)(2,1)S(1)} %slice.65), channel_id=1, source_target_pairs={{0,504},{8,0},{16,8},{24,16},{32,24},{40,32},{48,40},{56,48},{64,5... | collective-permute-start | bytes 147464 | tf_op jit(solution)/shard_map/ppermute | solution.py:20
  70.9 0.1 reduce_sum.50
  71.1 1.3 collective-permute-done.3
  72.6 2.7 %all-to-all-done.2 = bf16[8,32,768]{2,1,0:T(8,128)(2,1)S(1)} async-done(((bf16[8,32,768]{2,1,0:T(8,128)(2,1)}), bf16[8,32,768]{2,1,0:T(8,128)(2,1)S(1)}, u32[]{:S(2)}, u32[]{:S(2)}) %all-to-all-start.2) | async-done | bytes 393248 | tf_op jit(solution)/shard_map/all_to_all | solution.py:156
  75.5 0.2 multiply_reduce_fusion
  75.7 0.8 fusion.12
  76.5 3.9 %all-to-all-start.3 = ((bf16[8,64,96]{2,1,0:T(8,128)(2,1)}), bf16[8,64,96]{2,1,0:T(8,128)(2,1)S(1)}, u32[]{:S(2)}, u32[]{:S(2)}) async-start(bf16[8,64,96]{2,1,0:T(8,128)(2,1)} %fusion.12), calls=%async_computation.3 | async-start | bytes 262144 | tf_op jit(solution)/shard_map/all_to_all | solution.py:165
  80.6 0.7 pad.4
  81.3 7.0 %all-to-all-done.3 = bf16[8,64,96]{2,1,0:T(8,128)(2,1)S(1)} async-done(((bf16[8,64,96]{2,1,0:T(8,128)(2,1)}), bf16[8,64,96]{2,1,0:T(8,128)(2,1)S(1)}, u32[]{:S(2)}, u32[]{:S(2)}) %all-to-all-start.3) | async-done | bytes 98336 | tf_op jit(solution)/shard_map/all_to_all | solution.py:165
  88.3 17.4 %all-gather.2 = bf16[64,64,96]{2,1,0:T(8,128)(2,1)} all-gather(bf16[8,64,96]{2,1,0:T(8,128)(2,1)S(1)} %all-to-all-done.3), channel_id=4, replica_groups=mesh['y'=8,'z'=8,'xh'=2,'xl'=2,'core'=2] {'xh','xl','core'}, dimensions={0}, use_global_device_ids=true | all-gather | bytes 884736 | tf_op jit(solution)/shard_map/all_gather | solution.py:168
  105.7 4.5 %project_grads.1 = bf16[8,16,912]{2,1,0:T(8,128)(2,1)} custom-call(bf16[8,8,64,96]{3,2,1,0:T(8,128)(2,1)} %bitcast.27, bf16[8,912,256]{2,1,0:T(8,128)(2,1)} %bitcast.28), custom_call_target="tpu_custom_call" | custom-call | flops 717225984 | bytes 5000000 | tf_op jit(solution)/shard_map/project_grads/pallas_call | solution.py:97
  110.2 17.0 %all_to_all.25 = bf16[8,16,912]{2,1,0:T(8,128)(2,1)S(1)} all-to-all(bf16[8,16,912]{2,1,0:T(8,128)(2,1)} %project_grads.1), channel_id=1, replica_groups=mesh['y'=8,'z'=8,'xh'=2,'xl'=2,'core'=2] {'z'}, dimensions={0} | all-to-all | bytes 466944 | tf_op jit(solution)/shard_map/all_to_all | solution.py:170
  127.2 0.6 slice_bitcast_fusion
  127.8 0.6 slice_bitcast_fusion.1
  128.5 1.2 fusion.19
  129.6 1.1 convolution_convert_fusion.1
  130.7 1.0 convolution_convert_fusion.2
  (33 shorter events, 1.0 us)
Async XLA Ops:
  7.2 81.1 %all-gather.6.cloned.1.call-start = ((), (), s32[]{:S(2)}) async-start(), calls=%async_computation.5 | async-start | bytes 4202496 | tf_op jit(solution)/shard_map/all_gather | solution.py:127
  10.3 22.6 %all-to-all-start = ((bf16[8,64,768]{2,1,0:T(8,128)(2,1)}), bf16[8,64,768]{2,1,0:T(8,128)(2,1)S(1)}, u32[]{:S(2)}, u32[]{:S(2)}) async-start(bf16[8,64,768]{2,1,0:T(8,128)(2,1)} %get-tuple-element.9), calls=%async_computation | async-start | bytes 1572864 | tf_op jit(solution)/shard_map/all_to_all | solution.py:128
  20.7 37.0 %copy-start.2 = (s32[256]{0:T(256)S(1)}, s32[256]{0:T(256)}, u32[]{:S(2)}) copy-start(s32[256]{0:T(256)} %param.11) | copy-start | bytes 3076
  33.3 12.0 %collective-permute-start = (bf16[32,768]{1,0:T(8,128)(2,1)S(1)}, bf16[32,768]{1,0:T(8,128)(2,1)S(1)}, u32[]{:S(2)}, u32[]{:S(2)}) collective-permute-start(bf16[32,768]{1,0:T(8,128)(2,1)S(1)} %get-tuple-element.16), channel_id=1, source_target_pairs={{0,8},{8,16},{16,24},{24,32},{32,40},{40,48},{48,56},{56,64},{64,7... | collective-permute-start | bytes 147464 | tf_op jit(solution)/shard_map/ppermute | solution.py:20
  36.0 21.7 %all-to-all-start.1 = ((bf16[8,32,768]{2,1,0:T(8,128)(2,1)}), bf16[8,32,768]{2,1,0:T(8,128)(2,1)S(1)}, u32[]{:S(2)}, u32[]{:S(2)}) async-start(bf16[8,32,768]{2,1,0:T(8,128)(2,1)} %broadcast_in_dim.12), calls=%async_computation.1 | async-start | bytes 786432 | tf_op jit(solution)/shard_map/all_to_all | solution.py:135
  45.3 12.4 %collective-permute-start.1 = (bf16[64,768]{1,0:T(8,128)(2,1)S(1)}, bf16[64,768]{1,0:T(8,128)(2,1)S(1)}, u32[]{:S(2)}, u32[]{:S(2)}) collective-permute-start(bf16[64,768]{1,0:T(8,128)(2,1)S(1)} %pad_maximum_fusion.2), channel_id=1, source_target_pairs={{0,16},{8,24},{16,32},{24,40},{32,48},{40,56},{48,64},{56,72},{64,... | collective-permute-start | bytes 294920 | tf_op jit(solution)/shard_map/ppermute | solution.py:20
  58.2 9.0 %collective-permute-start.2 = (bf16[64,768]{1,0:T(8,128)(2,1)S(1)}, bf16[64,768]{1,0:T(8,128)(2,1)S(1)}, u32[]{:S(2)}, u32[]{:S(2)}) collective-permute-start(bf16[64,768]{1,0:T(8,128)(2,1)S(1)} %slice.64), channel_id=1, source_target_pairs={{0,496},{8,504},{16,0},{24,8},{32,16},{40,24},{48,32},{56,40},{64,... | collective-permute-start | bytes 294920 | tf_op jit(solution)/shard_map/ppermute | solution.py:20
  61.2 14.1 %all-to-all-start.2 = ((bf16[8,32,768]{2,1,0:T(8,128)(2,1)}), bf16[8,32,768]{2,1,0:T(8,128)(2,1)S(1)}, u32[]{:S(2)}, u32[]{:S(2)}) async-start(bf16[8,32,768]{2,1,0:T(8,128)(2,1)} %bitcast.4), calls=%async_computation.2 | async-start | bytes 786432 | tf_op jit(solution)/shard_map/all_to_all | solution.py:156
  67.3 5.1 %collective-permute-start.3 = (bf16[32,768]{1,0:T(8,128)(2,1)S(1)}, bf16[32,768]{1,0:T(8,128)(2,1)S(1)}, u32[]{:S(2)}, u32[]{:S(2)}) collective-permute-start(bf16[32,768]{1,0:T(8,128)(2,1)S(1)} %slice.65), channel_id=1, source_target_pairs={{0,504},{8,0},{16,8},{24,16},{32,24},{40,32},{48,40},{56,48},{64,5... | collective-permute-start | bytes 147464 | tf_op jit(solution)/shard_map/ppermute | solution.py:20
  76.5 11.8 %all-to-all-start.3 = ((bf16[8,64,96]{2,1,0:T(8,128)(2,1)}), bf16[8,64,96]{2,1,0:T(8,128)(2,1)S(1)}, u32[]{:S(2)}, u32[]{:S(2)}) async-start(bf16[8,64,96]{2,1,0:T(8,128)(2,1)} %fusion.12), calls=%async_computation.3 | async-start | bytes 262144 | tf_op jit(solution)/shard_map/all_to_all | solution.py:165
  80.4 48.0 %all-gather.8.cloned.1.call-start = ((), (), s32[]{:S(2)}) async-start(), calls=%async_computation.6 | async-start | bytes 1327104 | tf_op jit(solution)/shard_map/all_gather | solution.py:172
  110.2 19.5 %copy-start = (bf16[512,768]{1,0:T(8,128)(2,1)S(1)}, bf16[512,768]{1,0:T(8,128)(2,1)}, u32[]{:S(2)}) copy-start(bf16[512,768]{1,0:T(8,128)(2,1)} %txt_proj_ref.1) | copy-start | bytes 2359300
  127.2 3.5 %copy-start.1 = (bf16[400,768]{1,0:T(8,128)(2,1)S(1)}, bf16[400,768]{1,0:T(8,128)(2,1)}, u32[]{:S(2)}) copy-start(bf16[400,768]{1,0:T(8,128)(2,1)} %img_proj_ref.1) | copy-start | bytes 1843204
Sparse Core Ops, SparseCore 0:
  10.4 58.9 all-gather.5
  88.4 23.5 all-gather.7

commit v3 on v2

v3 whole, which is shorter than its diff:
```python
import jax
import jax.numpy as jnp
from jax import lax
from jax.experimental import pallas as pl
from jax.experimental.pallas import tpu as pltpu
from jax.sharding import Mesh, PartitionSpec as P

STEPS = 4
NORM_EPS = 1e-06
X = ("xh", "xl", "core")
DP = ("y", "z")
ACROSS = (((1,), (1,)), ((), ()))
DOWN = (((0,), (0,)), ((), ()))
HALF = 256
VMEM = 58 * 1024 * 1024


def shifted(value, steps):
    count = lax.axis_size(DP)
    pairs = [(source, (source + steps) % count) for source in range(count)]
    return lax.ppermute(value, DP, pairs)


def along(value, axis, steps):
    count = lax.axis_size(axis)
    return lax.ppermute(value, axis, [(source, (source + steps) % count) for source in range(count)])


def project_kernel(img_t_ref, txt_ref, img_proj_ref, txt_proj_ref, parts_ref, pack_ref):
    f32, bf16 = jnp.float32, jnp.bfloat16
    groups, share = parts_ref.shape[0], parts_ref.shape[1] // 2
    d_txt, d_img = txt_ref.shape[1], img_t_ref.shape[0]
    for half in range(d_txt // HALF):
        pack_ref[half * HALF : (half + 1) * HALF] = txt_ref[:, half * HALF : (half + 1) * HALF]
    pack_ref[d_txt:] = img_t_ref[...]
    txt = jnp.dot(txt_ref[...], txt_proj_ref[...], preferred_element_type=f32).astype(bf16)
    img = lax.dot_general(img_t_ref[...], img_proj_ref[...], DOWN, preferred_element_type=f32)
    img = img.astype(bf16)
    for member in range(groups):
        rows = slice(member * share, (member + 1) * share)
        parts_ref[member, :share] = img[rows]
        parts_ref[member, share:] = txt[rows]


def project(image_feats_t, text_feats, image_proj, text_proj, groups):
    rows, d_txt = text_feats.shape
    d_img, embed = image_proj.shape
    return pl.pallas_call(
        project_kernel,
        out_shape=(
            jax.ShapeDtypeStruct((groups, 2 * rows // groups, embed), jnp.bfloat16),
            jax.ShapeDtypeStruct((d_txt + d_img, HALF), jnp.bfloat16),
        ),
        compiler_params=pltpu.CompilerParams(vmem_limit_bytes=VMEM),
        cost_estimate=pl.CostEstimate(
            flops=2 * rows * (d_img + d_txt) * embed, bytes_accessed=4_000_000, transcendentals=0
        ),
        name="project",
    )(image_feats_t, text_feats, image_proj, text_proj)


def wgrad_kernel(y_ref, cols_ref, *refs):
    f32 = jnp.float32
    lines, (out_ref,) = refs[:-1], refs[-1:]
    groups, ny, both, wide = cols_ref.shape
    share = both // 2
    d_all = out_ref.shape[2]
    d_txt = 2 * HALF
    totals = [None] * 3
    for line_ref, back in zip(lines, (0, 1, -1, 2, -2, 3, -3, 4)):
        source = lax.rem(y_ref[0] + (ny - back), ny)
        img_cols = cols_ref[:, source, :share].reshape(groups * share, wide)
        txt_cols = cols_ref[:, source, share:].reshape(groups * share, wide)
        terms = [
            lax.dot_general(
                txt_cols, line_ref[:HALF], DOWN, preferred_element_type=f32
            ),
            lax.dot_general(
                txt_cols, line_ref[HALF:d_txt], DOWN, preferred_element_type=f32
            ),
            lax.dot_general(
                img_cols, line_ref[d_txt:], (((0,), (1,)), ((), ())), preferred_element_type=f32
            ),
        ]
        totals = [term if total is None else total + term for total, term in zip(totals, terms)]
    parts, padded, _ = out_ref.shape
    take = wide // parts
    starts = (0, HALF, d_txt, d_all)
    for part in range(parts):
        for piece in range(3):
            lanes = slice(starts[piece], starts[piece + 1])
            out_ref[part, :take, lanes] = totals[piece][part * take : (part + 1) * take].astype(
                out_ref.dtype
            )
        out_ref[part, take:] = jnp.zeros((padded - take, d_all), out_ref.dtype)


def project_grads(y_index, cols, lines, parts):
    groups, ny, both, wide = cols.shape
    d_all = lines[0].shape[0]
    padded = 16
    return pl.pallas_call(
        wgrad_kernel,
        in_specs=[pl.BlockSpec(memory_space=pltpu.SMEM)]
        + [pl.BlockSpec(memory_space=pltpu.VMEM)] * (1 + ny),
        out_shape=jax.ShapeDtypeStruct((parts, padded, d_all), jnp.bfloat16),
        compiler_params=pltpu.CompilerParams(vmem_limit_bytes=VMEM),
        cost_estimate=pl.CostEstimate(
            flops=4 * ny * HALF * wide * d_all, bytes_accessed=5_000_000, transcendentals=0
        ),
        name="project_grads",
    )(y_index, cols, *lines)


def feature_grads_kernel(
    member_ref, own_ref, core_ref, low_ref, high_ref, img_proj_ref, txt_proj_ref,
    img_ref, txt_ref, img_rows, txt_rows,
):
    share = own_ref.shape[0] // 2
    place = 0
    for ref in (own_ref, core_ref, low_ref, high_ref):
        for piece in range(ref.shape[0] // (2 * share)):
            row = pl.multiple_of((member_ref[0] ^ place) * share, share)
            first = piece * 2 * share
            img_rows[pl.ds(row, share)] = ref[first : first + share]
            txt_rows[pl.ds(row, share)] = ref[first + share : first + 2 * share]
            place += 1
    txt_ref[...] = lax.dot_general(
        txt_rows[...], txt_proj_ref[...], ACROSS, preferred_element_type=jnp.float32
    ).astype(txt_ref.dtype)
    img_ref[...] = lax.dot_general(
        img_proj_ref[...], img_rows[...], ACROSS, preferred_element_type=jnp.float32
    ).astype(img_ref.dtype)


def feature_grads(member, pieces, image_proj, text_proj, rows):
    d_img, embed = image_proj.shape
    d_txt = text_proj.shape[0]
    return pl.pallas_call(
        feature_grads_kernel,
        in_specs=[pl.BlockSpec(memory_space=pltpu.SMEM)]
        + [pl.BlockSpec(memory_space=pltpu.VMEM)] * 6,
        out_shape=(
            jax.ShapeDtypeStruct((d_img, rows), jnp.bfloat16),
            jax.ShapeDtypeStruct((rows, d_txt), jnp.bfloat16),
        ),
        scratch_shapes=[pltpu.VMEM((rows, embed), jnp.bfloat16)] * 2,
        compiler_params=pltpu.CompilerParams(vmem_limit_bytes=VMEM),
        cost_estimate=pl.CostEstimate(
            flops=2 * rows * (d_img + d_txt) * embed, bytes_accessed=4_000_000, transcendentals=0
        ),
        name="feature_grads",
    )(member, *pieces, image_proj, text_proj)


def on_device(image_feats, text_feats, image_proj, text_proj, labels, logit_scale, logit_bias):
    bf16, f32 = jnp.bfloat16, jnp.float32
    groups = lax.axis_size(X)
    member = lax.axis_index(X)
    anchor = lax.axis_index(DP)
    blocks = lax.axis_size(DP)
    ny, nz = lax.axis_size("y"), lax.axis_size("z")
    rows = image_feats.shape[0]
    share = rows // groups
    d_img, d_txt = image_feats.shape[1], text_feats.shape[1]
    embed = image_proj.shape[1]
    parts, pack = project(image_feats.T, text_feats, image_proj, text_proj, groups)
    up, down = along(pack, "y", 1), along(pack, "y", -1)
    parts = lax.all_to_all(parts, X, 0, 0, tiled=True)
    parts, up, down = lax.optimization_barrier((parts, up, down))
    summed = jnp.sum(parts.astype(f32), axis=0)
    length = jnp.sqrt(jnp.sum(summed * summed, axis=1, keepdims=True) + NORM_EPS)
    unit = summed / length
    emb = unit.astype(bf16)
    img_own, txt_own = emb[:share], emb[share:]
    img_all = jnp.broadcast_to(img_own[None], (groups, share, embed))
    img_all = lax.all_to_all(img_all, X, 0, 0, tiled=True).reshape(rows, embed)
    near = shifted(txt_own, 1)
    pair = jnp.concatenate([txt_own, near])
    pair, up, down = lax.optimization_barrier((pair, up, down))
    far = shifted(pair, 2)
    up2, down2 = along(up, "y", 1), along(down, "y", -1)
    cols = jnp.concatenate([pair, far])
    offsets = jnp.arange(STEPS, dtype=jnp.int32)
    col_ids = (
        jnp.mod(anchor - offsets, blocks)[:, None] * rows
        + member * share
        + jnp.arange(share, dtype=jnp.int32)[None, :]
    ).reshape(-1)
    scale_value, bias_value = logit_scale[0], logit_bias[0]
    polarity = jnp.where(labels[:, None] == col_ids[None, :], 1.0, -1.0).astype(f32)
    logits = (
        scale_value * lax.dot_general(img_all, cols, ACROSS, preferred_element_type=f32)
        + bias_value
    )
    weights = (-scale_value * polarity * jax.nn.sigmoid(-polarity * logits) / rows).astype(bf16)
    txt_terms = lax.dot_general(weights, img_all, DOWN, preferred_element_type=f32)
    img_terms = jnp.dot(weights, cols, preferred_element_type=f32).astype(bf16)
    img_terms, up2, down2 = lax.optimization_barrier((img_terms, up2, down2))
    up3, down3 = along(up2, "y", 1), along(down2, "y", -1)
    back = shifted(txt_terms[2 * share :].astype(bf16), -2)
    img_terms = lax.all_to_all(img_terms.reshape(groups, share, embed), X, 0, 0, tiled=True)
    img_terms, up3, down3 = lax.optimization_barrier((img_terms, up3, down3))
    up4 = along(up3, "y", 1)
    two = txt_terms[: 2 * share] + back.astype(f32)
    last = shifted(two[share:].astype(bf16), -1)
    grad_txt = two[:share] + last.astype(f32)
    grad_img = jnp.sum(img_terms.astype(f32), axis=0)
    grad = jnp.concatenate([grad_img, grad_txt])
    grad_summed = ((grad - unit * jnp.sum(unit * grad, axis=1, keepdims=True)) / length).astype(bf16)
    wide = embed // ny
    by_cols = grad_summed.reshape(2 * share, ny, wide).transpose(1, 0, 2)
    by_cols = lax.all_to_all(by_cols, "y", 0, 0, tiled=True)
    pieces = [grad_summed]
    for axis in ("core", "xl", "xh"):
        pieces.append(along(jnp.concatenate(pieces) if len(pieces) > 1 else pieces[0], axis, 1))
    by_cols, up4 = lax.optimization_barrier((by_cols, up4))
    cols_all = jnp.broadcast_to(by_cols[None], (groups,) + by_cols.shape)
    cols_all = lax.all_to_all(cols_all, X, 0, 0, tiled=True)
    y_index = lax.axis_index("y").astype(jnp.int32).reshape(1)
    wgrad = project_grads(y_index, cols_all, (pack, up, down, up2, down2, up3, down3, up4), nz)
    wgrad = lax.all_to_all(wgrad, "z", 0, 0, tiled=True)
    wgrad = jnp.sum(wgrad[:, : wide // nz].astype(f32), axis=0)
    member_index = member.astype(jnp.int32).reshape(1)
    image_grad, text_grad = feature_grads(member_index, pieces, image_proj, text_proj, rows)
    return (image_grad.T, text_grad, wgrad[:, d_txt:].T, wgrad[:, :d_txt].T)


def solution(mesh):
    fine = Mesh(mesh.devices.reshape(8, 8, 2, 2, 2), ("y", "z", "xh", "xl", "core"))
    placed = (P(DP, X), P(DP, X), P(X, None), P(X, None), P(DP), P(), P())
    return jax.shard_map(
        on_device,
        mesh=fine,
        in_specs=placed,
        out_specs=(P(DP, X), P(DP, X), P(X, DP), P(X, DP)),
        check_vma=False,
    )
```

time: 139 us -> 156 us (1.12)
  the two profiles are of different devices: /device:TPU:1 before, /device:TPU:48 now
where the time goes in v3:
time: 156 us; the launch traced here: 155 us
  starting transfers between devices  68.6 us (44%)
  waiting for transfers between devices  48 us (31%)
  blocking collectives  18.3 us (12%)
  Pallas kernels  9.92 us (6%)
  local copies, waits for them, and re-layouts  5.62 us (4%)
  between operations  2.34 us (2%)
    ppermute x10, starting transfers between devices, along(): lax.ppermute(value, axis, [(source, (source + steps) % count) for source...  31.2 us
    ppermute x10, waiting for transfers between devices, along(): lax.ppermute(value, axis, [(source, (source + steps) % count) for source...  28.7 us
    all_to_all x1, blocking collectives, on_device(): by_cols = lax.all_to_all(by_cols, 'y', 0, 0, tiled=True)  18.3 us
    ppermute x4, starting transfers between devices, shifted(): return lax.ppermute(value, DP, pairs)  13.9 us
    ppermute x4, waiting for transfers between devices, shifted(): return lax.ppermute(value, DP, pairs)  10.6 us
    all_to_all x1, waiting for transfers between devices, on_device(): wgrad = lax.all_to_all(wgrad, 'z', 0, 0, tiled=True)  7.8 us
    all_to_all x1, starting transfers between devices, on_device(): wgrad = lax.all_to_all(wgrad, 'z', 0, 0, tiled=True)  6.55 us
    all_to_all x1, starting transfers between devices, on_device(): lax.all_to_all(img_terms.reshape(groups, share, embed), X, 0, 0, tiled=True)  4.48 us
  transfers between devices with their start and end apart: 19, of which 10 were waited for; matrix products, arithmetic and copies ran while one was open for 2% of the time, Pallas kernels for 4%

profile of v3, /device:TPU:48, one launch (start us, length us, event | category | flops | bytes accessed | tf_op | source)
XLA Modules:
  0.0 155.2 jit_solution(15184095818289480206)
XLA Ops:
  0.6 3.1 %project.1 = (bf16[8,64,768]{2,1,0:T(8,128)(2,1)}, bf16[912,256]{1,0:T(8,128)(2,1)}) custom-call(bf16[400,256]{1,0:T(8,128)(2,1)} %bitcast.25, bf16[256,512]{1,0:T(8,128)(2,1)} %txt_ref.1, bf16[400,768]{1,0:T(8,128)(2,1)} %img_proj_ref.3, bf16[512,768]{1,0:T(8,128)(2,1)} %txt_proj_ref.3), custom_call_target="tpu_custom_call" | custom-call | flops 358612992 | bytes 4000000 | tf_op jit(solution)/shard_map/project/pallas_call | solution.py:48
  3.7 4.4 %all-to-all-start = ((bf16[8,64,768]{2,1,0:T(8,128)(2,1)}), bf16[8,64,768]{2,1,0:T(8,128)(2,1)S(1)}, u32[]{:S(2)}, u32[]{:S(2)}) async-start(bf16[8,64,768]{2,1,0:T(8,128)(2,1)} %get-tuple-element.22), calls=%async_computation | async-start | bytes 1572864 | tf_op jit(solution)/shard_map/all_to_all | solution.py:169
  8.1 2.6 %collective-permute-start = (bf16[912,256]{1,0:T(8,128)(2,1)S(1)}, bf16[912,256]{1,0:T(8,128)(2,1)S(1)}, u32[]{:S(2)}, u32[]{:S(2)}) collective-permute-start(bf16[912,256]{1,0:T(8,128)(2,1)S(1)} %copy-done.4), channel_id=1, source_target_pairs={{0,64},{64,128},{128,192},{192,256},{256,320},{320,384},{384,448},... | collective-permute-start | bytes 1400840 | tf_op jit(solution)/shard_map/ppermute | solution.py:26
  10.7 3.3 %collective-permute-start.1 = (bf16[912,256]{1,0:T(8,128)(2,1)S(1)}, bf16[912,256]{1,0:T(8,128)(2,1)S(1)}, u32[]{:S(2)}, u32[]{:S(2)}) collective-permute-start(bf16[912,256]{1,0:T(8,128)(2,1)S(1)} %copy-done.4), channel_id=1, source_target_pairs={{0,448},{64,0},{128,64},{192,128},{256,192},{320,256},{384,320},{4... | collective-permute-start | bytes 1400840 | tf_op jit(solution)/shard_map/ppermute | solution.py:26
  14.0 9.1 %collective-permute-done.refs_1_ = bf16[912,256]{1,0:T(8,128)(2,1)S(1)} collective-permute-done((bf16[912,256]{1,0:T(8,128)(2,1)S(1)}, bf16[912,256]{1,0:T(8,128)(2,1)S(1)}, u32[]{:S(2)}, u32[]{:S(2)}) %collective-permute-start) | collective-permute-done | bytes 466976 | tf_op jit(solution)/shard_map/ppermute | solution.py:26
  23.1 4.9 %collective-permute-done.1.refs_2_ = bf16[912,256]{1,0:T(8,128)(2,1)S(1)} collective-permute-done((bf16[912,256]{1,0:T(8,128)(2,1)S(1)}, bf16[912,256]{1,0:T(8,128)(2,1)S(1)}, u32[]{:S(2)}, u32[]{:S(2)}) %collective-permute-start.1) | collective-permute-done | bytes 466976 | tf_op jit(solution)/shard_map/ppermute | solution.py:26
  28.4 1.9 %collective-permute-start.2 = (bf16[32,768]{1,0:T(8,128)(2,1)S(1)}, bf16[32,768]{1,0:T(8,128)(2,1)S(1)}, u32[]{:S(2)}, u32[]{:S(2)}) collective-permute-start(bf16[32,768]{1,0:T(8,128)(2,1)S(1)} %get-tuple-element.40), channel_id=1, source_target_pairs={{0,8},{8,16},{16,24},{24,32},{32,40},{40,48},{48,56},{56,64},{64,7... | collective-permute-start | bytes 147464 | tf_op jit(solution)/shard_map/ppermute | solution.py:21
  32.5 4.5 %all-to-all-start.1 = ((bf16[8,32,768]{2,1,0:T(8,128)(2,1)}), bf16[8,32,768]{2,1,0:T(8,128)(2,1)S(1)}, u32[]{:S(2)}, u32[]{:S(2)}) async-start(bf16[8,32,768]{2,1,0:T(8,128)(2,1)} %broadcast_in_dim.14), calls=%async_computation.1 | async-start | bytes 786432 | tf_op jit(solution)/shard_map/all_to_all | solution.py:177
  37.0 2.6 %collective-permute-done.2 = bf16[32,768]{1,0:T(8,128)(2,1)S(1)} collective-permute-done((bf16[32,768]{1,0:T(8,128)(2,1)S(1)}, bf16[32,768]{1,0:T(8,128)(2,1)S(1)}, u32[]{:S(2)}, u32[]{:S(2)}) %collective-permute-start.2) | collective-permute-done | bytes 49184 | tf_op jit(solution)/shard_map/ppermute | solution.py:21
  39.6 3.3 %collective-permute-start.3 = (bf16[64,768]{1,0:T(8,128)(2,1)S(1)}, bf16[64,768]{1,0:T(8,128)(2,1)S(1)}, u32[]{:S(2)}, u32[]{:S(2)}) collective-permute-start(bf16[64,768]{1,0:T(8,128)(2,1)S(1)} %pad_maximum_fusion.3), channel_id=1, source_target_pairs={{0,16},{8,24},{16,32},{24,40},{32,48},{40,56},{48,64},{56,72},{64,... | collective-permute-start | bytes 294920 | tf_op jit(solution)/shard_map/ppermute | solution.py:21
  42.9 3.4 %collective-permute-start.4 = (bf16[912,256]{1,0:T(8,128)(2,1)S(1)}, bf16[912,256]{1,0:T(8,128)(2,1)S(1)}, u32[]{:S(2)}, u32[]{:S(2)}) collective-permute-start(bf16[912,256]{1,0:T(8,128)(2,1)S(1)} %collective-permute-done.refs_1_), channel_id=1, source_target_pairs={{0,64},{64,128},{128,192},{192,256},{256,320},{320,384},{384,448},... | collective-permute-start | bytes 1400840 | tf_op jit(solution)/shard_map/ppermute | solution.py:26
  46.4 2.4 %collective-permute-start.5 = (bf16[912,256]{1,0:T(8,128)(2,1)S(1)}, bf16[912,256]{1,0:T(8,128)(2,1)S(1)}, u32[]{:S(2)}, u32[]{:S(2)}) collective-permute-start(bf16[912,256]{1,0:T(8,128)(2,1)S(1)} %collective-permute-done.1.refs_2_), channel_id=1, source_target_pairs={{0,448},{64,0},{128,64},{192,128},{256,192},{320,256},{384,320},{4... | collective-permute-start | bytes 1400840 | tf_op jit(solution)/shard_map/ppermute | solution.py:26
  48.8 4.1 %collective-permute-done.3 = bf16[64,768]{1,0:T(8,128)(2,1)S(1)} collective-permute-done((bf16[64,768]{1,0:T(8,128)(2,1)S(1)}, bf16[64,768]{1,0:T(8,128)(2,1)S(1)}, u32[]{:S(2)}, u32[]{:S(2)}) %collective-permute-start.3) | collective-permute-done | bytes 98336 | tf_op jit(solution)/shard_map/ppermute | solution.py:21
  53.5 4.9 %collective-permute-start.8 = (bf16[64,768]{1,0:T(8,128)(2,1)S(1)}, bf16[64,768]{1,0:T(8,128)(2,1)S(1)}, u32[]{:S(2)}, u32[]{:S(2)}) collective-permute-start(bf16[64,768]{1,0:T(8,128)(2,1)S(1)} %slice.54), channel_id=1, source_target_pairs={{0,496},{8,504},{16,0},{24,8},{32,16},{40,24},{48,32},{56,40},{64,... | collective-permute-start | bytes 294920 | tf_op jit(solution)/shard_map/ppermute | solution.py:21
  59.4 2.4 %collective-permute-done.5.refs_4_ = bf16[912,256]{1,0:T(8,128)(2,1)S(1)} collective-permute-done((bf16[912,256]{1,0:T(8,128)(2,1)S(1)}, bf16[912,256]{1,0:T(8,128)(2,1)S(1)}, u32[]{:S(2)}, u32[]{:S(2)}) %collective-permute-start.5) | collective-permute-done | bytes 466976 | tf_op jit(solution)/shard_map/ppermute | solution.py:26
  61.8 2.6 %collective-permute-start.6 = (bf16[912,256]{1,0:T(8,128)(2,1)S(1)}, bf16[912,256]{1,0:T(8,128)(2,1)S(1)}, u32[]{:S(2)}, u32[]{:S(2)}) collective-permute-start(bf16[912,256]{1,0:T(8,128)(2,1)S(1)} %collective-permute-done.4.refs_3_), channel_id=1, source_target_pairs={{0,64},{64,128},{128,192},{192,256},{256,320},{320,384},{384,448},... | collective-permute-start | bytes 1400840 | tf_op jit(solution)/shard_map/ppermute | solution.py:26
  64.4 3.3 %collective-permute-start.7 = (bf16[912,256]{1,0:T(8,128)(2,1)S(1)}, bf16[912,256]{1,0:T(8,128)(2,1)S(1)}, u32[]{:S(2)}, u32[]{:S(2)}) collective-permute-start(bf16[912,256]{1,0:T(8,128)(2,1)S(1)} %collective-permute-done.5.refs_4_), channel_id=1, source_target_pairs={{0,448},{64,0},{128,64},{192,128},{256,192},{320,256},{384,320},{4... | collective-permute-start | bytes 1400840 | tf_op jit(solution)/shard_map/ppermute | solution.py:26
  67.7 4.5 %all-to-all-start.2 = ((bf16[8,32,768]{2,1,0:T(8,128)(2,1)}), bf16[8,32,768]{2,1,0:T(8,128)(2,1)S(1)}, u32[]{:S(2)}, u32[]{:S(2)}) async-start(bf16[8,32,768]{2,1,0:T(8,128)(2,1)} %bitcast.5), calls=%async_computation.2 | async-start | bytes 786432 | tf_op jit(solution)/shard_map/all_to_all | solution.py:202
  72.2 3.8 %collective-permute-start.9 = (bf16[32,768]{1,0:T(8,128)(2,1)S(1)}, bf16[32,768]{1,0:T(8,128)(2,1)S(1)}, u32[]{:S(2)}, u32[]{:S(2)}) collective-permute-start(bf16[32,768]{1,0:T(8,128)(2,1)S(1)} %slice.55), channel_id=1, source_target_pairs={{0,504},{8,0},{16,8},{24,16},{32,24},{40,32},{48,40},{56,48},{64,5... | collective-permute-start | bytes 147464 | tf_op jit(solution)/shard_map/ppermute | solution.py:21
  76.2 3.9 %collective-permute-done.9 = bf16[32,768]{1,0:T(8,128)(2,1)S(1)} collective-permute-done((bf16[32,768]{1,0:T(8,128)(2,1)S(1)}, bf16[32,768]{1,0:T(8,128)(2,1)S(1)}, u32[]{:S(2)}, u32[]{:S(2)}) %collective-permute-start.9) | collective-permute-done | bytes 49184 | tf_op jit(solution)/shard_map/ppermute | solution.py:21
  81.2 3.0 %collective-permute-start.13 = (bf16[912,256]{1,0:T(8,128)(2,1)S(1)}, bf16[912,256]{1,0:T(8,128)(2,1)S(1)}, u32[]{:S(2)}, u32[]{:S(2)}) collective-permute-start(bf16[912,256]{1,0:T(8,128)(2,1)S(1)} %collective-permute-done.6.refs_5_), channel_id=1, source_target_pairs={{0,64},{64,128},{128,192},{192,256},{256,320},{320,384},{384,448},... | collective-permute-start | bytes 1400840 | tf_op jit(solution)/shard_map/ppermute | solution.py:26
  84.6 18.3 %all_to_all.30 = bf16[8,64,96]{2,1,0:T(8,128)(2,1)S(1)} all-to-all(bf16[8,64,96]{2,1,0:T(8,128)(2,1)S(1)} %fusion.12), channel_id=1, replica_groups=mesh['y'=8,'z'=8,'xh'=2,'xl'=2,'core'=2] {'y'}, dimensions={0} | all-to-all | bytes 196608 | tf_op jit(solution)/shard_map/all_to_all | solution.py:213
  102.9 1.3 broadcast_in_dim.15
  104.2 3.6 %all-to-all-start.4 = ((bf16[8,8,64,96]{3,2,1,0:T(8,128)(2,1)}), bf16[8,8,64,96]{3,2,1,0:T(8,128)(2,1)S(1)}, u32[]{:S(2)}, u32[]{:S(2)}) async-start(bf16[8,8,64,96]{3,2,1,0:T(8,128)(2,1)} %broadcast_in_dim.15), calls=%async_computation.4 | async-start | bytes 2097152 | tf_op jit(solution)/shard_map/all_to_all | solution.py:219
  107.9 2.3 %collective-permute-start.10 = (bf16[64,768]{1,0:T(8,128)(2,1)S(1)}, bf16[64,768]{1,0:T(8,128)(2,1)S(1)}, u32[]{:S(2)}, u32[]{:S(2)}) collective-permute-start(bf16[64,768]{1,0:T(8,128)(2,1)S(1)} %divide_convert_fusion.own_ref), channel_id=1, source_target_pairs={{0,1},{1,0},{2,3},{3,2},{4,5},{5,4},{6,7},{7,6},{8,9},{9,8},{10,11... | collective-permute-start | bytes 294920 | tf_op jit(solution)/shard_map/ppermute | solution.py:26
  111.1 3.8 %collective-permute-start.11 = (bf16[128,768]{1,0:T(8,128)(2,1)S(1)}, bf16[128,768]{1,0:T(8,128)(2,1)S(1)}, u32[]{:S(2)}, u32[]{:S(2)}) collective-permute-start(bf16[128,768]{1,0:T(8,128)(2,1)S(1)} %pad_maximum_fusion.2), channel_id=1, source_target_pairs={{0,2},{2,0},{1,3},{3,1},{4,6},{6,4},{5,7},{7,5},{8,10},{10,8},{9,1... | collective-permute-start | bytes 589832 | tf_op jit(solution)/shard_map/ppermute | solution.py:26
  114.9 11.4 %collective-permute-done.11.low_ref = bf16[128,768]{1,0:T(8,128)(2,1)S(1)} collective-permute-done((bf16[128,768]{1,0:T(8,128)(2,1)S(1)}, bf16[128,768]{1,0:T(8,128)(2,1)S(1)}, u32[]{:S(2)}, u32[]{:S(2)}) %collective-permute-start.11) | collective-permute-done | bytes 196640 | tf_op jit(solution)/shard_map/ppermute | solution.py:26
  126.4 4.6 %collective-permute-start.12 = (bf16[256,768]{1,0:T(8,128)(2,1)S(1)}, bf16[256,768]{1,0:T(8,128)(2,1)S(1)}, u32[]{:S(2)}, u32[]{:S(2)}) collective-permute-start(bf16[256,768]{1,0:T(8,128)(2,1)S(1)} %pad_maximum_fusion), channel_id=1, source_target_pairs={{0,4},{4,0},{1,5},{5,1},{2,6},{6,2},{3,7},{7,3},{8,12},{12,8},{9,1... | collective-permute-start | bytes 1179656 | tf_op jit(solution)/shard_map/ppermute | solution.py:26
  132.0 4.0 %project_grads.1 = bf16[8,16,912]{2,1,0:T(8,128)(2,1)} custom-call(s32[1]{0:T(128)} %bitcast.7.y_ref, bf16[8,8,64,96]{3,2,1,0:T(8,128)(2,1)} %copy-done, bf16[912,256]{1,0:T(8,128)(2,1)} %get-tuple-element.23.refs_0_, bf16[912,256]{1,0:T(8,128)(2,1)} %copy-done.5, bf16[912,256]{1,0:T(8,128)(2,1)} %copy-done.6, bf16[912,256]{1,0:T(8,128)(2,1)} %copy-done.7, ...), custom_call_target="tpu_custom_call" | custom-call | flops 717225984 | bytes 5000000 | tf_op jit(solution)/shard_map/project_grads/pallas_call | solution.py:102
  136.0 6.5 %all-to-all-start.5 = ((bf16[8,16,912]{2,1,0:T(8,128)(2,1)}), bf16[8,16,912]{2,1,0:T(8,128)(2,1)S(1)}, u32[]{:S(2)}, u32[]{:S(2)}) async-start(bf16[8,16,912]{2,1,0:T(8,128)(2,1)} %project_grads.1), calls=%async_computation.5 | async-start | bytes 524288 | tf_op jit(solution)/shard_map/all_to_all | solution.py:222
  143.3 2.8 %feature_grads.1 = (bf16[400,256]{1,0:T(8,128)(2,1)}, bf16[256,512]{1,0:T(8,128)(2,1)}) custom-call(s32[1]{0:T(128)} %bitcast.member_ref, bf16[64,768]{1,0:T(8,128)(2,1)} %copy-done.1, bf16[64,768]{1,0:T(8,128)(2,1)} %copy-done.2, bf16[128,768]{1,0:T(8,128)(2,1)} %copy-done.3, bf16[256,768]{1,0:T(8,128)(2,1)} %copy-done.12, bf16[400,768]{1,0:T(8,128)(2,1)} %img_proj_ref.3, ...), custom_call_target="tpu_custom_call" | custom-call | flops 358612992 | bytes 4000000 | tf_op jit(solution)/shard_map/feature_grads/pallas_call | solution.py:139
  146.2 7.8 %all-to-all-done.5 = bf16[8,16,912]{2,1,0:T(8,128)(2,1)S(1)} async-done(((bf16[8,16,912]{2,1,0:T(8,128)(2,1)}), bf16[8,16,912]{2,1,0:T(8,128)(2,1)S(1)}, u32[]{:S(2)}, u32[]{:S(2)}) %all-to-all-start.5) | async-done | bytes 233504 | tf_op jit(solution)/shard_map/all_to_all | solution.py:222
  (72 shorter events, 8.7 us)
Async XLA Ops:
  3.7 4.4 %copy-start.4 = (bf16[912,256]{1,0:T(8,128)(2,1)S(1)}, bf16[912,256]{1,0:T(8,128)(2,1)}, u32[]{:S(2)}) copy-start(bf16[912,256]{1,0:T(8,128)(2,1)} %get-tuple-element.23.refs_0_) | copy-start | bytes 1400836
  3.7 24.3 %all-to-all-start = ((bf16[8,64,768]{2,1,0:T(8,128)(2,1)}), bf16[8,64,768]{2,1,0:T(8,128)(2,1)S(1)}, u32[]{:S(2)}, u32[]{:S(2)}) async-start(bf16[8,64,768]{2,1,0:T(8,128)(2,1)} %get-tuple-element.22), calls=%async_computation | async-start | bytes 1572864 | tf_op jit(solution)/shard_map/all_to_all | solution.py:169
  8.1 15.0 %collective-permute-start = (bf16[912,256]{1,0:T(8,128)(2,1)S(1)}, bf16[912,256]{1,0:T(8,128)(2,1)S(1)}, u32[]{:S(2)}, u32[]{:S(2)}) collective-permute-start(bf16[912,256]{1,0:T(8,128)(2,1)S(1)} %copy-done.4), channel_id=1, source_target_pairs={{0,64},{64,128},{128,192},{192,256},{256,320},{320,384},{384,448},... | collective-permute-start | bytes 1400840 | tf_op jit(solution)/shard_map/ppermute | solution.py:26
  10.7 17.3 %collective-permute-start.1 = (bf16[912,256]{1,0:T(8,128)(2,1)S(1)}, bf16[912,256]{1,0:T(8,128)(2,1)S(1)}, u32[]{:S(2)}, u32[]{:S(2)}) collective-permute-start(bf16[912,256]{1,0:T(8,128)(2,1)S(1)} %copy-done.4), channel_id=1, source_target_pairs={{0,448},{64,0},{128,64},{192,128},{256,192},{320,256},{384,320},{4... | collective-permute-start | bytes 1400840 | tf_op jit(solution)/shard_map/ppermute | solution.py:26
  23.1 19.8 %copy-start.5 = (bf16[912,256]{1,0:T(8,128)(2,1)}, bf16[912,256]{1,0:T(8,128)(2,1)S(1)}, u32[]{:S(2)}) copy-start(bf16[912,256]{1,0:T(8,128)(2,1)S(1)} %collective-permute-done.refs_1_) | copy-start | bytes 1400836
  28.0 18.3 %copy-start.6 = (bf16[912,256]{1,0:T(8,128)(2,1)}, bf16[912,256]{1,0:T(8,128)(2,1)S(1)}, u32[]{:S(2)}) copy-start(bf16[912,256]{1,0:T(8,128)(2,1)S(1)} %collective-permute-done.1.refs_2_) | copy-start | bytes 1400836
  28.3 24.6 %copy-start.13 = (s32[256]{0:T(256)S(1)}, s32[256]{0:T(256)}, u32[]{:S(2)}) copy-start(s32[256]{0:T(256)} %param.11) | copy-start | bytes 3076
  28.4 11.2 %collective-permute-start.2 = (bf16[32,768]{1,0:T(8,128)(2,1)S(1)}, bf16[32,768]{1,0:T(8,128)(2,1)S(1)}, u32[]{:S(2)}, u32[]{:S(2)}) collective-permute-start(bf16[32,768]{1,0:T(8,128)(2,1)S(1)} %get-tuple-element.40), channel_id=1, source_target_pairs={{0,8},{8,16},{16,24},{24,32},{32,40},{40,48},{48,56},{56,64},{64,7... | collective-permute-start | bytes 147464 | tf_op jit(solution)/shard_map/ppermute | solution.py:21
  32.5 20.4 %all-to-all-start.1 = ((bf16[8,32,768]{2,1,0:T(8,128)(2,1)}), bf16[8,32,768]{2,1,0:T(8,128)(2,1)S(1)}, u32[]{:S(2)}, u32[]{:S(2)}) async-start(bf16[8,32,768]{2,1,0:T(8,128)(2,1)} %broadcast_in_dim.14), calls=%async_computation.1 | async-start | bytes 786432 | tf_op jit(solution)/shard_map/all_to_all | solution.py:177
  39.6 13.3 %collective-permute-start.3 = (bf16[64,768]{1,0:T(8,128)(2,1)S(1)}, bf16[64,768]{1,0:T(8,128)(2,1)S(1)}, u32[]{:S(2)}, u32[]{:S(2)}) collective-permute-start(bf16[64,768]{1,0:T(8,128)(2,1)S(1)} %pad_maximum_fusion.3), channel_id=1, source_target_pairs={{0,16},{8,24},{16,32},{24,40},{32,48},{40,56},{48,64},{56,72},{64,... | collective-permute-start | bytes 294920 | tf_op jit(solution)/shard_map/ppermute | solution.py:21
  42.9 16.4 %collective-permute-start.4 = (bf16[912,256]{1,0:T(8,128)(2,1)S(1)}, bf16[912,256]{1,0:T(8,128)(2,1)S(1)}, u32[]{:S(2)}, u32[]{:S(2)}) collective-permute-start(bf16[912,256]{1,0:T(8,128)(2,1)S(1)} %collective-permute-done.refs_1_), channel_id=1, source_target_pairs={{0,64},{64,128},{128,192},{192,256},{256,320},{320,384},{384,448},... | collective-permute-start | bytes 1400840 | tf_op jit(solution)/shard_map/ppermute | solution.py:26
  46.4 15.5 %collective-permute-start.5 = (bf16[912,256]{1,0:T(8,128)(2,1)S(1)}, bf16[912,256]{1,0:T(8,128)(2,1)S(1)}, u32[]{:S(2)}, u32[]{:S(2)}) collective-permute-start(bf16[912,256]{1,0:T(8,128)(2,1)S(1)} %collective-permute-done.1.refs_2_), channel_id=1, source_target_pairs={{0,448},{64,0},{128,64},{192,128},{256,192},{320,256},{384,320},{4... | collective-permute-start | bytes 1400840 | tf_op jit(solution)/shard_map/ppermute | solution.py:26
  53.5 18.7 %collective-permute-start.8 = (bf16[64,768]{1,0:T(8,128)(2,1)S(1)}, bf16[64,768]{1,0:T(8,128)(2,1)S(1)}, u32[]{:S(2)}, u32[]{:S(2)}) collective-permute-start(bf16[64,768]{1,0:T(8,128)(2,1)S(1)} %slice.54), channel_id=1, source_target_pairs={{0,496},{8,504},{16,0},{24,8},{32,16},{40,24},{48,32},{56,40},{64,... | collective-permute-start | bytes 294920 | tf_op jit(solution)/shard_map/ppermute | solution.py:21
  59.4 20.8 %copy-start.7 = (bf16[912,256]{1,0:T(8,128)(2,1)}, bf16[912,256]{1,0:T(8,128)(2,1)S(1)}, u32[]{:S(2)}) copy-start(bf16[912,256]{1,0:T(8,128)(2,1)S(1)} %collective-permute-done.4.refs_3_) | copy-start | bytes 1400836
  61.8 18.4 %copy-start.8 = (bf16[912,256]{1,0:T(8,128)(2,1)}, bf16[912,256]{1,0:T(8,128)(2,1)S(1)}, u32[]{:S(2)}) copy-start(bf16[912,256]{1,0:T(8,128)(2,1)S(1)} %collective-permute-done.5.refs_4_) | copy-start | bytes 1400836
  61.8 19.3 %collective-permute-start.6 = (bf16[912,256]{1,0:T(8,128)(2,1)S(1)}, bf16[912,256]{1,0:T(8,128)(2,1)S(1)}, u32[]{:S(2)}, u32[]{:S(2)}) collective-permute-start(bf16[912,256]{1,0:T(8,128)(2,1)S(1)} %collective-permute-done.4.refs_3_), channel_id=1, source_target_pairs={{0,64},{64,128},{128,192},{192,256},{256,320},{320,384},{384,448},... | collective-permute-start | bytes 1400840 | tf_op jit(solution)/shard_map/ppermute | solution.py:26
  64.4 16.7 %collective-permute-start.7 = (bf16[912,256]{1,0:T(8,128)(2,1)S(1)}, bf16[912,256]{1,0:T(8,128)(2,1)S(1)}, u32[]{:S(2)}, u32[]{:S(2)}) collective-permute-start(bf16[912,256]{1,0:T(8,128)(2,1)S(1)} %collective-permute-done.5.refs_4_), channel_id=1, source_target_pairs={{0,448},{64,0},{128,64},{192,128},{256,192},{320,256},{384,320},{4... | collective-permute-start | bytes 1400840 | tf_op jit(solution)/shard_map/ppermute | solution.py:26
  67.7 13.4 %all-to-all-start.2 = ((bf16[8,32,768]{2,1,0:T(8,128)(2,1)}), bf16[8,32,768]{2,1,0:T(8,128)(2,1)S(1)}, u32[]{:S(2)}, u32[]{:S(2)}) async-start(bf16[8,32,768]{2,1,0:T(8,128)(2,1)} %bitcast.5), calls=%async_computation.2 | async-start | bytes 786432 | tf_op jit(solution)/shard_map/all_to_all | solution.py:202
  72.2 7.9 %collective-permute-start.9 = (bf16[32,768]{1,0:T(8,128)(2,1)S(1)}, bf16[32,768]{1,0:T(8,128)(2,1)S(1)}, u32[]{:S(2)}, u32[]{:S(2)}) collective-permute-start(bf16[32,768]{1,0:T(8,128)(2,1)S(1)} %slice.55), channel_id=1, source_target_pairs={{0,504},{8,0},{16,8},{24,16},{32,24},{40,32},{48,40},{56,48},{64,5... | collective-permute-start | bytes 147464 | tf_op jit(solution)/shard_map/ppermute | solution.py:21
  81.1 21.8 %copy-start.9 = (bf16[912,256]{1,0:T(8,128)(2,1)}, bf16[912,256]{1,0:T(8,128)(2,1)S(1)}, u32[]{:S(2)}) copy-start(bf16[912,256]{1,0:T(8,128)(2,1)S(1)} %collective-permute-done.6.refs_5_) | copy-start | bytes 1400836
  81.1 21.8 %copy-start.10 = (bf16[912,256]{1,0:T(8,128)(2,1)}, bf16[912,256]{1,0:T(8,128)(2,1)S(1)}, u32[]{:S(2)}) copy-start(bf16[912,256]{1,0:T(8,128)(2,1)S(1)} %collective-permute-done.7.refs_6_) | copy-start | bytes 1400836
  81.2 21.7 %collective-permute-start.13 = (bf16[912,256]{1,0:T(8,128)(2,1)S(1)}, bf16[912,256]{1,0:T(8,128)(2,1)S(1)}, u32[]{:S(2)}, u32[]{:S(2)}) collective-permute-start(bf16[912,256]{1,0:T(8,128)(2,1)S(1)} %collective-permute-done.6.refs_5_), channel_id=1, source_target_pairs={{0,64},{64,128},{128,192},{192,256},{256,320},{320,384},{384,448},... | collective-permute-start | bytes 1400840 | tf_op jit(solution)/shard_map/ppermute | solution.py:26
  102.9 1.3 copy-start.11
  104.2 26.8 %all-to-all-start.4 = ((bf16[8,8,64,96]{3,2,1,0:T(8,128)(2,1)}), bf16[8,8,64,96]{3,2,1,0:T(8,128)(2,1)S(1)}, u32[]{:S(2)}, u32[]{:S(2)}) async-start(bf16[8,8,64,96]{3,2,1,0:T(8,128)(2,1)} %broadcast_in_dim.15), calls=%async_computation.4 | async-start | bytes 2097152 | tf_op jit(solution)/shard_map/all_to_all | solution.py:219
  107.9 28.1 %copy-start.1 = (bf16[64,768]{1,0:T(8,128)(2,1)}, bf16[64,768]{1,0:T(8,128)(2,1)S(1)}, u32[]{:S(2)}) copy-start(bf16[64,768]{1,0:T(8,128)(2,1)S(1)} %divide_convert_fusion.own_ref) | copy-start | bytes 294916
  107.9 3.2 %collective-permute-start.10 = (bf16[64,768]{1,0:T(8,128)(2,1)S(1)}, bf16[64,768]{1,0:T(8,128)(2,1)S(1)}, u32[]{:S(2)}, u32[]{:S(2)}) collective-permute-start(bf16[64,768]{1,0:T(8,128)(2,1)S(1)} %divide_convert_fusion.own_ref), channel_id=1, source_target_pairs={{0,1},{1,0},{2,3},{3,2},{4,5},{5,4},{6,7},{7,6},{8,9},{9,8},{10,11... | collective-permute-start | bytes 294920 | tf_op jit(solution)/shard_map/ppermute | solution.py:26
  111.1 24.9 %copy-start.2 = (bf16[64,768]{1,0:T(8,128)(2,1)}, bf16[64,768]{1,0:T(8,128)(2,1)S(1)}, u32[]{:S(2)}) copy-start(bf16[64,768]{1,0:T(8,128)(2,1)S(1)} %collective-permute-done.10.core_ref) | copy-start | bytes 294916
  111.1 15.2 %collective-permute-start.11 = (bf16[128,768]{1,0:T(8,128)(2,1)S(1)}, bf16[128,768]{1,0:T(8,128)(2,1)S(1)}, u32[]{:S(2)}, u32[]{:S(2)}) collective-permute-start(bf16[128,768]{1,0:T(8,128)(2,1)S(1)} %pad_maximum_fusion.2), channel_id=1, source_target_pairs={{0,2},{2,0},{1,3},{3,1},{4,6},{6,4},{5,7},{7,5},{8,10},{10,8},{9,1... | collective-permute-start | bytes 589832 | tf_op jit(solution)/shard_map/ppermute | solution.py:26
  126.3 9.7 %copy-start.3 = (bf16[128,768]{1,0:T(8,128)(2,1)}, bf16[128,768]{1,0:T(8,128)(2,1)S(1)}, u32[]{:S(2)}) copy-start(bf16[128,768]{1,0:T(8,128)(2,1)S(1)} %collective-permute-done.11.low_ref) | copy-start | bytes 589828
  126.4 16.2 %collective-permute-start.12 = (bf16[256,768]{1,0:T(8,128)(2,1)S(1)}, bf16[256,768]{1,0:T(8,128)(2,1)S(1)}, u32[]{:S(2)}, u32[]{:S(2)}) collective-permute-start(bf16[256,768]{1,0:T(8,128)(2,1)S(1)} %pad_maximum_fusion), channel_id=1, source_target_pairs={{0,4},{4,0},{1,5},{5,1},{2,6},{6,2},{3,7},{7,3},{8,12},{12,8},{9,1... | collective-permute-start | bytes 1179656 | tf_op jit(solution)/shard_map/ppermute | solution.py:26
  131.0 1.0 copy-start
  136.0 17.9 %all-to-all-start.5 = ((bf16[8,16,912]{2,1,0:T(8,128)(2,1)}), bf16[8,16,912]{2,1,0:T(8,128)(2,1)S(1)}, u32[]{:S(2)}, u32[]{:S(2)}) async-start(bf16[8,16,912]{2,1,0:T(8,128)(2,1)} %project_grads.1), calls=%async_computation.5 | async-start | bytes 524288 | tf_op jit(solution)/shard_map/all_to_all | solution.py:222
  (1 other events, 0.7 us)

commit v4 on v1

v4 whole, which is shorter than its diff:
```python
import jax
import jax.numpy as jnp
from jax import lax
from jax.experimental import pallas as pl
from jax.experimental.pallas import tpu as pltpu
from jax.sharding import Mesh, PartitionSpec as P

STEPS = 4
NORM_EPS = 1e-06
X = ("xh", "xl", "core")
DP = ("yh", "yl", "z")
ACROSS = (((1,), (1,)), ((), ()))
DOWN = (((0,), (0,)), ((), ()))
HALF = 256
VMEM = 58 * 1024 * 1024
F32, BF16 = jnp.float32, jnp.bfloat16


def shifted(value, steps):
    count = lax.axis_size(DP)
    pairs = [(source, (source + steps) % count) for source in range(count)]
    return lax.ppermute(value, DP, pairs)


def swapped(value, axis, bits):
    count = lax.axis_size(axis)
    return lax.ppermute(value, axis, [(source, source ^ bits) for source in range(count)])


def call(kernel, name, out_shape, args, flops, scratch=(), scalars=0):
    spaces = [pltpu.SMEM] * scalars + [pltpu.VMEM] * (len(args) - scalars)
    return pl.pallas_call(
        kernel,
        out_shape=out_shape,
        in_specs=[pl.BlockSpec(memory_space=space) for space in spaces],
        scratch_shapes=list(scratch),
        compiler_params=pltpu.CompilerParams(vmem_limit_bytes=VMEM),
        cost_estimate=pl.CostEstimate(flops=flops, bytes_accessed=4_000_000, transcendentals=0),
        name=name,
    )(*args)


def project_kernel(img_t_ref, txt_ref, img_proj_ref, txt_proj_ref, parts_ref, pack_ref):
    groups, share = parts_ref.shape[0], parts_ref.shape[1] // 2
    d_txt = txt_ref.shape[1]
    for half in range(d_txt // HALF):
        pack_ref[half * HALF : (half + 1) * HALF] = txt_ref[:, half * HALF : (half + 1) * HALF]
    pack_ref[d_txt:] = img_t_ref[...]
    txt = jnp.dot(txt_ref[...], txt_proj_ref[...], preferred_element_type=F32).astype(BF16)
    img = lax.dot_general(img_t_ref[...], img_proj_ref[...], DOWN, preferred_element_type=F32)
    img = img.astype(BF16)
    for member in range(groups):
        rows = slice(member * share, (member + 1) * share)
        parts_ref[member, :share] = img[rows]
        parts_ref[member, share:] = txt[rows]


def wgrad_kernel(place_ref, cols_ref, *refs):
    lines, out_ref, total_ref = refs[:-2], refs[-2], refs[-1]
    groups, quad, share, wide = cols_ref.shape
    wide //= 2
    d_all = lines[0].shape[0]
    d_txt = 2 * HALF
    d_img = d_all - d_txt
    sums = [None] * 3
    for bits, line_ref in enumerate(lines):
        cols = cols_ref[:, place_ref[0] ^ bits].reshape(groups * share, 2 * wide)
        cols = cols.T
        img_cols, txt_cols = cols[:wide], cols[wide:]
        terms = [
            jnp.dot(txt_cols, line_ref[:HALF], preferred_element_type=F32),
            jnp.dot(txt_cols, line_ref[HALF:d_txt], preferred_element_type=F32),
            lax.dot_general(img_cols, line_ref[d_txt:], ACROSS, preferred_element_type=F32),
        ]
        sums = [term if total is None else total + term for total, term in zip(sums, terms)]
    peers, height, _ = out_ref.shape
    take = height // 4
    for peer in range(peers):
        rows = slice(peer * take, (peer + 1) * take)
        total_ref[peer, :take] = sums[0][rows]
        total_ref[peer, take : 2 * take] = sums[1][rows]
        total_ref[peer, 2 * take : 3 * take] = sums[2][rows, :HALF]
        total_ref[peer, 3 * take :, : d_img - HALF] = sums[2][rows, HALF:]
        total_ref[peer, 3 * take :, d_img - HALF :] = jnp.zeros((take, 2 * HALF - d_img), F32)
    out_ref[...] = total_ref[...].astype(BF16)


def total_kernel(blocks_ref, img_ref, txt_ref, total_ref):
    take = img_ref.shape[0]
    d_img = img_ref.shape[1]
    total = blocks_ref[0].astype(F32)
    for peer in range(1, blocks_ref.shape[0]):
        total = total + blocks_ref[peer].astype(F32)
    total_ref[...] = total
    txt_ref[:, :HALF] = total_ref[:take]
    txt_ref[:, HALF:] = total_ref[take : 2 * take]
    img_ref[:, :HALF] = total_ref[2 * take : 3 * take]
    img_ref[:, HALF:] = total_ref[3 * take :, : d_img - HALF]


def feature_grads_kernel(rows_ref, img_proj_ref, txt_proj_ref, img_ref, txt_ref):
    groups, share, embed = rows_ref.shape
    share //= 2
    img_rows = rows_ref[:, :share].reshape(groups * share, embed)
    txt_rows = rows_ref[:, share:].reshape(groups * share, embed)
    txt_ref[...] = lax.dot_general(
        txt_rows, txt_proj_ref[...], ACROSS, preferred_element_type=F32
    ).astype(BF16)
    img_ref[...] = lax.dot_general(
        img_proj_ref[...], img_rows, ACROSS, preferred_element_type=F32
    ).astype(BF16)


def on_device(image_feats, text_feats, image_proj, text_proj, labels, logit_scale, logit_bias):
    groups = lax.axis_size(X)
    member = lax.axis_index(X)
    anchor = lax.axis_index(DP)
    blocks = lax.axis_size(DP)
    quad = lax.axis_size("yl")
    peers = blocks // quad
    rows = image_feats.shape[0]
    share = rows // groups
    d_img, d_txt = image_feats.shape[1], text_feats.shape[1]
    embed = image_proj.shape[1]
    parts, pack = call(
        project_kernel,
        "project",
        (
            jax.ShapeDtypeStruct((groups, 2 * share, embed), BF16),
            jax.ShapeDtypeStruct((d_txt + d_img, HALF), BF16),
        ),
        (image_feats.T, text_feats, image_proj, text_proj),
        2 * rows * (d_img + d_txt) * embed,
    )
    lines = [pack] + [swapped(pack, "yl", bits) for bits in range(1, quad)]
    parts = lax.all_to_all(parts, X, 0, 0, tiled=True)
    summed = jnp.sum(parts.astype(F32), axis=0)
    length = jnp.sqrt(jnp.sum(summed * summed, axis=1, keepdims=True) + NORM_EPS)
    unit = summed / length
    emb = unit.astype(BF16)
    img_own, txt_own = emb[:share], emb[share:]
    img_all = jnp.broadcast_to(img_own[None], (groups, share, embed))
    img_all = lax.all_to_all(img_all, X, 0, 0, tiled=True).reshape(rows, embed)
    near = shifted(txt_own, 1)
    pair = jnp.concatenate([txt_own, near])
    far = shifted(pair, 2)
    cols = jnp.concatenate([pair, far])
    offsets = jnp.arange(STEPS, dtype=jnp.int32)
    col_ids = (
        jnp.mod(anchor - offsets, blocks)[:, None] * rows
        + member * share
        + jnp.arange(share, dtype=jnp.int32)[None, :]
    ).reshape(-1)
    scale_value, bias_value = logit_scale[0], logit_bias[0]
    polarity = jnp.where(labels[:, None] == col_ids[None, :], 1.0, -1.0).astype(F32)
    logits = (
        scale_value * lax.dot_general(img_all, cols, ACROSS, preferred_element_type=F32)
        + bias_value
    )
    weights = (-scale_value * polarity * jax.nn.sigmoid(-polarity * logits) / rows).astype(BF16)
    txt_terms = lax.dot_general(weights, img_all, DOWN, preferred_element_type=F32)
    img_terms = jnp.dot(weights, cols, preferred_element_type=F32).astype(BF16)
    back = shifted(txt_terms[2 * share :].astype(BF16), -2)
    img_terms = lax.all_to_all(img_terms.reshape(groups, share, embed), X, 0, 0, tiled=True)
    img_terms, lines = lax.optimization_barrier((img_terms, lines))
    two = txt_terms[: 2 * share] + back.astype(F32)
    last = shifted(two[share:].astype(BF16), -1)
    grad_txt = two[:share] + last.astype(F32)
    grad_img = jnp.sum(img_terms.astype(F32), axis=0)
    grad = jnp.concatenate([grad_img, grad_txt])
    grad_summed = ((grad - unit * jnp.sum(unit * grad, axis=1, keepdims=True)) / length).astype(BF16)
    strip = embed // (blocks // lax.axis_size("z"))
    by_cols = grad_summed.reshape(2, share, embed // (quad * strip), quad, strip)
    by_cols = by_cols.transpose(3, 1, 0, 2, 4).reshape(quad, share, 2 * embed // quad)
    by_cols = lax.all_to_all(by_cols, "yl", 0, 0, tiled=True)
    cols_all = lax.all_gather(by_cols, X, axis=0, tiled=False)
    height = 4 * embed // blocks
    wgrad = call(
        wgrad_kernel,
        "project_grads",
        jax.ShapeDtypeStruct((peers, height, HALF), BF16),
        (lax.axis_index("yl").astype(jnp.int32).reshape(1), cols_all, *lines),
        2 * quad * rows * (embed // quad) * (d_img + d_txt),
        scratch=(pltpu.VMEM((peers, height, HALF), F32),),
        scalars=1,
    )
    wgrad = lax.all_to_all(wgrad, ("yh", "z"), 0, 0, tiled=True)
    rows_all = lax.all_gather(grad_summed, X, axis=0, tiled=False)
    image_grad, text_grad = call(
        feature_grads_kernel,
        "feature_grads",
        (jax.ShapeDtypeStruct((d_img, rows), BF16), jax.ShapeDtypeStruct((rows, d_txt), BF16)),
        (rows_all, image_proj, text_proj),
        2 * rows * (d_img + d_txt) * embed,
    )
    img_wgrad, txt_wgrad = call(
        total_kernel,
        "total",
        (
            jax.ShapeDtypeStruct((embed // blocks, d_img), F32),
            jax.ShapeDtypeStruct((embed // blocks, d_txt), F32),
        ),
        (wgrad,),
        peers * height * HALF,
        scratch=(pltpu.VMEM((height, HALF), F32),),
    )
    return (image_grad.T, text_grad, img_wgrad.T, txt_wgrad.T)


def solution(mesh):
    fine = Mesh(mesh.devices.reshape(2, 4, 8, 2, 2, 2), DP + X)
    placed = (P(DP, X), P(DP, X), P(X, None), P(X, None), P(DP), P(), P())
    return jax.shard_map(
        on_device,
        mesh=fine,
        in_specs=placed,
        out_specs=(P(DP, X), P(DP, X), P(X, DP), P(X, DP)),
        check_vma=False,
    )
```

time: 241 us -> 147 us (0.61)
  the two profiles are of different devices: /device:TPU:6 before, /device:TPU:1 now
where the time goes in v4:
time: 147 us; the launch traced here: 146 us
  blocking collectives  60.3 us (41%)
  starting transfers between devices  49.4 us (34%)
  waiting for transfers between devices  18.5 us (13%)
  Pallas kernels  10.7 us (7%)
  local copies, waits for them, and re-layouts  2.44 us (2%)
  between operations  2.21 us (2%)
  matrix products  1.5 us (1%)
    all_to_all x1, blocking collectives, on_device(): by_cols = lax.all_to_all(by_cols, 'yl', 0, 0, tiled=True)  29 us
    all_gather x1, blocking collectives, on_device(): cols_all = lax.all_gather(by_cols, X, axis=0, tiled=False)  16.5 us
    all_gather x1, blocking collectives, on_device(): rows_all = lax.all_gather(grad_summed, X, axis=0, tiled=False)  14.7 us
    ppermute x4, waiting for transfers between devices, shifted(): return lax.ppermute(value, DP, pairs)  12.8 us
    ppermute x4, starting transfers between devices, shifted(): return lax.ppermute(value, DP, pairs)  12.3 us
    pallas_call x4, Pallas kernels, call(): pl.pallas_call(kernel, out_shape=out_shape, in_specs=[pl.BlockSpec(memory...  10.7 us
    all_to_all x1, starting transfers between devices, on_device(): parts = lax.all_to_all(parts, X, 0, 0, tiled=True)  10.5 us
    ppermute x3, starting transfers between devices, swapped(): lax.ppermute(value, axis, [(source, source ^ bits) for source in range(co...  9.26 us
  transfers between devices with their start and end apart: 11, of which 5 were waited for; matrix products, arithmetic and copies ran while one was open for 2% of the time, Pallas kernels for 2%

profile of v4, /device:TPU:1, one launch (start us, length us, event | category | flops | bytes accessed | tf_op | source)
XLA Modules:
  0.0 146.1 jit_solution(7741835145935197553)
XLA Ops:
  0.6 3.1 %project.1 = (bf16[8,64,768]{2,1,0:T(8,128)(2,1)}, bf16[912,256]{1,0:T(8,128)(2,1)}) custom-call(bf16[400,256]{1,0:T(8,128)(2,1)} %bitcast.32, bf16[256,512]{1,0:T(8,128)(2,1)} %txt_ref.1, bf16[400,768]{1,0:T(8,128)(2,1)} %img_proj_ref.3, bf16[512,768]{1,0:T(8,128)(2,1)} %txt_proj_ref.3), custom_call_target="tpu_custom_call" | custom-call | flops 358612992 | bytes 4000000 | tf_op jit(solution)/shard_map/project/pallas_call | solution.py:32
  3.7 10.5 %all-to-all-start = ((bf16[8,64,768]{2,1,0:T(8,128)(2,1)}), bf16[8,64,768]{2,1,0:T(8,128)(2,1)S(1)}, u32[]{:S(2)}, u32[]{:S(2)}) async-start(bf16[8,64,768]{2,1,0:T(8,128)(2,1)} %get-tuple-element.15), calls=%async_computation | async-start | bytes 1572864 | tf_op jit(solution)/shard_map/all_to_all | solution.py:136
  14.2 1.9 %collective-permute-start.4 = (bf16[912,256]{1,0:T(8,128)(2,1)S(1)}, bf16[912,256]{1,0:T(8,128)(2,1)S(1)}, u32[]{:S(2)}, u32[]{:S(2)}) collective-permute-start(bf16[912,256]{1,0:T(8,128)(2,1)S(1)} %copy-done.1), channel_id=1, source_target_pairs={{0,192},{64,128},{128,64},{192,0},{1,193},{65,129},{129,65},{193,1... | collective-permute-start | bytes 1400840 | tf_op jit(solution)/shard_map/ppermute | solution.py:27
  16.1 1.9 %collective-permute-start.3 = (bf16[912,256]{1,0:T(8,128)(2,1)S(1)}, bf16[912,256]{1,0:T(8,128)(2,1)S(1)}, u32[]{:S(2)}, u32[]{:S(2)}) collective-permute-start(bf16[912,256]{1,0:T(8,128)(2,1)S(1)} %copy-done.1), channel_id=1, source_target_pairs={{0,128},{64,192},{128,0},{192,64},{1,129},{65,193},{129,1},{193,65... | collective-permute-start | bytes 1400840 | tf_op jit(solution)/shard_map/ppermute | solution.py:27
  18.1 5.4 %collective-permute-start.2 = (bf16[912,256]{1,0:T(8,128)(2,1)S(1)}, bf16[912,256]{1,0:T(8,128)(2,1)S(1)}, u32[]{:S(2)}, u32[]{:S(2)}) collective-permute-start(bf16[912,256]{1,0:T(8,128)(2,1)S(1)} %copy-done.1), channel_id=1, source_target_pairs={{0,64},{64,0},{128,192},{192,128},{1,65},{65,1},{129,193},{193,129... | collective-permute-start | bytes 1400840 | tf_op jit(solution)/shard_map/ppermute | solution.py:27
  23.5 3.0 %all-to-all-done = bf16[8,64,768]{2,1,0:T(8,128)(2,1)S(1)} async-done(((bf16[8,64,768]{2,1,0:T(8,128)(2,1)}), bf16[8,64,768]{2,1,0:T(8,128)(2,1)S(1)}, u32[]{:S(2)}, u32[]{:S(2)}) %all-to-all-start) | async-done | bytes 786464 | tf_op jit(solution)/shard_map/all_to_all | solution.py:136
  26.9 1.9 %collective-permute-start = (bf16[32,768]{1,0:T(8,128)(2,1)S(1)}, bf16[32,768]{1,0:T(8,128)(2,1)S(1)}, u32[]{:S(2)}, u32[]{:S(2)}) collective-permute-start(bf16[32,768]{1,0:T(8,128)(2,1)S(1)} %get-tuple-element.28), channel_id=1, source_target_pairs={{0,8},{8,16},{16,24},{24,32},{32,40},{40,48},{48,56},{56,64},{64,7... | collective-permute-start | bytes 147464 | tf_op jit(solution)/shard_map/ppermute | solution.py:22
  28.8 0.8 broadcast_in_dim.12
  29.6 4.2 %all-to-all-start.1 = ((bf16[8,32,768]{2,1,0:T(8,128)(2,1)}), bf16[8,32,768]{2,1,0:T(8,128)(2,1)S(1)}, u32[]{:S(2)}, u32[]{:S(2)}) async-start(bf16[8,32,768]{2,1,0:T(8,128)(2,1)} %broadcast_in_dim.12), calls=%async_computation.1 | async-start | bytes 786432 | tf_op jit(solution)/shard_map/all_to_all | solution.py:143
  33.8 3.6 %collective-permute-done = bf16[32,768]{1,0:T(8,128)(2,1)S(1)} collective-permute-done((bf16[32,768]{1,0:T(8,128)(2,1)S(1)}, bf16[32,768]{1,0:T(8,128)(2,1)S(1)}, u32[]{:S(2)}, u32[]{:S(2)}) %collective-permute-start) | collective-permute-done | bytes 49184 | tf_op jit(solution)/shard_map/ppermute | solution.py:22
  37.4 1.9 %collective-permute-start.1 = (bf16[64,768]{1,0:T(8,128)(2,1)S(1)}, bf16[64,768]{1,0:T(8,128)(2,1)S(1)}, u32[]{:S(2)}, u32[]{:S(2)}) collective-permute-start(bf16[64,768]{1,0:T(8,128)(2,1)S(1)} %pad_maximum_fusion.2), channel_id=1, source_target_pairs={{0,16},{8,24},{16,32},{24,40},{32,48},{40,56},{48,64},{56,72},{64,... | collective-permute-start | bytes 294920 | tf_op jit(solution)/shard_map/ppermute | solution.py:22
  40.8 6.2 %collective-permute-done.1 = bf16[64,768]{1,0:T(8,128)(2,1)S(1)} collective-permute-done((bf16[64,768]{1,0:T(8,128)(2,1)S(1)}, bf16[64,768]{1,0:T(8,128)(2,1)S(1)}, u32[]{:S(2)}, u32[]{:S(2)}) %collective-permute-start.1) | collective-permute-done | bytes 98336 | tf_op jit(solution)/shard_map/ppermute | solution.py:22
  47.0 0.3 fusion.8
  47.3 0.2 fusion.21
  47.5 6.6 %collective-permute-start.5 = (bf16[64,768]{1,0:T(8,128)(2,1)S(1)}, bf16[64,768]{1,0:T(8,128)(2,1)S(1)}, u32[]{:S(2)}, u32[]{:S(2)}) collective-permute-start(bf16[64,768]{1,0:T(8,128)(2,1)S(1)} %slice.36), channel_id=1, source_target_pairs={{0,496},{8,504},{16,0},{24,8},{32,16},{40,24},{48,32},{56,40},{64,... | collective-permute-start | bytes 294920 | tf_op jit(solution)/shard_map/ppermute | solution.py:22
  54.1 1.0 convolution_convert_fusion
  55.1 5.7 %all-to-all-start.2 = ((bf16[8,32,768]{2,1,0:T(8,128)(2,1)}), bf16[8,32,768]{2,1,0:T(8,128)(2,1)S(1)}, u32[]{:S(2)}, u32[]{:S(2)}) async-start(bf16[8,32,768]{2,1,0:T(8,128)(2,1)} %bitcast.4), calls=%async_computation.2 | async-start | bytes 786432 | tf_op jit(solution)/shard_map/all_to_all | solution.py:164
  60.8 1.9 %collective-permute-start.6 = (bf16[32,768]{1,0:T(8,128)(2,1)S(1)}, bf16[32,768]{1,0:T(8,128)(2,1)S(1)}, u32[]{:S(2)}, u32[]{:S(2)}) collective-permute-start(bf16[32,768]{1,0:T(8,128)(2,1)S(1)} %slice.37), channel_id=1, source_target_pairs={{0,504},{8,0},{16,8},{24,16},{32,24},{40,32},{48,40},{56,48},{64,5... | collective-permute-start | bytes 147464 | tf_op jit(solution)/shard_map/ppermute | solution.py:22
  62.8 0.2 reduce_sum.45
  63.0 3.0 %collective-permute-done.6 = bf16[32,768]{1,0:T(8,128)(2,1)S(1)} collective-permute-done((bf16[32,768]{1,0:T(8,128)(2,1)S(1)}, bf16[32,768]{1,0:T(8,128)(2,1)S(1)}, u32[]{:S(2)}, u32[]{:S(2)}) %collective-permute-start.6) | collective-permute-done | bytes 49184 | tf_op jit(solution)/shard_map/ppermute | solution.py:22
  66.1 2.7 %all-to-all-done.2 = bf16[8,32,768]{2,1,0:T(8,128)(2,1)S(1)} async-done(((bf16[8,32,768]{2,1,0:T(8,128)(2,1)}), bf16[8,32,768]{2,1,0:T(8,128)(2,1)S(1)}, u32[]{:S(2)}, u32[]{:S(2)}) %all-to-all-start.2) | async-done | bytes 393248 | tf_op jit(solution)/shard_map/all_to_all | solution.py:164
  68.9 0.2 pad_maximum_fusion.1
  69.2 0.2 concatenate.31
  69.4 0.2 fusion.13
  69.9 29.0 %all_to_all.25 = bf16[4,32,384]{2,1,0:T(8,128)(2,1)S(1)} all-to-all(bf16[4,32,384]{2,1,0:T(8,128)(2,1)S(1)} %reshape.186), channel_id=1, replica_groups=mesh['yh'=2,'yl'=4,'z'=8,'xh'=2,'xl'=2,'core'=2] {'yl'}, dimensions={0} | all-to-all | bytes 196608 | tf_op jit(solution)/shard_map/all_to_all | solution.py:175
  98.9 16.5 %all-gather = bf16[32,32,384]{2,1,0:T(8,128)(2,1)} all-gather(bf16[4,32,384]{2,1,0:T(8,128)(2,1)S(1)} %all_to_all.25), channel_id=2, replica_groups=mesh['yh'=2,'yl'=4,'z'=8,'xh'=2,'xl'=2,'core'=2] {'xh','xl','core'}, dimensions={0}, use_global_device_ids=true | all-gather | bytes 884736 | tf_op jit(solution)/shard_map/all_gather | solution.py:176
  115.4 3.1 %project_grads.1 = bf16[16,48,256]{2,1,0:T(8,128)(2,1)} custom-call(s32[1]{0:T(128)} %bitcast.9.place_ref, bf16[8,4,32,384]{3,2,1,0:T(8,128)(2,1)} %bitcast.27, bf16[912,256]{1,0:T(8,128)(2,1)} %get-tuple-element.20.refs_0_, bf16[912,256]{1,0:T(8,128)(2,1)} %copy-done.4, bf16[912,256]{1,0:T(8,128)(2,1)} %copy-done.3, bf16[912,256]{1,0:T(8,128)(2,1)} %copy-done.2), custom_call_target="tpu_custom_call" | custom-call | flops 358612992 | bytes 4000000 | tf_op jit(solution)/shard_map/project_grads/pallas_call | solution.py:32
  118.6 7.5 %all-to-all-start.4 = ((bf16[16,48,256]{2,1,0:T(8,128)(2,1)}), bf16[16,48,256]{2,1,0:T(8,128)(2,1)S(1)}, u32[]{:S(2)}, u32[]{:S(2)}) async-start(bf16[16,48,256]{2,1,0:T(8,128)(2,1)} %project_grads.1), calls=%async_computation.4 | async-start | bytes 786432 | tf_op jit(solution)/shard_map/all_to_all | solution.py:187
  126.2 14.7 %all_gather.10.rows_ref = bf16[8,64,768]{2,1,0:T(8,128)(2,1)} all-gather(bf16[1,64,768]{2,1,0:T(8,128)(2,1)S(1)} %fusion.11), channel_id=1, replica_groups=mesh['yh'=2,'yl'=4,'z'=8,'xh'=2,'xl'=2,'core'=2] {'xh','xl','core'}, dimensions={0}, use_global_device_ids=true | all-gather | bytes 884736 | tf_op jit(solution)/shard_map/all_gather | solution.py:188
  140.9 2.8 %feature_grads.1 = (bf16[400,256]{1,0:T(8,128)(2,1)}, bf16[256,512]{1,0:T(8,128)(2,1)}) custom-call(bf16[8,64,768]{2,1,0:T(8,128)(2,1)} %all_gather.10.rows_ref, bf16[400,768]{1,0:T(8,128)(2,1)} %img_proj_ref.3, bf16[512,768]{1,0:T(8,128)(2,1)} %txt_proj_ref.3), custom_call_target="tpu_custom_call" | custom-call | flops 358612992 | bytes 4000000 | tf_op jit(solution)/shard_map/feature_grads/pallas_call | solution.py:32
  143.7 0.7 copy-done
  144.5 1.7 %total.1 = (f32[12,400]{1,0:T(8,128)}, f32[12,512]{1,0:T(8,128)}) custom-call(bf16[16,48,256]{2,1,0:T(8,128)(2,1)} %copy-done), custom_call_target="tpu_custom_call" | custom-call | flops 196608 | bytes 4000000 | tf_op jit(solution)/shard_map/total/pallas_call | solution.py:32
  (36 shorter events, 1.2 us)
Async XLA Ops:
  3.7 10.5 %copy-start.1 = (bf16[912,256]{1,0:T(8,128)(2,1)S(1)}, bf16[912,256]{1,0:T(8,128)(2,1)}, u32[]{:S(2)}) copy-start(bf16[912,256]{1,0:T(8,128)(2,1)} %get-tuple-element.20.refs_0_) | copy-start | bytes 1400836
  3.7 22.8 %all-to-all-start = ((bf16[8,64,768]{2,1,0:T(8,128)(2,1)}), bf16[8,64,768]{2,1,0:T(8,128)(2,1)S(1)}, u32[]{:S(2)}, u32[]{:S(2)}) async-start(bf16[8,64,768]{2,1,0:T(8,128)(2,1)} %get-tuple-element.15), calls=%async_computation | async-start | bytes 1572864 | tf_op jit(solution)/shard_map/all_to_all | solution.py:136
  14.2 51.9 %collective-permute-start.4 = (bf16[912,256]{1,0:T(8,128)(2,1)S(1)}, bf16[912,256]{1,0:T(8,128)(2,1)S(1)}, u32[]{:S(2)}, u32[]{:S(2)}) collective-permute-start(bf16[912,256]{1,0:T(8,128)(2,1)S(1)} %copy-done.1), channel_id=1, source_target_pairs={{0,192},{64,128},{128,64},{192,0},{1,193},{65,129},{129,65},{193,1... | collective-permute-start | bytes 1400840 | tf_op jit(solution)/shard_map/ppermute | solution.py:27
  16.1 50.0 %collective-permute-start.3 = (bf16[912,256]{1,0:T(8,128)(2,1)S(1)}, bf16[912,256]{1,0:T(8,128)(2,1)S(1)}, u32[]{:S(2)}, u32[]{:S(2)}) collective-permute-start(bf16[912,256]{1,0:T(8,128)(2,1)S(1)} %copy-done.1), channel_id=1, source_target_pairs={{0,128},{64,192},{128,0},{192,64},{1,129},{65,193},{129,1},{193,65... | collective-permute-start | bytes 1400840 | tf_op jit(solution)/shard_map/ppermute | solution.py:27
  18.1 48.1 %collective-permute-start.2 = (bf16[912,256]{1,0:T(8,128)(2,1)S(1)}, bf16[912,256]{1,0:T(8,128)(2,1)S(1)}, u32[]{:S(2)}, u32[]{:S(2)}) collective-permute-start(bf16[912,256]{1,0:T(8,128)(2,1)S(1)} %copy-done.1), channel_id=1, source_target_pairs={{0,64},{64,0},{128,192},{192,128},{1,65},{65,1},{129,193},{193,129... | collective-permute-start | bytes 1400840 | tf_op jit(solution)/shard_map/ppermute | solution.py:27
  26.9 20.1 %copy-start.5 = (s32[256]{0:T(256)S(1)}, s32[256]{0:T(256)}, u32[]{:S(2)}) copy-start(s32[256]{0:T(256)} %param.11) | copy-start | bytes 3076
  26.9 10.5 %collective-permute-start = (bf16[32,768]{1,0:T(8,128)(2,1)S(1)}, bf16[32,768]{1,0:T(8,128)(2,1)S(1)}, u32[]{:S(2)}, u32[]{:S(2)}) collective-permute-start(bf16[32,768]{1,0:T(8,128)(2,1)S(1)} %get-tuple-element.28), channel_id=1, source_target_pairs={{0,8},{8,16},{16,24},{24,32},{32,40},{40,48},{48,56},{56,64},{64,7... | collective-permute-start | bytes 147464 | tf_op jit(solution)/shard_map/ppermute | solution.py:22
  29.6 17.4 %all-to-all-start.1 = ((bf16[8,32,768]{2,1,0:T(8,128)(2,1)}), bf16[8,32,768]{2,1,0:T(8,128)(2,1)S(1)}, u32[]{:S(2)}, u32[]{:S(2)}) async-start(bf16[8,32,768]{2,1,0:T(8,128)(2,1)} %broadcast_in_dim.12), calls=%async_computation.1 | async-start | bytes 786432 | tf_op jit(solution)/shard_map/all_to_all | solution.py:143
  37.4 9.6 %collective-permute-start.1 = (bf16[64,768]{1,0:T(8,128)(2,1)S(1)}, bf16[64,768]{1,0:T(8,128)(2,1)S(1)}, u32[]{:S(2)}, u32[]{:S(2)}) collective-permute-start(bf16[64,768]{1,0:T(8,128)(2,1)S(1)} %pad_maximum_fusion.2), channel_id=1, source_target_pairs={{0,16},{8,24},{16,32},{24,40},{32,48},{40,56},{48,64},{56,72},{64,... | collective-permute-start | bytes 294920 | tf_op jit(solution)/shard_map/ppermute | solution.py:22
  47.5 13.2 %collective-permute-start.5 = (bf16[64,768]{1,0:T(8,128)(2,1)S(1)}, bf16[64,768]{1,0:T(8,128)(2,1)S(1)}, u32[]{:S(2)}, u32[]{:S(2)}) collective-permute-start(bf16[64,768]{1,0:T(8,128)(2,1)S(1)} %slice.36), channel_id=1, source_target_pairs={{0,496},{8,504},{16,0},{24,8},{32,16},{40,24},{48,32},{56,40},{64,... | collective-permute-start | bytes 294920 | tf_op jit(solution)/shard_map/ppermute | solution.py:22
  55.1 13.8 %all-to-all-start.2 = ((bf16[8,32,768]{2,1,0:T(8,128)(2,1)}), bf16[8,32,768]{2,1,0:T(8,128)(2,1)S(1)}, u32[]{:S(2)}, u32[]{:S(2)}) async-start(bf16[8,32,768]{2,1,0:T(8,128)(2,1)} %bitcast.4), calls=%async_computation.2 | async-start | bytes 786432 | tf_op jit(solution)/shard_map/all_to_all | solution.py:164
  60.8 5.3 %collective-permute-start.6 = (bf16[32,768]{1,0:T(8,128)(2,1)S(1)}, bf16[32,768]{1,0:T(8,128)(2,1)S(1)}, u32[]{:S(2)}, u32[]{:S(2)}) collective-permute-start(bf16[32,768]{1,0:T(8,128)(2,1)S(1)} %slice.37), channel_id=1, source_target_pairs={{0,504},{8,0},{16,8},{24,16},{32,24},{40,32},{48,40},{56,48},{64,5... | collective-permute-start | bytes 147464 | tf_op jit(solution)/shard_map/ppermute | solution.py:22
  66.1 3.5 %copy-start.2 = (bf16[912,256]{1,0:T(8,128)(2,1)}, bf16[912,256]{1,0:T(8,128)(2,1)S(1)}, u32[]{:S(2)}) copy-start(bf16[912,256]{1,0:T(8,128)(2,1)S(1)} %collective-permute-done.4.refs_3_) | copy-start | bytes 1400836
  66.1 3.5 %copy-start.3 = (bf16[912,256]{1,0:T(8,128)(2,1)}, bf16[912,256]{1,0:T(8,128)(2,1)S(1)}, u32[]{:S(2)}) copy-start(bf16[912,256]{1,0:T(8,128)(2,1)S(1)} %collective-permute-done.3.refs_2_) | copy-start | bytes 1400836
  66.1 3.5 %copy-start.4 = (bf16[912,256]{1,0:T(8,128)(2,1)}, bf16[912,256]{1,0:T(8,128)(2,1)S(1)}, u32[]{:S(2)}) copy-start(bf16[912,256]{1,0:T(8,128)(2,1)S(1)} %collective-permute-done.2.refs_1_) | copy-start | bytes 1400836
  118.6 25.1 %all-to-all-start.4 = ((bf16[16,48,256]{2,1,0:T(8,128)(2,1)}), bf16[16,48,256]{2,1,0:T(8,128)(2,1)S(1)}, u32[]{:S(2)}, u32[]{:S(2)}) async-start(bf16[16,48,256]{2,1,0:T(8,128)(2,1)} %project_grads.1), calls=%async_computation.4 | async-start | bytes 786432 | tf_op jit(solution)/shard_map/all_to_all | solution.py:187
  143.7 0.7 copy-start

commit v5 on v4

--- a/solution.py
+++ b/solution.py
@@ -7,7 +7,9 @@
 
 STEPS = 4
 NORM_EPS = 1e-06
-X = ("xh", "xl", "core")
+CHIPS = ("xh", "xl")
+X = CHIPS + ("core",)
+Y = ("yh", "yl")
 DP = ("yh", "yl", "z")
 ACROSS = (((1,), (1,)), ((), ()))
 DOWN = (((0,), (0,)), ((), ()))
@@ -22,9 +24,14 @@
     return lax.ppermute(value, DP, pairs)
 
 
-def swapped(value, axis, bits):
-    count = lax.axis_size(axis)
-    return lax.ppermute(value, axis, [(source, source ^ bits) for source in range(count)])
+def along_y(value, steps):
+    count = lax.axis_size(Y)
+    pairs = [(source, (source + steps) % count) for source in range(count)]
+    return lax.ppermute(value, Y, pairs)
+
+
+def core_swapped(value):
+    return lax.ppermute(value, "core", [(0, 1), (1, 0)])
 
 
 def call(kernel, name, out_shape, args, flops, scratch=(), scalars=0):
@@ -40,7 +47,9 @@
     )(*args)
 
 
-def project_kernel(img_t_ref, txt_ref, img_proj_ref, txt_proj_ref, parts_ref, pack_ref):
+def project_kernel(
+    core_ref, img_t_ref, txt_ref, img_proj_ref, txt_proj_ref, mine_ref, other_ref, pack_ref, parts_ref
+):
     groups, share = parts_ref.shape[0], parts_ref.shape[1] // 2
     d_txt = txt_ref.shape[1]
     for half in range(d_txt // HALF):
@@ -53,20 +62,27 @@
         rows = slice(member * share, (member + 1) * share)
         parts_ref[member, :share] = img[rows]
         parts_ref[member, share:] = txt[rows]
-
-
-def wgrad_kernel(place_ref, cols_ref, *refs):
-    lines, out_ref, total_ref = refs[:-2], refs[-2], refs[-1]
-    groups, quad, share, wide = cols_ref.shape
-    wide //= 2
+    core = core_ref[0]
+    for chip in range(groups // 2):
+        mine_ref[chip] = parts_ref[2 * chip + core]
+        other_ref[chip] = parts_ref[2 * chip + 1 - core]
+
+
+def wgrad_kernel(core_ref, mine_ref, other_ref, *refs):
+    lines, out_ref, total_ref, cols_ref = refs[:-3], refs[-3], refs[-2], refs[-1]
+    chips, height, wide = mine_ref.shape
+    share = height // 8
     d_all = lines[0].shape[0]
     d_txt = 2 * HALF
     d_img = d_all - d_txt
     sums = [None] * 3
-    for bits, line_ref in enumerate(lines):
-        cols = cols_ref[:, place_ref[0] ^ bits].reshape(groups * share, 2 * wide)
-        cols = cols.T
-        img_cols, txt_cols = cols[:wide], cols[wide:]
+    for step, line_ref in enumerate(lines):
+        for chip in range(chips):
+            for ref, core in ((mine_ref, core_ref[0]), (other_ref, 1 - core_ref[0])):
+                row = pl.multiple_of((2 * chip + core) * share, share)
+                cols_ref[step, pl.ds(row, share)] = ref[chip, step * share : (step + 1) * share]
+        cols = cols_ref[step].T
+        img_cols, txt_cols = cols[: wide // 2], cols[wide // 2 :]
         terms = [
             jnp.dot(txt_cols, line_ref[:HALF], preferred_element_type=F32),
             jnp.dot(txt_cols, line_ref[HALF:d_txt], preferred_element_type=F32),
@@ -98,16 +114,24 @@
     img_ref[:, HALF:] = total_ref[3 * take :, : d_img - HALF]
 
 
-def feature_grads_kernel(rows_ref, img_proj_ref, txt_proj_ref, img_ref, txt_ref):
-    groups, share, embed = rows_ref.shape
-    share //= 2
-    img_rows = rows_ref[:, :share].reshape(groups * share, embed)
-    txt_rows = rows_ref[:, share:].reshape(groups * share, embed)
+def feature_grads_kernel(
+    core_ref, mine_ref, other_ref, img_proj_ref, txt_proj_ref, img_ref, txt_ref, img_rows, txt_rows
+):
+    chips, height, wide = mine_ref.shape
+    share = height // 8
+    for chip in range(chips):
+        for ref, core in ((mine_ref, core_ref[0]), (other_ref, 1 - core_ref[0])):
+            row = pl.multiple_of((2 * chip + core) * share, share)
+            for part in range(2):
+                lanes = slice(part * wide, (part + 1) * wide)
+                first = (4 + 2 * part) * share
+                img_rows[pl.ds(row, share), lanes] = ref[chip, first : first + share]
+                txt_rows[pl.ds(row, share), lanes] = ref[chip, first + share : first + 2 * share]
     txt_ref[...] = lax.dot_general(
-        txt_rows, txt_proj_ref[...], ACROSS, preferred_element_type=F32
+        txt_rows[...], txt_proj_ref[...], ACROSS, preferred_element_type=F32
     ).astype(BF16)
     img_ref[...] = lax.dot_general(
-        img_proj_ref[...], img_rows, ACROSS, preferred_element_type=F32
+        img_proj_ref[...], img_rows[...], ACROSS, preferred_element_type=F32
     ).astype(BF16)
 
 
@@ -122,18 +146,21 @@
     share = rows // groups
     d_img, d_txt = image_feats.shape[1], text_feats.shape[1]
     embed = image_proj.shape[1]
-    parts, pack = call(
+    chips = lax.axis_size(CHIPS)
+    core_index = lax.axis_index("core").astype(jnp.int32).reshape(1)
+    halves = jax.ShapeDtypeStruct((chips, 2 * share, embed), BF16)
+    mine, other, pack = call(
         project_kernel,
         "project",
-        (
-            jax.ShapeDtypeStruct((groups, 2 * share, embed), BF16),
-            jax.ShapeDtypeStruct((d_txt + d_img, HALF), BF16),
-        ),
-        (image_feats.T, text_feats, image_proj, text_proj),
+        (halves, halves, jax.ShapeDtypeStruct((d_txt + d_img, HALF), BF16)),
+        (core_index, image_feats.T, text_feats, image_proj, text_proj),
         2 * rows * (d_img + d_txt) * embed,
-    )
-    lines = [pack] + [swapped(pack, "yl", bits) for bits in range(1, quad)]
-    parts = lax.all_to_all(parts, X, 0, 0, tiled=True)
+        scratch=(pltpu.VMEM((groups, 2 * share, embed), BF16),),
+        scalars=1,
+    )
+    parts = (mine.astype(F32) + core_swapped(other).astype(F32)).astype(BF16)
+    lines = [along_y(pack, 1), pack, along_y(pack, -1), along_y(pack, -2)]
+    parts = lax.all_to_all(parts, CHIPS, 0, 0, tiled=True)
     summed = jnp.sum(parts.astype(F32), axis=0)
     length = jnp.sqrt(jnp.sum(summed * summed, axis=1, keepdims=True) + NORM_EPS)
     unit = summed / length
@@ -169,29 +196,40 @@
     grad_img = jnp.sum(img_terms.astype(F32), axis=0)
     grad = jnp.concatenate([grad_img, grad_txt])
     grad_summed = ((grad - unit * jnp.sum(unit * grad, axis=1, keepdims=True)) / length).astype(BF16)
-    strip = embed // (blocks // lax.axis_size("z"))
+    strip = embed // lax.axis_size(Y)
     by_cols = grad_summed.reshape(2, share, embed // (quad * strip), quad, strip)
     by_cols = by_cols.transpose(3, 1, 0, 2, 4).reshape(quad, share, 2 * embed // quad)
-    by_cols = lax.all_to_all(by_cols, "yl", 0, 0, tiled=True)
-    cols_all = lax.all_gather(by_cols, X, axis=0, tiled=False)
+    by_cols = jnp.concatenate([by_cols] * (lax.axis_size(Y) // quad))
+    by_cols = lax.all_to_all(by_cols, Y, 0, 0, tiled=True)
+    y_index = lax.axis_index(Y)
+    window = [
+        lax.dynamic_index_in_dim(by_cols, lax.rem(y_index + (step + lax.axis_size(Y)), lax.axis_size(Y)), 0, False)
+        for step in (-1, 0, 1, 2)
+    ]
+    wide = 2 * embed // quad
+    mine = jnp.concatenate(window + [grad_summed[:, :wide], grad_summed[:, wide:]])
+    mine = jnp.broadcast_to(mine[None], (chips,) + mine.shape)
+    mine = lax.all_to_all(mine, CHIPS, 0, 0, tiled=True)
+    other = core_swapped(mine)
     height = 4 * embed // blocks
     wgrad = call(
         wgrad_kernel,
         "project_grads",
         jax.ShapeDtypeStruct((peers, height, HALF), BF16),
-        (lax.axis_index("yl").astype(jnp.int32).reshape(1), cols_all, *lines),
+        (core_index, mine, other, *lines),
         2 * quad * rows * (embed // quad) * (d_img + d_txt),
-        scratch=(pltpu.VMEM((peers, height, HALF), F32),),
+        scratch=(pltpu.VMEM((peers, height, HALF), F32), pltpu.VMEM((quad, rows, wide), BF16)),
         scalars=1,
     )
     wgrad = lax.all_to_all(wgrad, ("yh", "z"), 0, 0, tiled=True)
-    rows_all = lax.all_gather(grad_summed, X, axis=0, tiled=False)
     image_grad, text_grad = call(
         feature_grads_kernel,
         "feature_grads",
         (jax.ShapeDtypeStruct((d_img, rows), BF16), jax.ShapeDtypeStruct((rows, d_txt), BF16)),
-        (rows_all, image_proj, text_proj),
+        (core_index, mine, other, image_proj, text_proj),
         2 * rows * (d_img + d_txt) * embed,
+        scratch=(pltpu.VMEM((rows, embed), BF16), pltpu.VMEM((rows, embed), BF16)),
+        scalars=1,
     )
     img_wgrad, txt_wgrad = call(
         total_kernel,

time: 147 us -> 141 us (0.959)
  the two profiles are of different devices: /device:TPU:1 before, /device:TPU:16 now
where the time goes in v5:
time: 141 us; the launch traced here: 140 us
  starting transfers between devices  53.7 us (38%)
  waiting for transfers between devices  50 us (35%)
  blocking collectives  13.2 us (9%)
  Pallas kernels  11.3 us (8%)
  local copies, waits for them, and re-layouts  4.2 us (3%)
  other arithmetic  3.5 us (2%)
  between operations  2.28 us (2%)
  matrix products  1.51 us (1%)
    ppermute x4, waiting for transfers between devices, shifted(): return lax.ppermute(value, DP, pairs)  20.3 us
    all_to_all x1, waiting for transfers between devices, on_device(): wgrad = lax.all_to_all(wgrad, ('yh', 'z'), 0, 0, tiled=True)  15.3 us
    all_to_all x1, blocking collectives, on_device(): mine = lax.all_to_all(mine, CHIPS, 0, 0, tiled=True)  13.2 us
    ppermute x3, starting transfers between devices, along_y(): return lax.ppermute(value, Y, pairs)  12.6 us
    pallas_call x4, Pallas kernels, call(): pl.pallas_call(kernel, out_shape=out_shape, in_specs=[pl.BlockSpec(memory...  11.3 us
    all_to_all x1, starting transfers between devices, on_device(): wgrad = lax.all_to_all(wgrad, ('yh', 'z'), 0, 0, tiled=True)  7.89 us
    all_to_all x1, starting transfers between devices, on_device(): by_cols = lax.all_to_all(by_cols, Y, 0, 0, tiled=True)  7.85 us
    ppermute x4, starting transfers between devices, shifted(): return lax.ppermute(value, DP, pairs)  7.78 us
  transfers between devices with their start and end apart: 14, of which 8 were waited for; matrix products, arithmetic and copies ran while one was open for 2% of the time, Pallas kernels for 2%

profile of v5, /device:TPU:16, one launch (start us, length us, event | category | flops | bytes accessed | tf_op | source)
XLA Modules:
  0.0 139.6 jit_solution(18212699108604788008)
XLA Ops:
  0.6 3.2 %project.1 = (bf16[4,64,768]{2,1,0:T(8,128)(2,1)}, bf16[4,64,768]{2,1,0:T(8,128)(2,1)}, bf16[912,256]{1,0:T(8,128)(2,1)}) custom-call(s32[1]{0:T(128)} %bitcast.core_ref, bf16[400,256]{1,0:T(8,128)(2,1)} %bitcast.28, bf16[256,512]{1,0:T(8,128)(2,1)} %txt_ref.1, bf16[400,768]{1,0:T(8,128)(2,1)} %img_proj_ref.3, bf16[512,768]{1,0:T(8,128)(2,1)} %txt_proj_ref.3), custom_call_target="tpu_custom_call" | custom-call | flops 358612992 | bytes 4000000 | tf_op jit(solution)/shard_map/project/pallas_call | solution.py:39
  3.8 1.9 %collective-permute-start = (bf16[4,64,768]{2,1,0:T(8,128)(2,1)}, bf16[4,64,768]{2,1,0:T(8,128)(2,1)S(1)}, u32[]{:S(2)}, u32[]{:S(2)}) collective-permute-start(bf16[4,64,768]{2,1,0:T(8,128)(2,1)} %get-tuple-element.17), channel_id=1, source_target_pairs={{0,1},{1,0},{2,3},{3,2},{4,5},{5,4},{6,7},{7,6},{8,9},{9,8},{10,11... | collective-permute-start | bytes 1179656 | tf_op jit(solution)/shard_map/ppermute | solution.py:34
  5.7 1.9 %collective-permute-done = bf16[4,64,768]{2,1,0:T(8,128)(2,1)S(1)} collective-permute-done((bf16[4,64,768]{2,1,0:T(8,128)(2,1)}, bf16[4,64,768]{2,1,0:T(8,128)(2,1)S(1)}, u32[]{:S(2)}, u32[]{:S(2)}) %collective-permute-start) | collective-permute-done | bytes 393248 | tf_op jit(solution)/shard_map/ppermute | solution.py:34
  7.6 1.8 %add_convert_fusion = bf16[4,64,768]{2,1,0:T(8,128)(2,1)} fusion(bf16[4,64,768]{2,1,0:T(8,128)(2,1)S(1)} %collective-permute-done, bf16[4,64,768]{2,1,0:T(8,128)(2,1)} %get-tuple-element.16), kind=kLoop, calls=%fused_computation.13 | loop fusion | flops 786432 | bytes 1179648 | tf_op jit(solution)/shard_map/convert_element_type | solution.py:161
  9.5 4.4 %all-to-all-start = ((bf16[4,64,768]{2,1,0:T(8,128)(2,1)}), bf16[4,64,768]{2,1,0:T(8,128)(2,1)S(1)}, u32[]{:S(2)}, u32[]{:S(2)}) async-start(bf16[4,64,768]{2,1,0:T(8,128)(2,1)} %add_convert_fusion), calls=%async_computation | async-start | bytes 786432 | tf_op jit(solution)/shard_map/all_to_all | solution.py:163
  13.9 6.8 %collective-permute-start.5 = (bf16[912,256]{1,0:T(8,128)(2,1)S(1)}, bf16[912,256]{1,0:T(8,128)(2,1)S(1)}, u32[]{:S(2)}, u32[]{:S(2)}) collective-permute-start(bf16[912,256]{1,0:T(8,128)(2,1)S(1)} %copy-done.3), channel_id=1, source_target_pairs={{0,384},{64,448},{128,0},{192,64},{256,128},{320,192},{384,256},{4... | collective-permute-start | bytes 1400840 | tf_op jit(solution)/shard_map/ppermute | solution.py:30
  20.7 1.9 %collective-permute-start.4 = (bf16[912,256]{1,0:T(8,128)(2,1)S(1)}, bf16[912,256]{1,0:T(8,128)(2,1)S(1)}, u32[]{:S(2)}, u32[]{:S(2)}) collective-permute-start(bf16[912,256]{1,0:T(8,128)(2,1)S(1)} %copy-done.3), channel_id=1, source_target_pairs={{0,448},{64,0},{128,64},{192,128},{256,192},{320,256},{384,320},{4... | collective-permute-start | bytes 1400840 | tf_op jit(solution)/shard_map/ppermute | solution.py:30
  22.6 3.9 %collective-permute-start.3 = (bf16[912,256]{1,0:T(8,128)(2,1)S(1)}, bf16[912,256]{1,0:T(8,128)(2,1)S(1)}, u32[]{:S(2)}, u32[]{:S(2)}) collective-permute-start(bf16[912,256]{1,0:T(8,128)(2,1)S(1)} %copy-done.3), channel_id=1, source_target_pairs={{0,64},{64,128},{128,192},{192,256},{256,320},{320,384},{384,448},... | collective-permute-start | bytes 1400840 | tf_op jit(solution)/shard_map/ppermute | solution.py:30
  26.9 1.9 %collective-permute-start.1 = (bf16[32,768]{1,0:T(8,128)(2,1)S(1)}, bf16[32,768]{1,0:T(8,128)(2,1)S(1)}, u32[]{:S(2)}, u32[]{:S(2)}) collective-permute-start(bf16[32,768]{1,0:T(8,128)(2,1)S(1)} %get-tuple-element.30), channel_id=1, source_target_pairs={{0,8},{8,16},{16,24},{24,32},{32,40},{40,48},{48,56},{56,64},{64,7... | collective-permute-start | bytes 147464 | tf_op jit(solution)/shard_map/ppermute | solution.py:24
  28.8 0.8 broadcast_in_dim.14
  29.6 4.7 %all-to-all-start.1 = ((bf16[8,32,768]{2,1,0:T(8,128)(2,1)}), bf16[8,32,768]{2,1,0:T(8,128)(2,1)S(1)}, u32[]{:S(2)}, u32[]{:S(2)}) async-start(bf16[8,32,768]{2,1,0:T(8,128)(2,1)} %broadcast_in_dim.14), calls=%async_computation.1 | async-start | bytes 786432 | tf_op jit(solution)/shard_map/all_to_all | solution.py:170
  34.4 10.5 %collective-permute-done.1 = bf16[32,768]{1,0:T(8,128)(2,1)S(1)} collective-permute-done((bf16[32,768]{1,0:T(8,128)(2,1)S(1)}, bf16[32,768]{1,0:T(8,128)(2,1)S(1)}, u32[]{:S(2)}, u32[]{:S(2)}) %collective-permute-start.1) | collective-permute-done | bytes 49184 | tf_op jit(solution)/shard_map/ppermute | solution.py:24
  44.8 1.9 %collective-permute-start.2 = (bf16[64,768]{1,0:T(8,128)(2,1)S(1)}, bf16[64,768]{1,0:T(8,128)(2,1)S(1)}, u32[]{:S(2)}, u32[]{:S(2)}) collective-permute-start(bf16[64,768]{1,0:T(8,128)(2,1)S(1)} %pad_maximum_fusion.3), channel_id=1, source_target_pairs={{0,16},{8,24},{16,32},{24,40},{32,48},{40,56},{48,64},{56,72},{64,... | collective-permute-start | bytes 294920 | tf_op jit(solution)/shard_map/ppermute | solution.py:24
  48.2 6.1 %collective-permute-done.2 = bf16[64,768]{1,0:T(8,128)(2,1)S(1)} collective-permute-done((bf16[64,768]{1,0:T(8,128)(2,1)S(1)}, bf16[64,768]{1,0:T(8,128)(2,1)S(1)}, u32[]{:S(2)}, u32[]{:S(2)}) %collective-permute-start.2) | collective-permute-done | bytes 98336 | tf_op jit(solution)/shard_map/ppermute | solution.py:24
  55.6 1.9 %collective-permute-start.6 = (bf16[64,768]{1,0:T(8,128)(2,1)S(1)}, bf16[64,768]{1,0:T(8,128)(2,1)S(1)}, u32[]{:S(2)}, u32[]{:S(2)}) collective-permute-start(bf16[64,768]{1,0:T(8,128)(2,1)S(1)} %slice.48), channel_id=1, source_target_pairs={{0,496},{8,504},{16,0},{24,8},{32,16},{40,24},{48,32},{56,40},{64,... | collective-permute-start | bytes 294920 | tf_op jit(solution)/shard_map/ppermute | solution.py:24
  57.5 1.0 convolution_convert_fusion
  58.5 4.5 %all-to-all-start.2 = ((bf16[8,32,768]{2,1,0:T(8,128)(2,1)}), bf16[8,32,768]{2,1,0:T(8,128)(2,1)S(1)}, u32[]{:S(2)}, u32[]{:S(2)}) async-start(bf16[8,32,768]{2,1,0:T(8,128)(2,1)} %bitcast.5), calls=%async_computation.2 | async-start | bytes 786432 | tf_op jit(solution)/shard_map/all_to_all | solution.py:191
  63.1 2.0 %collective-permute-start.7 = (bf16[32,768]{1,0:T(8,128)(2,1)S(1)}, bf16[32,768]{1,0:T(8,128)(2,1)S(1)}, u32[]{:S(2)}, u32[]{:S(2)}) collective-permute-start(bf16[32,768]{1,0:T(8,128)(2,1)S(1)} %slice.49), channel_id=1, source_target_pairs={{0,504},{8,0},{16,8},{24,16},{32,24},{40,32},{48,40},{56,48},{64,5... | collective-permute-start | bytes 147464 | tf_op jit(solution)/shard_map/ppermute | solution.py:24
  65.4 3.7 %collective-permute-done.7 = bf16[32,768]{1,0:T(8,128)(2,1)S(1)} collective-permute-done((bf16[32,768]{1,0:T(8,128)(2,1)S(1)}, bf16[32,768]{1,0:T(8,128)(2,1)S(1)}, u32[]{:S(2)}, u32[]{:S(2)}) %collective-permute-start.7) | collective-permute-done | bytes 49184 | tf_op jit(solution)/shard_map/ppermute | solution.py:24
  69.2 2.8 %all-to-all-done.2 = bf16[8,32,768]{2,1,0:T(8,128)(2,1)S(1)} async-done(((bf16[8,32,768]{2,1,0:T(8,128)(2,1)}), bf16[8,32,768]{2,1,0:T(8,128)(2,1)S(1)}, u32[]{:S(2)}, u32[]{:S(2)}) %all-to-all-start.2) | async-done | bytes 393248 | tf_op jit(solution)/shard_map/all_to_all | solution.py:191
  73.8 7.9 %all-to-all-start.3 = ((bf16[8,32,384]{2,1,0:T(8,128)(2,1)}), bf16[8,32,384]{2,1,0:T(8,128)(2,1)S(1)}, u32[]{:S(2)}, u32[]{:S(2)}) async-start(bf16[8,32,384]{2,1,0:T(8,128)(2,1)} %pad_maximum_fusion.2), calls=%async_computation.3 | async-start | bytes 393216 | tf_op jit(solution)/shard_map/all_to_all | solution.py:203
  81.7 7.4 %all-to-all-done.3 = bf16[8,32,384]{2,1,0:T(8,128)(2,1)S(1)} async-done(((bf16[8,32,384]{2,1,0:T(8,128)(2,1)}), bf16[8,32,384]{2,1,0:T(8,128)(2,1)S(1)}, u32[]{:S(2)}, u32[]{:S(2)}) %all-to-all-start.3) | async-done | bytes 196640 | tf_op jit(solution)/shard_map/all_to_all | solution.py:203
  89.2 13.2 %all_to_all.30.mine_ref = bf16[4,256,384]{2,1,0:T(8,128)(2,1)S(1)} all-to-all(bf16[4,256,384]{2,1,0:T(8,128)(2,1)S(1)} %broadcast_in_dim.15), channel_id=1, replica_groups=mesh['yh'=2,'yl'=4,'z'=8,'xh'=2,'xl'=2,'core'=2] {'xh','xl'}, dimensions={0} | all-to-all | bytes 1572864 | tf_op jit(solution)/shard_map/all_to_all | solution.py:212
  102.4 1.9 %collective-permute-start.8 = (bf16[4,256,384]{2,1,0:T(8,128)(2,1)S(1)}, bf16[4,256,384]{2,1,0:T(8,128)(2,1)S(1)}, u32[]{:S(2)}, u32[]{:S(2)}) collective-permute-start(bf16[4,256,384]{2,1,0:T(8,128)(2,1)S(1)} %all_to_all.30.mine_ref), channel_id=1, source_target_pairs={{0,1},{1,0},{2,3},{3,2},{4,5},{5,4},{6,7},{7,6},{8,9},{9,8},{10,11... | collective-permute-start | bytes 2359304 | tf_op jit(solution)/shard_map/ppermute | solution.py:34
  104.4 2.3 %collective-permute-done.8.other_ref = bf16[4,256,384]{2,1,0:T(8,128)(2,1)S(1)} collective-permute-done((bf16[4,256,384]{2,1,0:T(8,128)(2,1)S(1)}, bf16[4,256,384]{2,1,0:T(8,128)(2,1)S(1)}, u32[]{:S(2)}, u32[]{:S(2)}) %collective-permute-start.8) | collective-permute-done | bytes 786464 | tf_op jit(solution)/shard_map/ppermute | solution.py:34
  106.6 0.9 copy-done.1
  107.5 3.4 %project_grads.1 = bf16[16,48,256]{2,1,0:T(8,128)(2,1)} custom-call(s32[1]{0:T(128)} %bitcast.core_ref, bf16[4,256,384]{2,1,0:T(8,128)(2,1)} %copy-done, bf16[4,256,384]{2,1,0:T(8,128)(2,1)} %copy-done.1, bf16[912,256]{1,0:T(8,128)(2,1)} %copy-done.6, bf16[912,256]{1,0:T(8,128)(2,1)} %get-tuple-element.23.refs_1_, bf16[912,256]{1,0:T(8,128)(2,1)} %copy-done.5, ...), custom_call_target="tpu_custom_call" | custom-call | flops 358612992 | bytes 4000000 | tf_op jit(solution)/shard_map/project_grads/pallas_call | solution.py:39
  110.9 7.9 %all-to-all-start.5 = ((bf16[16,48,256]{2,1,0:T(8,128)(2,1)}), bf16[16,48,256]{2,1,0:T(8,128)(2,1)S(1)}, u32[]{:S(2)}, u32[]{:S(2)}) async-start(bf16[16,48,256]{2,1,0:T(8,128)(2,1)} %project_grads.1), calls=%async_computation.5 | async-start | bytes 786432 | tf_op jit(solution)/shard_map/all_to_all | solution.py:224
  118.8 3.0 %feature_grads.1 = (bf16[400,256]{1,0:T(8,128)(2,1)}, bf16[256,512]{1,0:T(8,128)(2,1)}) custom-call(s32[1]{0:T(128)} %bitcast.core_ref, bf16[4,256,384]{2,1,0:T(8,128)(2,1)} %copy-done, bf16[4,256,384]{2,1,0:T(8,128)(2,1)} %copy-done.1, bf16[400,768]{1,0:T(8,128)(2,1)} %img_proj_ref.3, bf16[512,768]{1,0:T(8,128)(2,1)} %txt_proj_ref.3), custom_call_target="tpu_custom_call" | custom-call | flops 358612992 | bytes 4000000 | tf_op jit(solution)/shard_map/feature_grads/pallas_call | solution.py:39
  121.9 15.3 %all-to-all-done.5.blocks_ref = bf16[16,48,256]{2,1,0:T(8,128)(2,1)S(1)} async-done(((bf16[16,48,256]{2,1,0:T(8,128)(2,1)}), bf16[16,48,256]{2,1,0:T(8,128)(2,1)S(1)}, u32[]{:S(2)}, u32[]{:S(2)}) %all-to-all-start.5) | async-done | bytes 393248 | tf_op jit(solution)/shard_map/all_to_all | solution.py:224
  137.2 0.8 copy-done.2
  137.9 1.7 %total.1 = (f32[12,400]{1,0:T(8,128)}, f32[12,512]{1,0:T(8,128)}) custom-call(bf16[16,48,256]{2,1,0:T(8,128)(2,1)} %copy-done.2), custom_call_target="tpu_custom_call" | custom-call | flops 196608 | bytes 4000000 | tf_op jit(solution)/shard_map/total/pallas_call | solution.py:39
  (53 shorter events, 3.9 us)
Async XLA Ops:
  3.8 3.8 %collective-permute-start = (bf16[4,64,768]{2,1,0:T(8,128)(2,1)}, bf16[4,64,768]{2,1,0:T(8,128)(2,1)S(1)}, u32[]{:S(2)}, u32[]{:S(2)}) collective-permute-start(bf16[4,64,768]{2,1,0:T(8,128)(2,1)} %get-tuple-element.17), channel_id=1, source_target_pairs={{0,1},{1,0},{2,3},{3,2},{4,5},{5,4},{6,7},{7,6},{8,9},{9,8},{10,11... | collective-permute-start | bytes 1179656 | tf_op jit(solution)/shard_map/ppermute | solution.py:34
  9.5 4.4 %copy-start.3 = (bf16[912,256]{1,0:T(8,128)(2,1)S(1)}, bf16[912,256]{1,0:T(8,128)(2,1)}, u32[]{:S(2)}) copy-start(bf16[912,256]{1,0:T(8,128)(2,1)} %get-tuple-element.23.refs_1_) | copy-start | bytes 1400836
  9.5 17.1 %all-to-all-start = ((bf16[4,64,768]{2,1,0:T(8,128)(2,1)}), bf16[4,64,768]{2,1,0:T(8,128)(2,1)S(1)}, u32[]{:S(2)}, u32[]{:S(2)}) async-start(bf16[4,64,768]{2,1,0:T(8,128)(2,1)} %add_convert_fusion), calls=%async_computation | async-start | bytes 786432 | tf_op jit(solution)/shard_map/all_to_all | solution.py:163
  13.9 55.3 %collective-permute-start.5 = (bf16[912,256]{1,0:T(8,128)(2,1)S(1)}, bf16[912,256]{1,0:T(8,128)(2,1)S(1)}, u32[]{:S(2)}, u32[]{:S(2)}) collective-permute-start(bf16[912,256]{1,0:T(8,128)(2,1)S(1)} %copy-done.3), channel_id=1, source_target_pairs={{0,384},{64,448},{128,0},{192,64},{256,128},{320,192},{384,256},{4... | collective-permute-start | bytes 1400840 | tf_op jit(solution)/shard_map/ppermute | solution.py:30
  20.7 48.5 %collective-permute-start.4 = (bf16[912,256]{1,0:T(8,128)(2,1)S(1)}, bf16[912,256]{1,0:T(8,128)(2,1)S(1)}, u32[]{:S(2)}, u32[]{:S(2)}) collective-permute-start(bf16[912,256]{1,0:T(8,128)(2,1)S(1)} %copy-done.3), channel_id=1, source_target_pairs={{0,448},{64,0},{128,64},{192,128},{256,192},{320,256},{384,320},{4... | collective-permute-start | bytes 1400840 | tf_op jit(solution)/shard_map/ppermute | solution.py:30
  22.6 46.6 %collective-permute-start.3 = (bf16[912,256]{1,0:T(8,128)(2,1)S(1)}, bf16[912,256]{1,0:T(8,128)(2,1)S(1)}, u32[]{:S(2)}, u32[]{:S(2)}) collective-permute-start(bf16[912,256]{1,0:T(8,128)(2,1)S(1)} %copy-done.3), channel_id=1, source_target_pairs={{0,64},{64,128},{128,192},{192,256},{256,320},{320,384},{384,448},... | collective-permute-start | bytes 1400840 | tf_op jit(solution)/shard_map/ppermute | solution.py:30
  26.9 17.9 %collective-permute-start.1 = (bf16[32,768]{1,0:T(8,128)(2,1)S(1)}, bf16[32,768]{1,0:T(8,128)(2,1)S(1)}, u32[]{:S(2)}, u32[]{:S(2)}) collective-permute-start(bf16[32,768]{1,0:T(8,128)(2,1)S(1)} %get-tuple-element.30), channel_id=1, source_target_pairs={{0,8},{8,16},{16,24},{24,32},{32,40},{40,48},{48,56},{56,64},{64,7... | collective-permute-start | bytes 147464 | tf_op jit(solution)/shard_map/ppermute | solution.py:24
  29.6 24.8 %all-to-all-start.1 = ((bf16[8,32,768]{2,1,0:T(8,128)(2,1)}), bf16[8,32,768]{2,1,0:T(8,128)(2,1)S(1)}, u32[]{:S(2)}, u32[]{:S(2)}) async-start(bf16[8,32,768]{2,1,0:T(8,128)(2,1)} %broadcast_in_dim.14), calls=%async_computation.1 | async-start | bytes 786432 | tf_op jit(solution)/shard_map/all_to_all | solution.py:170
  44.8 9.5 %collective-permute-start.2 = (bf16[64,768]{1,0:T(8,128)(2,1)S(1)}, bf16[64,768]{1,0:T(8,128)(2,1)S(1)}, u32[]{:S(2)}, u32[]{:S(2)}) collective-permute-start(bf16[64,768]{1,0:T(8,128)(2,1)S(1)} %pad_maximum_fusion.3), channel_id=1, source_target_pairs={{0,16},{8,24},{16,32},{24,40},{32,48},{40,56},{48,64},{56,72},{64,... | collective-permute-start | bytes 294920 | tf_op jit(solution)/shard_map/ppermute | solution.py:24
  54.4 0.7 copy-start.7
  55.6 7.5 %collective-permute-start.6 = (bf16[64,768]{1,0:T(8,128)(2,1)S(1)}, bf16[64,768]{1,0:T(8,128)(2,1)S(1)}, u32[]{:S(2)}, u32[]{:S(2)}) collective-permute-start(bf16[64,768]{1,0:T(8,128)(2,1)S(1)} %slice.48), channel_id=1, source_target_pairs={{0,496},{8,504},{16,0},{24,8},{32,16},{40,24},{48,32},{56,40},{64,... | collective-permute-start | bytes 294920 | tf_op jit(solution)/shard_map/ppermute | solution.py:24
  58.5 13.5 %all-to-all-start.2 = ((bf16[8,32,768]{2,1,0:T(8,128)(2,1)}), bf16[8,32,768]{2,1,0:T(8,128)(2,1)S(1)}, u32[]{:S(2)}, u32[]{:S(2)}) async-start(bf16[8,32,768]{2,1,0:T(8,128)(2,1)} %bitcast.5), calls=%async_computation.2 | async-start | bytes 786432 | tf_op jit(solution)/shard_map/all_to_all | solution.py:191
  63.1 6.0 %collective-permute-start.7 = (bf16[32,768]{1,0:T(8,128)(2,1)S(1)}, bf16[32,768]{1,0:T(8,128)(2,1)S(1)}, u32[]{:S(2)}, u32[]{:S(2)}) collective-permute-start(bf16[32,768]{1,0:T(8,128)(2,1)S(1)} %slice.49), channel_id=1, source_target_pairs={{0,504},{8,0},{16,8},{24,16},{32,24},{40,32},{48,40},{56,48},{64,5... | collective-permute-start | bytes 147464 | tf_op jit(solution)/shard_map/ppermute | solution.py:24
  69.2 3.2 %copy-start.4 = (bf16[912,256]{1,0:T(8,128)(2,1)}, bf16[912,256]{1,0:T(8,128)(2,1)S(1)}, u32[]{:S(2)}) copy-start(bf16[912,256]{1,0:T(8,128)(2,1)S(1)} %collective-permute-done.5.refs_3_) | copy-start | bytes 1400836
  69.2 3.2 %copy-start.5 = (bf16[912,256]{1,0:T(8,128)(2,1)}, bf16[912,256]{1,0:T(8,128)(2,1)S(1)}, u32[]{:S(2)}) copy-start(bf16[912,256]{1,0:T(8,128)(2,1)S(1)} %collective-permute-done.4.refs_2_) | copy-start | bytes 1400836
  69.2 3.2 %copy-start.6 = (bf16[912,256]{1,0:T(8,128)(2,1)}, bf16[912,256]{1,0:T(8,128)(2,1)S(1)}, u32[]{:S(2)}) copy-start(bf16[912,256]{1,0:T(8,128)(2,1)S(1)} %collective-permute-done.3.refs_0_) | copy-start | bytes 1400836
  73.8 15.2 %all-to-all-start.3 = ((bf16[8,32,384]{2,1,0:T(8,128)(2,1)}), bf16[8,32,384]{2,1,0:T(8,128)(2,1)S(1)}, u32[]{:S(2)}, u32[]{:S(2)}) async-start(bf16[8,32,384]{2,1,0:T(8,128)(2,1)} %pad_maximum_fusion.2), calls=%async_computation.3 | async-start | bytes 393216 | tf_op jit(solution)/shard_map/all_to_all | solution.py:203
  102.4 4.2 %copy-start = (bf16[4,256,384]{2,1,0:T(8,128)(2,1)}, bf16[4,256,384]{2,1,0:T(8,128)(2,1)S(1)}, u32[]{:S(2)}) copy-start(bf16[4,256,384]{2,1,0:T(8,128)(2,1)S(1)} %all_to_all.30.mine_ref) | copy-start | bytes 2359300
  102.4 4.2 %collective-permute-start.8 = (bf16[4,256,384]{2,1,0:T(8,128)(2,1)S(1)}, bf16[4,256,384]{2,1,0:T(8,128)(2,1)S(1)}, u32[]{:S(2)}, u32[]{:S(2)}) collective-permute-start(bf16[4,256,384]{2,1,0:T(8,128)(2,1)S(1)} %all_to_all.30.mine_ref), channel_id=1, source_target_pairs={{0,1},{1,0},{2,3},{3,2},{4,5},{5,4},{6,7},{7,6},{8,9},{9,8},{10,11... | collective-permute-start | bytes 2359304 | tf_op jit(solution)/shard_map/ppermute | solution.py:34
  106.6 0.9 copy-start.1
  110.9 26.3 %all-to-all-start.5 = ((bf16[16,48,256]{2,1,0:T(8,128)(2,1)}), bf16[16,48,256]{2,1,0:T(8,128)(2,1)S(1)}, u32[]{:S(2)}, u32[]{:S(2)}) async-start(bf16[16,48,256]{2,1,0:T(8,128)(2,1)} %project_grads.1), calls=%async_computation.5 | async-start | bytes 786432 | tf_op jit(solution)/shard_map/all_to_all | solution.py:224
  137.2 0.8 copy-start.2

commit v6 on v5

--- a/solution.py
+++ b/solution.py
@@ -30,26 +30,28 @@
     return lax.ppermute(value, Y, pairs)
 
 
+def swapped(value, axis):
+    return lax.ppermute(value, axis, [(0, 1), (1, 0)])
+
+
 def core_swapped(value):
-    return lax.ppermute(value, "core", [(0, 1), (1, 0)])
-
-
-def call(kernel, name, out_shape, args, flops, scratch=(), scalars=0):
+    return swapped(value, "core")
+
+
+def call(kernel, name, out_shape, args, flops, scratch=(), scalars=0, vmem=VMEM):
     spaces = [pltpu.SMEM] * scalars + [pltpu.VMEM] * (len(args) - scalars)
     return pl.pallas_call(
         kernel,
         out_shape=out_shape,
         in_specs=[pl.BlockSpec(memory_space=space) for space in spaces],
         scratch_shapes=list(scratch),
-        compiler_params=pltpu.CompilerParams(vmem_limit_bytes=VMEM),
+        compiler_params=pltpu.CompilerParams(vmem_limit_bytes=vmem),
         cost_estimate=pl.CostEstimate(flops=flops, bytes_accessed=4_000_000, transcendentals=0),
         name=name,
     )(*args)
 
 
-def project_kernel(
-    core_ref, img_t_ref, txt_ref, img_proj_ref, txt_proj_ref, mine_ref, other_ref, pack_ref, parts_ref
-):
+def project_kernel(img_t_ref, txt_ref, img_proj_ref, txt_proj_ref, parts_ref, pack_ref):
     groups, share = parts_ref.shape[0], parts_ref.shape[1] // 2
     d_txt = txt_ref.shape[1]
     for half in range(d_txt // HALF):
@@ -62,16 +64,12 @@
         rows = slice(member * share, (member + 1) * share)
         parts_ref[member, :share] = img[rows]
         parts_ref[member, share:] = txt[rows]
-    core = core_ref[0]
-    for chip in range(groups // 2):
-        mine_ref[chip] = parts_ref[2 * chip + core]
-        other_ref[chip] = parts_ref[2 * chip + 1 - core]
 
 
 def wgrad_kernel(core_ref, mine_ref, other_ref, *refs):
     lines, out_ref, total_ref, cols_ref = refs[:-3], refs[-3], refs[-2], refs[-1]
     chips, height, wide = mine_ref.shape
-    share = height // 8
+    share = height // len(refs[:-3])
     d_all = lines[0].shape[0]
     d_txt = 2 * HALF
     d_img = d_all - d_txt
@@ -115,24 +113,23 @@
 
 
 def feature_grads_kernel(
-    core_ref, mine_ref, other_ref, img_proj_ref, txt_proj_ref, img_ref, txt_ref, img_rows, txt_rows
+    member_ref, own_ref, high_ref, low_ref, core_ref, img_proj_ref, txt_proj_ref,
+    img_ref, txt_ref, img_rows, txt_rows,
 ):
-    chips, height, wide = mine_ref.shape
-    share = height // 8
-    for chip in range(chips):
-        for ref, core in ((mine_ref, core_ref[0]), (other_ref, 1 - core_ref[0])):
-            row = pl.multiple_of((2 * chip + core) * share, share)
-            for part in range(2):
-                lanes = slice(part * wide, (part + 1) * wide)
-                first = (4 + 2 * part) * share
-                img_rows[pl.ds(row, share), lanes] = ref[chip, first : first + share]
-                txt_rows[pl.ds(row, share), lanes] = ref[chip, first + share : first + 2 * share]
+    share = own_ref.shape[0] // 2
+    places = iter((0, 4, 2, 6, 1, 5, 3, 7))
+    for ref in (own_ref, high_ref, low_ref, core_ref):
+        for piece in range(ref.shape[0] // (2 * share)):
+            row = pl.multiple_of((member_ref[0] ^ next(places)) * share, share)
+            first = piece * 2 * share
+            img_rows[pl.ds(row, share)] = ref[first : first + share]
+            txt_rows[pl.ds(row, share)] = ref[first + share : first + 2 * share]
     txt_ref[...] = lax.dot_general(
         txt_rows[...], txt_proj_ref[...], ACROSS, preferred_element_type=F32
-    ).astype(BF16)
+    ).astype(txt_ref.dtype)
     img_ref[...] = lax.dot_general(
         img_proj_ref[...], img_rows[...], ACROSS, preferred_element_type=F32
-    ).astype(BF16)
+    ).astype(img_ref.dtype)
 
 
 def on_device(image_feats, text_feats, image_proj, text_proj, labels, logit_scale, logit_bias):
@@ -147,20 +144,18 @@
     d_img, d_txt = image_feats.shape[1], text_feats.shape[1]
     embed = image_proj.shape[1]
     chips = lax.axis_size(CHIPS)
-    core_index = lax.axis_index("core").astype(jnp.int32).reshape(1)
-    halves = jax.ShapeDtypeStruct((chips, 2 * share, embed), BF16)
-    mine, other, pack = call(
+    parts, pack = call(
         project_kernel,
         "project",
-        (halves, halves, jax.ShapeDtypeStruct((d_txt + d_img, HALF), BF16)),
-        (core_index, image_feats.T, text_feats, image_proj, text_proj),
+        (
+            jax.ShapeDtypeStruct((groups, 2 * share, embed), BF16),
+            jax.ShapeDtypeStruct((d_txt + d_img, HALF), BF16),
+        ),
+        (image_feats.T, text_feats, image_proj, text_proj),
         2 * rows * (d_img + d_txt) * embed,
-        scratch=(pltpu.VMEM((groups, 2 * share, embed), BF16),),
-        scalars=1,
-    )
-    parts = (mine.astype(F32) + core_swapped(other).astype(F32)).astype(BF16)
-    lines = [along_y(pack, 1), pack, along_y(pack, -1), along_y(pack, -2)]
-    parts = lax.all_to_all(parts, CHIPS, 0, 0, tiled=True)
+    )
+    below, above = along_y(pack, 1), along_y(pack, -1)
+    parts = lax.all_to_all(parts, X, 0, 0, tiled=True)
     summed = jnp.sum(parts.astype(F32), axis=0)
     length = jnp.sqrt(jnp.sum(summed * summed, axis=1, keepdims=True) + NORM_EPS)
     unit = summed / length
@@ -170,7 +165,9 @@
     img_all = lax.all_to_all(img_all, X, 0, 0, tiled=True).reshape(rows, embed)
     near = shifted(txt_own, 1)
     pair = jnp.concatenate([txt_own, near])
+    pair, below, above = lax.optimization_barrier((pair, below, above))
     far = shifted(pair, 2)
+    lines = [below, pack, above, along_y(above, -1)]
     cols = jnp.concatenate([pair, far])
     offsets = jnp.arange(STEPS, dtype=jnp.int32)
     col_ids = (
@@ -189,7 +186,7 @@
     img_terms = jnp.dot(weights, cols, preferred_element_type=F32).astype(BF16)
     back = shifted(txt_terms[2 * share :].astype(BF16), -2)
     img_terms = lax.all_to_all(img_terms.reshape(groups, share, embed), X, 0, 0, tiled=True)
-    img_terms, lines = lax.optimization_barrier((img_terms, lines))
+    img_terms, lines[3] = lax.optimization_barrier((img_terms, lines[3]))
     two = txt_terms[: 2 * share] + back.astype(F32)
     last = shifted(two[share:].astype(BF16), -1)
     grad_txt = two[:share] + last.astype(F32)
@@ -201,22 +198,26 @@
     by_cols = by_cols.transpose(3, 1, 0, 2, 4).reshape(quad, share, 2 * embed // quad)
     by_cols = jnp.concatenate([by_cols] * (lax.axis_size(Y) // quad))
     by_cols = lax.all_to_all(by_cols, Y, 0, 0, tiled=True)
+    pieces = [grad_summed, swapped(grad_summed, "xh")]
+    by_cols, pieces = lax.optimization_barrier((by_cols, pieces))
     y_index = lax.axis_index(Y)
     window = [
         lax.dynamic_index_in_dim(by_cols, lax.rem(y_index + (step + lax.axis_size(Y)), lax.axis_size(Y)), 0, False)
         for step in (-1, 0, 1, 2)
     ]
-    wide = 2 * embed // quad
-    mine = jnp.concatenate(window + [grad_summed[:, :wide], grad_summed[:, wide:]])
+    mine = jnp.concatenate(window)
     mine = jnp.broadcast_to(mine[None], (chips,) + mine.shape)
     mine = lax.all_to_all(mine, CHIPS, 0, 0, tiled=True)
     other = core_swapped(mine)
+    pieces.append(swapped(jnp.concatenate(pieces), "xl"))
+    pieces.append(core_swapped(jnp.concatenate(pieces)))
+    wide = 2 * embed // quad
     height = 4 * embed // blocks
     wgrad = call(
         wgrad_kernel,
         "project_grads",
         jax.ShapeDtypeStruct((peers, height, HALF), BF16),
-        (core_index, mine, other, *lines),
+        (lax.axis_index("core").astype(jnp.int32).reshape(1), mine, other, *lines),
         2 * quad * rows * (embed // quad) * (d_img + d_txt),
         scratch=(pltpu.VMEM((peers, height, HALF), F32), pltpu.VMEM((quad, rows, wide), BF16)),
         scalars=1,
@@ -226,7 +227,7 @@
         feature_grads_kernel,
         "feature_grads",
         (jax.ShapeDtypeStruct((d_img, rows), BF16), jax.ShapeDtypeStruct((rows, d_txt), BF16)),
-        (core_index, mine, other, image_proj, text_proj),
+        (member.astype(jnp.int32).reshape(1), *pieces, image_proj, text_proj),
         2 * rows * (d_img + d_txt) * embed,
         scratch=(pltpu.VMEM((rows, embed), BF16), pltpu.VMEM((rows, embed), BF16)),
         scalars=1,
@@ -241,6 +242,7 @@
         (wgrad,),
         peers * height * HALF,
         scratch=(pltpu.VMEM((height, HALF), F32),),
+        vmem=VMEM // 4,
     )
     return (image_grad.T, text_grad, img_wgrad.T, txt_wgrad.T)
 

time: 141 us -> 132 us (0.936)
  the two profiles are of different devices: /device:TPU:16 before, /device:TPU:8 now
where the time goes in v6:
time: 132 us; the launch traced here: 131 us
  starting transfers between devices  70.2 us (53%)
  waiting for transfers between devices  32.2 us (24%)
  blocking collectives  10.2 us (8%)
  Pallas kernels  9.8 us (7%)
  local copies, waits for them, and re-layouts  3.31 us (3%)
  between operations  2.42 us (2%)
  other arithmetic  1.75 us (1%)
  matrix products  1.53 us (1%)
    ppermute x4, starting transfers between devices, shifted(): return lax.ppermute(value, DP, pairs)  17 us
    ppermute x3, starting transfers between devices, along_y(): return lax.ppermute(value, Y, pairs)  12.9 us
    all_to_all x1, waiting for transfers between devices, on_device(): wgrad = lax.all_to_all(wgrad, ('yh', 'z'), 0, 0, tiled=True)  11.1 us
    ppermute x4, starting transfers between devices, swapped(): return lax.ppermute(value, axis, [(0, 1), (1, 0)])  10.5 us
    all_to_all x1, blocking collectives, on_device(): mine = lax.all_to_all(mine, CHIPS, 0, 0, tiled=True)  10.2 us
    pallas_call x4, Pallas kernels, call(): pl.pallas_call(kernel, out_shape=out_shape, in_specs=[pl.BlockSpec(memory...  9.8 us
    ppermute x4, waiting for transfers between devices, shifted(): return lax.ppermute(value, DP, pairs)  8.73 us
    all_to_all x1, starting transfers between devices, on_device(): wgrad = lax.all_to_all(wgrad, ('yh', 'z'), 0, 0, tiled=True)  8.52 us
  transfers between devices with their start and end apart: 16, of which 9 were waited for; matrix products, arithmetic and copies ran while one was open for 2% of the time, Pallas kernels for 5%

profile of v6, /device:TPU:8, one launch (start us, length us, event | category | flops | bytes accessed | tf_op | source)
XLA Modules:
  0.0 131.5 jit_solution(16352291108258134118)
XLA Ops:
  0.6 3.1 %project.1 = (bf16[8,64,768]{2,1,0:T(8,128)(2,1)}, bf16[912,256]{1,0:T(8,128)(2,1)}) custom-call(bf16[400,256]{1,0:T(8,128)(2,1)} %bitcast.31, bf16[256,512]{1,0:T(8,128)(2,1)} %txt_ref.1, bf16[400,768]{1,0:T(8,128)(2,1)} %img_proj_ref.3, bf16[512,768]{1,0:T(8,128)(2,1)} %txt_proj_ref.3), custom_call_target="tpu_custom_call" | custom-call | flops 358612992 | bytes 4000000 | tf_op jit(solution)/shard_map/project/pallas_call | solution.py:43
  3.7 4.4 %all-to-all-start = ((bf16[8,64,768]{2,1,0:T(8,128)(2,1)}), bf16[8,64,768]{2,1,0:T(8,128)(2,1)S(1)}, u32[]{:S(2)}, u32[]{:S(2)}) async-start(bf16[8,64,768]{2,1,0:T(8,128)(2,1)} %get-tuple-element.18), calls=%async_computation | async-start | bytes 1572864 | tf_op jit(solution)/shard_map/all_to_all | solution.py:158
  8.2 3.5 %collective-permute-start.1 = (bf16[912,256]{1,0:T(8,128)(2,1)S(1)}, bf16[912,256]{1,0:T(8,128)(2,1)S(1)}, u32[]{:S(2)}, u32[]{:S(2)}) collective-permute-start(bf16[912,256]{1,0:T(8,128)(2,1)S(1)} %copy-done.4), channel_id=1, source_target_pairs={{0,64},{64,128},{128,192},{192,256},{256,320},{320,384},{384,448},... | collective-permute-start | bytes 1400840 | tf_op jit(solution)/shard_map/ppermute | solution.py:30
  11.7 5.4 %collective-permute-start.2 = (bf16[912,256]{1,0:T(8,128)(2,1)S(1)}, bf16[912,256]{1,0:T(8,128)(2,1)S(1)}, u32[]{:S(2)}, u32[]{:S(2)}) collective-permute-start(bf16[912,256]{1,0:T(8,128)(2,1)S(1)} %copy-done.4), channel_id=1, source_target_pairs={{0,448},{64,0},{128,64},{192,128},{256,192},{320,256},{384,320},{4... | collective-permute-start | bytes 1400840 | tf_op jit(solution)/shard_map/ppermute | solution.py:30
  17.1 4.2 %all-to-all-done = bf16[8,64,768]{2,1,0:T(8,128)(2,1)S(1)} async-done(((bf16[8,64,768]{2,1,0:T(8,128)(2,1)}), bf16[8,64,768]{2,1,0:T(8,128)(2,1)S(1)}, u32[]{:S(2)}, u32[]{:S(2)}) %all-to-all-start) | async-done | bytes 786464 | tf_op jit(solution)/shard_map/all_to_all | solution.py:158
  21.7 4.3 %collective-permute-start = (bf16[32,768]{1,0:T(8,128)(2,1)S(1)}, bf16[32,768]{1,0:T(8,128)(2,1)S(1)}, u32[]{:S(2)}, u32[]{:S(2)}) collective-permute-start(bf16[32,768]{1,0:T(8,128)(2,1)S(1)} %get-tuple-element.38), channel_id=1, source_target_pairs={{0,8},{8,16},{16,24},{24,32},{32,40},{40,48},{48,56},{56,64},{64,7... | collective-permute-start | bytes 147464 | tf_op jit(solution)/shard_map/ppermute | solution.py:24
  27.4 0.8 broadcast_in_dim.14
  28.2 3.6 %all-to-all-start.1 = ((bf16[8,32,768]{2,1,0:T(8,128)(2,1)}), bf16[8,32,768]{2,1,0:T(8,128)(2,1)S(1)}, u32[]{:S(2)}, u32[]{:S(2)}) async-start(bf16[8,32,768]{2,1,0:T(8,128)(2,1)} %broadcast_in_dim.14), calls=%async_computation.1 | async-start | bytes 786432 | tf_op jit(solution)/shard_map/all_to_all | solution.py:165
  31.8 2.8 %collective-permute-done = bf16[32,768]{1,0:T(8,128)(2,1)S(1)} collective-permute-done((bf16[32,768]{1,0:T(8,128)(2,1)S(1)}, bf16[32,768]{1,0:T(8,128)(2,1)S(1)}, u32[]{:S(2)}, u32[]{:S(2)}) %collective-permute-start) | collective-permute-done | bytes 49184 | tf_op jit(solution)/shard_map/ppermute | solution.py:24
  34.6 3.4 %collective-permute-start.3 = (bf16[64,768]{1,0:T(8,128)(2,1)S(1)}, bf16[64,768]{1,0:T(8,128)(2,1)S(1)}, u32[]{:S(2)}, u32[]{:S(2)}) collective-permute-start(bf16[64,768]{1,0:T(8,128)(2,1)S(1)} %pad_maximum_fusion.4), channel_id=1, source_target_pairs={{0,16},{8,24},{16,32},{24,40},{32,48},{40,56},{48,64},{56,72},{64,... | collective-permute-start | bytes 294920 | tf_op jit(solution)/shard_map/ppermute | solution.py:24
  38.0 3.9 %collective-permute-start.4 = (bf16[912,256]{1,0:T(8,128)(2,1)S(1)}, bf16[912,256]{1,0:T(8,128)(2,1)S(1)}, u32[]{:S(2)}, u32[]{:S(2)}) collective-permute-start(bf16[912,256]{1,0:T(8,128)(2,1)S(1)} %collective-permute-done.2.refs_2_), channel_id=1, source_target_pairs={{0,448},{64,0},{128,64},{192,128},{256,192},{320,256},{384,320},{4... | collective-permute-start | bytes 1400840 | tf_op jit(solution)/shard_map/ppermute | solution.py:30
  41.9 4.5 %collective-permute-done.3 = bf16[64,768]{1,0:T(8,128)(2,1)S(1)} collective-permute-done((bf16[64,768]{1,0:T(8,128)(2,1)S(1)}, bf16[64,768]{1,0:T(8,128)(2,1)S(1)}, u32[]{:S(2)}, u32[]{:S(2)}) %collective-permute-start.3) | collective-permute-done | bytes 98336 | tf_op jit(solution)/shard_map/ppermute | solution.py:24
  47.1 4.1 %collective-permute-start.5 = (bf16[64,768]{1,0:T(8,128)(2,1)S(1)}, bf16[64,768]{1,0:T(8,128)(2,1)S(1)}, u32[]{:S(2)}, u32[]{:S(2)}) collective-permute-start(bf16[64,768]{1,0:T(8,128)(2,1)S(1)} %slice.36), channel_id=1, source_target_pairs={{0,496},{8,504},{16,0},{24,8},{32,16},{40,24},{48,32},{56,40},{64,... | collective-permute-start | bytes 294920 | tf_op jit(solution)/shard_map/ppermute | solution.py:24
  51.2 1.0 convolution_convert_fusion
  52.2 5.7 %all-to-all-start.2 = ((bf16[8,32,768]{2,1,0:T(8,128)(2,1)}), bf16[8,32,768]{2,1,0:T(8,128)(2,1)S(1)}, u32[]{:S(2)}, u32[]{:S(2)}) async-start(bf16[8,32,768]{2,1,0:T(8,128)(2,1)} %bitcast.5), calls=%async_computation.2 | async-start | bytes 786432 | tf_op jit(solution)/shard_map/all_to_all | solution.py:188
  58.0 5.2 %collective-permute-start.6 = (bf16[32,768]{1,0:T(8,128)(2,1)S(1)}, bf16[32,768]{1,0:T(8,128)(2,1)S(1)}, u32[]{:S(2)}, u32[]{:S(2)}) collective-permute-start(bf16[32,768]{1,0:T(8,128)(2,1)S(1)} %slice.37), channel_id=1, source_target_pairs={{0,504},{8,0},{16,8},{24,16},{32,24},{40,32},{48,40},{56,48},{64,5... | collective-permute-start | bytes 147464 | tf_op jit(solution)/shard_map/ppermute | solution.py:24
  63.5 1.4 %collective-permute-done.6 = bf16[32,768]{1,0:T(8,128)(2,1)S(1)} collective-permute-done((bf16[32,768]{1,0:T(8,128)(2,1)S(1)}, bf16[32,768]{1,0:T(8,128)(2,1)S(1)}, u32[]{:S(2)}, u32[]{:S(2)}) %collective-permute-start.6) | collective-permute-done | bytes 49184 | tf_op jit(solution)/shard_map/ppermute | solution.py:24
  65.0 1.9 %all-to-all-done.2 = bf16[8,32,768]{2,1,0:T(8,128)(2,1)S(1)} async-done(((bf16[8,32,768]{2,1,0:T(8,128)(2,1)}), bf16[8,32,768]{2,1,0:T(8,128)(2,1)S(1)}, u32[]{:S(2)}, u32[]{:S(2)}) %all-to-all-start.2) | async-done | bytes 393248 | tf_op jit(solution)/shard_map/all_to_all | solution.py:188
  68.7 7.7 %all-to-all-start.3 = ((bf16[8,32,384]{2,1,0:T(8,128)(2,1)}), bf16[8,32,384]{2,1,0:T(8,128)(2,1)S(1)}, u32[]{:S(2)}, u32[]{:S(2)}) async-start(bf16[8,32,384]{2,1,0:T(8,128)(2,1)} %pad_maximum_fusion.2), calls=%async_computation.3 | async-start | bytes 393216 | tf_op jit(solution)/shard_map/all_to_all | solution.py:200
  76.4 4.2 %collective-permute-start.7 = (bf16[64,768]{1,0:T(8,128)(2,1)S(1)}, bf16[64,768]{1,0:T(8,128)(2,1)S(1)}, u32[]{:S(2)}, u32[]{:S(2)}) collective-permute-start(bf16[64,768]{1,0:T(8,128)(2,1)S(1)} %get-tuple-element.23.own_ref), channel_id=1, source_target_pairs={{0,4},{4,0},{1,5},{5,1},{2,6},{6,2},{3,7},{7,3},{8,12},{12,8},{9,1... | collective-permute-start | bytes 294920 | tf_op jit(solution)/shard_map/ppermute | solution.py:34
  80.6 3.8 %collective-permute-done.7.high_ref = bf16[64,768]{1,0:T(8,128)(2,1)S(1)} collective-permute-done((bf16[64,768]{1,0:T(8,128)(2,1)S(1)}, bf16[64,768]{1,0:T(8,128)(2,1)S(1)}, u32[]{:S(2)}, u32[]{:S(2)}) %collective-permute-start.7) | collective-permute-done | bytes 98336 | tf_op jit(solution)/shard_map/ppermute | solution.py:34
  84.4 0.8 all-to-all-done.3
  85.3 10.2 %all_to_all.30.mine_ref = bf16[4,128,384]{2,1,0:T(8,128)(2,1)S(1)} all-to-all(bf16[4,128,384]{2,1,0:T(8,128)(2,1)S(1)} %broadcast_in_dim.15), channel_id=1, replica_groups=mesh['yh'=2,'yl'=4,'z'=8,'xh'=2,'xl'=2,'core'=2] {'xh','xl'}, dimensions={0} | all-to-all | bytes 786432 | tf_op jit(solution)/shard_map/all_to_all | solution.py:210
  95.5 1.9 %collective-permute-start.10 = (bf16[4,128,384]{2,1,0:T(8,128)(2,1)S(1)}, bf16[4,128,384]{2,1,0:T(8,128)(2,1)S(1)}, u32[]{:S(2)}, u32[]{:S(2)}) collective-permute-start(bf16[4,128,384]{2,1,0:T(8,128)(2,1)S(1)} %all_to_all.30.mine_ref), channel_id=1, source_target_pairs={{0,1},{1,0},{2,3},{3,2},{4,5},{5,4},{6,7},{7,6},{8,9},{9,8},{10,11... | collective-permute-start | bytes 1179656 | tf_op jit(solution)/shard_map/ppermute | solution.py:34
  97.4 2.5 %collective-permute-start.8 = (bf16[128,768]{1,0:T(8,128)(2,1)S(1)}, bf16[128,768]{1,0:T(8,128)(2,1)S(1)}, u32[]{:S(2)}, u32[]{:S(2)}) collective-permute-start(bf16[128,768]{1,0:T(8,128)(2,1)S(1)} %pad_maximum_fusion.3), channel_id=1, source_target_pairs={{0,2},{2,0},{1,3},{3,1},{4,6},{6,4},{5,7},{7,5},{8,10},{10,8},{9,1... | collective-permute-start | bytes 589832 | tf_op jit(solution)/shard_map/ppermute | solution.py:34
  100.7 3.2 %project_grads.1 = bf16[16,48,256]{2,1,0:T(8,128)(2,1)} custom-call(s32[1]{0:T(128)} %bitcast.8.core_ref, bf16[4,128,384]{2,1,0:T(8,128)(2,1)} %copy-done.1, bf16[4,128,384]{2,1,0:T(8,128)(2,1)} %copy-done.8, bf16[912,256]{1,0:T(8,128)(2,1)} %copy-done.5, bf16[912,256]{1,0:T(8,128)(2,1)} %get-tuple-element.19.refs_1_, bf16[912,256]{1,0:T(8,128)(2,1)} %copy-done.6, ...), custom_call_target="tpu_custom_call" | custom-call | flops 358612992 | bytes 4000000 | tf_op jit(solution)/shard_map/project_grads/pallas_call | solution.py:43
  103.9 8.5 %all-to-all-start.5 = ((bf16[16,48,256]{2,1,0:T(8,128)(2,1)}), bf16[16,48,256]{2,1,0:T(8,128)(2,1)S(1)}, u32[]{:S(2)}, u32[]{:S(2)}) async-start(bf16[16,48,256]{2,1,0:T(8,128)(2,1)} %project_grads.1), calls=%async_computation.5 | async-start | bytes 786432 | tf_op jit(solution)/shard_map/all_to_all | solution.py:225
  112.5 1.9 %collective-permute-start.9 = (bf16[256,768]{1,0:T(8,128)(2,1)S(1)}, bf16[256,768]{1,0:T(8,128)(2,1)S(1)}, u32[]{:S(2)}, u32[]{:S(2)}) collective-permute-start(bf16[256,768]{1,0:T(8,128)(2,1)S(1)} %pad_maximum_fusion), channel_id=1, source_target_pairs={{0,1},{1,0},{2,3},{3,2},{4,5},{5,4},{6,7},{7,6},{8,9},{9,8},{10,11... | collective-permute-start | bytes 1179656 | tf_op jit(solution)/shard_map/ppermute | solution.py:34
  114.4 1.7 %collective-permute-done.9.core_ref = bf16[256,768]{1,0:T(8,128)(2,1)S(1)} collective-permute-done((bf16[256,768]{1,0:T(8,128)(2,1)S(1)}, bf16[256,768]{1,0:T(8,128)(2,1)S(1)}, u32[]{:S(2)}, u32[]{:S(2)}) %collective-permute-start.9) | collective-permute-done | bytes 393248 | tf_op jit(solution)/shard_map/ppermute | solution.py:34
  116.1 0.7 copy-done.9
  116.8 2.8 %feature_grads.1 = (bf16[400,256]{1,0:T(8,128)(2,1)}, bf16[256,512]{1,0:T(8,128)(2,1)}) custom-call(s32[1]{0:T(128)} %bitcast.member_ref, bf16[64,768]{1,0:T(8,128)(2,1)} %copy-done, bf16[64,768]{1,0:T(8,128)(2,1)} %copy-done.2, bf16[128,768]{1,0:T(8,128)(2,1)} %copy-done.3, bf16[256,768]{1,0:T(8,128)(2,1)} %copy-done.9, bf16[400,768]{1,0:T(8,128)(2,1)} %img_proj_ref.3, ...), custom_call_target="tpu_custom_call" | custom-call | flops 358612992 | bytes 4000000 | tf_op jit(solution)/shard_map/feature_grads/pallas_call | solution.py:43
  119.7 11.1 %all-to-all-done.5.blocks_ref = bf16[16,48,256]{2,1,0:T(8,128)(2,1)S(1)} async-done(((bf16[16,48,256]{2,1,0:T(8,128)(2,1)}), bf16[16,48,256]{2,1,0:T(8,128)(2,1)S(1)}, u32[]{:S(2)}, u32[]{:S(2)}) %all-to-all-start.5) | async-done | bytes 393248 | tf_op jit(solution)/shard_map/all_to_all | solution.py:225
  (62 shorter events, 4.8 us)
Async XLA Ops:
  3.7 4.4 %copy-start.4 = (bf16[912,256]{1,0:T(8,128)(2,1)S(1)}, bf16[912,256]{1,0:T(8,128)(2,1)}, u32[]{:S(2)}) copy-start(bf16[912,256]{1,0:T(8,128)(2,1)} %get-tuple-element.19.refs_1_) | copy-start | bytes 1400836
  3.7 17.6 %all-to-all-start = ((bf16[8,64,768]{2,1,0:T(8,128)(2,1)}), bf16[8,64,768]{2,1,0:T(8,128)(2,1)S(1)}, u32[]{:S(2)}, u32[]{:S(2)}) async-start(bf16[8,64,768]{2,1,0:T(8,128)(2,1)} %get-tuple-element.18), calls=%async_computation | async-start | bytes 1572864 | tf_op jit(solution)/shard_map/all_to_all | solution.py:158
  8.2 26.4 %collective-permute-start.1 = (bf16[912,256]{1,0:T(8,128)(2,1)S(1)}, bf16[912,256]{1,0:T(8,128)(2,1)S(1)}, u32[]{:S(2)}, u32[]{:S(2)}) collective-permute-start(bf16[912,256]{1,0:T(8,128)(2,1)S(1)} %copy-done.4), channel_id=1, source_target_pairs={{0,64},{64,128},{128,192},{192,256},{256,320},{320,384},{384,448},... | collective-permute-start | bytes 1400840 | tf_op jit(solution)/shard_map/ppermute | solution.py:30
  11.7 22.9 %collective-permute-start.2 = (bf16[912,256]{1,0:T(8,128)(2,1)S(1)}, bf16[912,256]{1,0:T(8,128)(2,1)S(1)}, u32[]{:S(2)}, u32[]{:S(2)}) collective-permute-start(bf16[912,256]{1,0:T(8,128)(2,1)S(1)} %copy-done.4), channel_id=1, source_target_pairs={{0,448},{64,0},{128,64},{192,128},{256,192},{320,256},{384,320},{4... | collective-permute-start | bytes 1400840 | tf_op jit(solution)/shard_map/ppermute | solution.py:30
  21.7 12.9 %collective-permute-start = (bf16[32,768]{1,0:T(8,128)(2,1)S(1)}, bf16[32,768]{1,0:T(8,128)(2,1)S(1)}, u32[]{:S(2)}, u32[]{:S(2)}) collective-permute-start(bf16[32,768]{1,0:T(8,128)(2,1)S(1)} %get-tuple-element.38), channel_id=1, source_target_pairs={{0,8},{8,16},{16,24},{24,32},{32,40},{40,48},{48,56},{56,64},{64,7... | collective-permute-start | bytes 147464 | tf_op jit(solution)/shard_map/ppermute | solution.py:24
  28.2 18.3 %copy-start.10 = (s32[256]{0:T(256)S(1)}, s32[256]{0:T(256)}, u32[]{:S(2)}) copy-start(s32[256]{0:T(256)} %param.11) | copy-start | bytes 3076
  28.2 18.3 %all-to-all-start.1 = ((bf16[8,32,768]{2,1,0:T(8,128)(2,1)}), bf16[8,32,768]{2,1,0:T(8,128)(2,1)S(1)}, u32[]{:S(2)}, u32[]{:S(2)}) async-start(bf16[8,32,768]{2,1,0:T(8,128)(2,1)} %broadcast_in_dim.14), calls=%async_computation.1 | async-start | bytes 786432 | tf_op jit(solution)/shard_map/all_to_all | solution.py:165
  34.6 12.2 %copy-start.5 = (bf16[912,256]{1,0:T(8,128)(2,1)}, bf16[912,256]{1,0:T(8,128)(2,1)S(1)}, u32[]{:S(2)}) copy-start(bf16[912,256]{1,0:T(8,128)(2,1)S(1)} %collective-permute-done.1.refs_0_) | copy-start | bytes 1400836
  34.6 12.2 %copy-start.6 = (bf16[912,256]{1,0:T(8,128)(2,1)}, bf16[912,256]{1,0:T(8,128)(2,1)S(1)}, u32[]{:S(2)}) copy-start(bf16[912,256]{1,0:T(8,128)(2,1)S(1)} %collective-permute-done.2.refs_2_) | copy-start | bytes 1400836
  34.6 11.8 %collective-permute-start.3 = (bf16[64,768]{1,0:T(8,128)(2,1)S(1)}, bf16[64,768]{1,0:T(8,128)(2,1)S(1)}, u32[]{:S(2)}, u32[]{:S(2)}) collective-permute-start(bf16[64,768]{1,0:T(8,128)(2,1)S(1)} %pad_maximum_fusion.4), channel_id=1, source_target_pairs={{0,16},{8,24},{16,32},{24,40},{32,48},{40,56},{48,64},{56,72},{64,... | collective-permute-start | bytes 294920 | tf_op jit(solution)/shard_map/ppermute | solution.py:24
  38.0 27.0 %collective-permute-start.4 = (bf16[912,256]{1,0:T(8,128)(2,1)S(1)}, bf16[912,256]{1,0:T(8,128)(2,1)S(1)}, u32[]{:S(2)}, u32[]{:S(2)}) collective-permute-start(bf16[912,256]{1,0:T(8,128)(2,1)S(1)} %collective-permute-done.2.refs_2_), channel_id=1, source_target_pairs={{0,448},{64,0},{128,64},{192,128},{256,192},{320,256},{384,320},{4... | collective-permute-start | bytes 1400840 | tf_op jit(solution)/shard_map/ppermute | solution.py:30
  47.1 10.8 %collective-permute-start.5 = (bf16[64,768]{1,0:T(8,128)(2,1)S(1)}, bf16[64,768]{1,0:T(8,128)(2,1)S(1)}, u32[]{:S(2)}, u32[]{:S(2)}) collective-permute-start(bf16[64,768]{1,0:T(8,128)(2,1)S(1)} %slice.36), channel_id=1, source_target_pairs={{0,496},{8,504},{16,0},{24,8},{32,16},{40,24},{48,32},{56,40},{64,... | collective-permute-start | bytes 294920 | tf_op jit(solution)/shard_map/ppermute | solution.py:24
  52.2 14.7 %all-to-all-start.2 = ((bf16[8,32,768]{2,1,0:T(8,128)(2,1)}), bf16[8,32,768]{2,1,0:T(8,128)(2,1)S(1)}, u32[]{:S(2)}, u32[]{:S(2)}) async-start(bf16[8,32,768]{2,1,0:T(8,128)(2,1)} %bitcast.5), calls=%async_computation.2 | async-start | bytes 786432 | tf_op jit(solution)/shard_map/all_to_all | solution.py:188
  58.0 7.0 %collective-permute-start.6 = (bf16[32,768]{1,0:T(8,128)(2,1)S(1)}, bf16[32,768]{1,0:T(8,128)(2,1)S(1)}, u32[]{:S(2)}, u32[]{:S(2)}) collective-permute-start(bf16[32,768]{1,0:T(8,128)(2,1)S(1)} %slice.37), channel_id=1, source_target_pairs={{0,504},{8,0},{16,8},{24,16},{32,24},{40,32},{48,40},{56,48},{64,5... | collective-permute-start | bytes 147464 | tf_op jit(solution)/shard_map/ppermute | solution.py:24
  65.0 2.3 %copy-start.7 = (bf16[912,256]{1,0:T(8,128)(2,1)}, bf16[912,256]{1,0:T(8,128)(2,1)S(1)}, u32[]{:S(2)}) copy-start(bf16[912,256]{1,0:T(8,128)(2,1)S(1)} %collective-permute-done.4.refs_3_) | copy-start | bytes 1400836
  67.2 45.2 %copy-start = (bf16[64,768]{1,0:T(8,128)(2,1)}, bf16[64,768]{1,0:T(8,128)(2,1)S(1)}, u32[]{:S(2)}) copy-start(bf16[64,768]{1,0:T(8,128)(2,1)S(1)} %get-tuple-element.23.own_ref) | copy-start | bytes 294916
  68.7 16.5 %all-to-all-start.3 = ((bf16[8,32,384]{2,1,0:T(8,128)(2,1)}), bf16[8,32,384]{2,1,0:T(8,128)(2,1)S(1)}, u32[]{:S(2)}, u32[]{:S(2)}) async-start(bf16[8,32,384]{2,1,0:T(8,128)(2,1)} %pad_maximum_fusion.2), calls=%async_computation.3 | async-start | bytes 393216 | tf_op jit(solution)/shard_map/all_to_all | solution.py:200
  76.4 8.0 %collective-permute-start.7 = (bf16[64,768]{1,0:T(8,128)(2,1)S(1)}, bf16[64,768]{1,0:T(8,128)(2,1)S(1)}, u32[]{:S(2)}, u32[]{:S(2)}) collective-permute-start(bf16[64,768]{1,0:T(8,128)(2,1)S(1)} %get-tuple-element.23.own_ref), channel_id=1, source_target_pairs={{0,4},{4,0},{1,5},{5,1},{2,6},{6,2},{3,7},{7,3},{8,12},{12,8},{9,1... | collective-permute-start | bytes 294920 | tf_op jit(solution)/shard_map/ppermute | solution.py:34
  84.4 28.0 %copy-start.2 = (bf16[64,768]{1,0:T(8,128)(2,1)}, bf16[64,768]{1,0:T(8,128)(2,1)S(1)}, u32[]{:S(2)}) copy-start(bf16[64,768]{1,0:T(8,128)(2,1)S(1)} %collective-permute-done.7.high_ref) | copy-start | bytes 294916
  95.5 4.4 %copy-start.1 = (bf16[4,128,384]{2,1,0:T(8,128)(2,1)}, bf16[4,128,384]{2,1,0:T(8,128)(2,1)S(1)}, u32[]{:S(2)}) copy-start(bf16[4,128,384]{2,1,0:T(8,128)(2,1)S(1)} %all_to_all.30.mine_ref) | copy-start | bytes 1179652
  95.5 4.4 %collective-permute-start.10 = (bf16[4,128,384]{2,1,0:T(8,128)(2,1)S(1)}, bf16[4,128,384]{2,1,0:T(8,128)(2,1)S(1)}, u32[]{:S(2)}, u32[]{:S(2)}) collective-permute-start(bf16[4,128,384]{2,1,0:T(8,128)(2,1)S(1)} %all_to_all.30.mine_ref), channel_id=1, source_target_pairs={{0,1},{1,0},{2,3},{3,2},{4,5},{5,4},{6,7},{7,6},{8,9},{9,8},{10,11... | collective-permute-start | bytes 1179656 | tf_op jit(solution)/shard_map/ppermute | solution.py:34
  97.4 15.0 %collective-permute-start.8 = (bf16[128,768]{1,0:T(8,128)(2,1)S(1)}, bf16[128,768]{1,0:T(8,128)(2,1)S(1)}, u32[]{:S(2)}, u32[]{:S(2)}) collective-permute-start(bf16[128,768]{1,0:T(8,128)(2,1)S(1)} %pad_maximum_fusion.3), channel_id=1, source_target_pairs={{0,2},{2,0},{1,3},{3,1},{4,6},{6,4},{5,7},{7,5},{8,10},{10,8},{9,1... | collective-permute-start | bytes 589832 | tf_op jit(solution)/shard_map/ppermute | solution.py:34
  99.9 0.8 copy-start.8
  103.9 26.9 %all-to-all-start.5 = ((bf16[16,48,256]{2,1,0:T(8,128)(2,1)}), bf16[16,48,256]{2,1,0:T(8,128)(2,1)S(1)}, u32[]{:S(2)}, u32[]{:S(2)}) async-start(bf16[16,48,256]{2,1,0:T(8,128)(2,1)} %project_grads.1), calls=%async_computation.5 | async-start | bytes 786432 | tf_op jit(solution)/shard_map/all_to_all | solution.py:225
  112.4 3.7 %copy-start.3 = (bf16[128,768]{1,0:T(8,128)(2,1)}, bf16[128,768]{1,0:T(8,128)(2,1)S(1)}, u32[]{:S(2)}) copy-start(bf16[128,768]{1,0:T(8,128)(2,1)S(1)} %collective-permute-done.8.low_ref) | copy-start | bytes 589828
  112.5 3.6 %collective-permute-start.9 = (bf16[256,768]{1,0:T(8,128)(2,1)S(1)}, bf16[256,768]{1,0:T(8,128)(2,1)S(1)}, u32[]{:S(2)}, u32[]{:S(2)}) collective-permute-start(bf16[256,768]{1,0:T(8,128)(2,1)S(1)} %pad_maximum_fusion), channel_id=1, source_target_pairs={{0,1},{1,0},{2,3},{3,2},{4,5},{5,4},{6,7},{7,6},{8,9},{9,8},{10,11... | collective-permute-start | bytes 1179656 | tf_op jit(solution)/shard_map/ppermute | solution.py:34
  116.1 0.7 copy-start.9

commit v7 on v6

--- a/solution.py
+++ b/solution.py
@@ -9,8 +9,8 @@
 NORM_EPS = 1e-06
 CHIPS = ("xh", "xl")
 X = CHIPS + ("core",)
-Y = ("yh", "yl")
-DP = ("yh", "yl", "z")
+Y = ("yq", "yp")
+DP = Y + ("z",)
 ACROSS = (((1,), (1,)), ((), ()))
 DOWN = (((0,), (0,)), ((), ()))
 HALF = 256
@@ -26,7 +26,11 @@
 
 def along_y(value, steps):
     count = lax.axis_size(Y)
-    pairs = [(source, (source + steps) % count) for source in range(count)]
+    sign = 1 if steps % 2 else -1
+    pairs = [
+        (source, (source + (sign * steps if source % 2 else -sign * steps)) % count)
+        for source in range(count)
+    ]
     return lax.ppermute(value, Y, pairs)
 
 
@@ -38,8 +42,9 @@
     return swapped(value, "core")
 
 
-def call(kernel, name, out_shape, args, flops, scratch=(), scalars=0, vmem=VMEM):
-    spaces = [pltpu.SMEM] * scalars + [pltpu.VMEM] * (len(args) - scalars)
+def call(kernel, name, out_shape, args, flops, scratch=(), scalars=0, far=0, vmem=VMEM):
+    near = len(args) - scalars - far
+    spaces = [pltpu.SMEM] * scalars + [pltpu.VMEM] * near + [pltpu.HBM] * far
     return pl.pallas_call(
         kernel,
         out_shape=out_shape,
@@ -67,19 +72,26 @@
 
 
 def wgrad_kernel(core_ref, mine_ref, other_ref, *refs):
-    lines, out_ref, total_ref, cols_ref = refs[:-3], refs[-3], refs[-2], refs[-1]
+    far, (out_ref, total_ref, cols_ref, lines, sems) = refs[:-5], refs[-5:]
+    copies = [
+        pltpu.make_async_copy(ref, lines.at[step], sems.at[step]) for step, ref in enumerate(far)
+    ]
+    for copy in copies:
+        copy.start()
     chips, height, wide = mine_ref.shape
-    share = height // len(refs[:-3])
-    d_all = lines[0].shape[0]
+    share = height // len(far)
+    d_all = far[0].shape[0]
     d_txt = 2 * HALF
     d_img = d_all - d_txt
     sums = [None] * 3
-    for step, line_ref in enumerate(lines):
+    for step, copy in enumerate(copies):
+        line_ref = lines.at[step]
         for chip in range(chips):
             for ref, core in ((mine_ref, core_ref[0]), (other_ref, 1 - core_ref[0])):
                 row = pl.multiple_of((2 * chip + core) * share, share)
                 cols_ref[step, pl.ds(row, share)] = ref[chip, step * share : (step + 1) * share]
         cols = cols_ref[step].T
+        copy.wait()
         img_cols, txt_cols = cols[: wide // 2], cols[wide // 2 :]
         terms = [
             jnp.dot(txt_cols, line_ref[:HALF], preferred_element_type=F32),
@@ -137,7 +149,7 @@
     member = lax.axis_index(X)
     anchor = lax.axis_index(DP)
     blocks = lax.axis_size(DP)
-    quad = lax.axis_size("yl")
+    quad = lax.axis_size("yq")
     peers = blocks // quad
     rows = image_feats.shape[0]
     share = rows // groups
@@ -154,7 +166,7 @@
         (image_feats.T, text_feats, image_proj, text_proj),
         2 * rows * (d_img + d_txt) * embed,
     )
-    below, above = along_y(pack, 1), along_y(pack, -1)
+    second = along_y(pack, 1)
     parts = lax.all_to_all(parts, X, 0, 0, tiled=True)
     summed = jnp.sum(parts.astype(F32), axis=0)
     length = jnp.sqrt(jnp.sum(summed * summed, axis=1, keepdims=True) + NORM_EPS)
@@ -165,9 +177,9 @@
     img_all = lax.all_to_all(img_all, X, 0, 0, tiled=True).reshape(rows, embed)
     near = shifted(txt_own, 1)
     pair = jnp.concatenate([txt_own, near])
-    pair, below, above = lax.optimization_barrier((pair, below, above))
+    pair, second, held = lax.optimization_barrier((pair, second, pack))
     far = shifted(pair, 2)
-    lines = [below, pack, above, along_y(above, -1)]
+    third = along_y(held, 2)
     cols = jnp.concatenate([pair, far])
     offsets = jnp.arange(STEPS, dtype=jnp.int32)
     col_ids = (
@@ -186,32 +198,34 @@
     img_terms = jnp.dot(weights, cols, preferred_element_type=F32).astype(BF16)
     back = shifted(txt_terms[2 * share :].astype(BF16), -2)
     img_terms = lax.all_to_all(img_terms.reshape(groups, share, embed), X, 0, 0, tiled=True)
-    img_terms, lines[3] = lax.optimization_barrier((img_terms, lines[3]))
+    img_terms, third = lax.optimization_barrier((img_terms, third))
     two = txt_terms[: 2 * share] + back.astype(F32)
     last = shifted(two[share:].astype(BF16), -1)
     grad_txt = two[:share] + last.astype(F32)
     grad_img = jnp.sum(img_terms.astype(F32), axis=0)
     grad = jnp.concatenate([grad_img, grad_txt])
     grad_summed = ((grad - unit * jnp.sum(unit * grad, axis=1, keepdims=True)) / length).astype(BF16)
-    strip = embed // lax.axis_size(Y)
-    by_cols = grad_summed.reshape(2, share, embed // (quad * strip), quad, strip)
-    by_cols = by_cols.transpose(3, 1, 0, 2, 4).reshape(quad, share, 2 * embed // quad)
-    by_cols = jnp.concatenate([by_cols] * (lax.axis_size(Y) // quad))
+    wide = embed // quad
+    by_cols = grad_summed.reshape(2, share, quad, 1, wide).transpose(2, 3, 1, 0, 4)
+    by_cols = jnp.broadcast_to(by_cols, (quad, lax.axis_size("yp"), share, 2, wide))
+    by_cols = by_cols.reshape(lax.axis_size(Y), share, 2 * wide)
     by_cols = lax.all_to_all(by_cols, Y, 0, 0, tiled=True)
     pieces = [grad_summed, swapped(grad_summed, "xh")]
     by_cols, pieces = lax.optimization_barrier((by_cols, pieces))
     y_index = lax.axis_index(Y)
+    sign = 2 * lax.axis_index("yp") - 1
     window = [
-        lax.dynamic_index_in_dim(by_cols, lax.rem(y_index + (step + lax.axis_size(Y)), lax.axis_size(Y)), 0, False)
-        for step in (-1, 0, 1, 2)
+        lax.dynamic_index_in_dim(by_cols, (y_index + sign * step) & (lax.axis_size(Y) - 1), 0, False)
+        for step in range(quad)
     ]
     mine = jnp.concatenate(window)
+    mine, second = lax.optimization_barrier((mine, second))
+    lines = [pack, second, third, along_y(second, 2)]
     mine = jnp.broadcast_to(mine[None], (chips,) + mine.shape)
     mine = lax.all_to_all(mine, CHIPS, 0, 0, tiled=True)
     other = core_swapped(mine)
     pieces.append(swapped(jnp.concatenate(pieces), "xl"))
     pieces.append(core_swapped(jnp.concatenate(pieces)))
-    wide = 2 * embed // quad
     height = 4 * embed // blocks
     wgrad = call(
         wgrad_kernel,
@@ -219,10 +233,17 @@
         jax.ShapeDtypeStruct((peers, height, HALF), BF16),
         (lax.axis_index("core").astype(jnp.int32).reshape(1), mine, other, *lines),
         2 * quad * rows * (embed // quad) * (d_img + d_txt),
-        scratch=(pltpu.VMEM((peers, height, HALF), F32), pltpu.VMEM((quad, rows, wide), BF16)),
+        scratch=(
+            pltpu.VMEM((peers, height, HALF), F32),
+            pltpu.VMEM((quad, rows, 2 * wide), BF16),
+            pltpu.VMEM((quad, d_txt + d_img, HALF), BF16),
+            pltpu.SemaphoreType.DMA((quad,)),
+        ),
         scalars=1,
-    )
-    wgrad = lax.all_to_all(wgrad, ("yh", "z"), 0, 0, tiled=True)
+        far=quad,
+        vmem=VMEM // 4,
+    )
+    wgrad = lax.all_to_all(wgrad, ("yp", "z"), 0, 0, tiled=True)
     image_grad, text_grad = call(
         feature_grads_kernel,
         "feature_grads",
@@ -231,6 +252,7 @@
         2 * rows * (d_img + d_txt) * embed,
         scratch=(pltpu.VMEM((rows, embed), BF16), pltpu.VMEM((rows, embed), BF16)),
         scalars=1,
+        vmem=VMEM // 4,
     )
     img_wgrad, txt_wgrad = call(
         total_kernel,
@@ -248,7 +270,7 @@
 
 
 def solution(mesh):
-    fine = Mesh(mesh.devices.reshape(2, 4, 8, 2, 2, 2), DP + X)
+    fine = Mesh(mesh.devices.reshape(4, 2, 8, 2, 2, 2), DP + X)
     placed = (P(DP, X), P(DP, X), P(X, None), P(X, None), P(DP), P(), P())
     return jax.shard_map(
         on_device,

time: 132 us -> 125 us (0.947)
  the two profiles are of different devices: /device:TPU:8 before, /device:TPU:6 now
where the time goes in v7:
time: 125 us; the launch traced here: 123 us
  starting transfers between devices  67.9 us (54%)
  waiting for transfers between devices  38.6 us (31%)
  Pallas kernels  8.11 us (6%)
  local copies, waits for them, and re-layouts  3.4 us (3%)
  between operations  2.29 us (2%)
  matrix products  1.51 us (1%)
    ppermute x4, starting transfers between devices, shifted(): return lax.ppermute(value, DP, pairs)  16.3 us
    all_to_all x1, starting transfers between devices, on_device(): parts = lax.all_to_all(parts, X, 0, 0, tiled=True)  9.46 us
    ppermute x4, waiting for transfers between devices, shifted(): return lax.ppermute(value, DP, pairs)  9.14 us
    ppermute x3, starting transfers between devices, along_y(): return lax.ppermute(value, Y, pairs)  9.13 us
    all_to_all x1, waiting for transfers between devices, on_device(): parts = lax.all_to_all(parts, X, 0, 0, tiled=True)  9.11 us
    ppermute x4, starting transfers between devices, swapped(): return lax.ppermute(value, axis, [(0, 1), (1, 0)])  9.08 us
    pallas_call x4, Pallas kernels, call(): pl.pallas_call(kernel, out_shape=out_shape, in_specs=[pl.BlockSpec(memory...  8.11 us
    ppermute x4, waiting for transfers between devices, swapped(): return lax.ppermute(value, axis, [(0, 1), (1, 0)])  6.34 us
  transfers between devices with their start and end apart: 17, of which 10 were waited for; matrix products, arithmetic and copies ran while one was open for 3% of the time, Pallas kernels for 4%

profile of v7, /device:TPU:6, one launch (start us, length us, event | category | flops | bytes accessed | tf_op | source)
XLA Modules:
  0.0 122.8 jit_solution(13203433122997665567)
XLA Ops:
  0.6 3.1 %project.1 = (bf16[8,64,768]{2,1,0:T(8,128)(2,1)}, bf16[912,256]{1,0:T(8,128)(2,1)}) custom-call(bf16[400,256]{1,0:T(8,128)(2,1)} %bitcast.33, bf16[256,512]{1,0:T(8,128)(2,1)} %txt_ref.1, bf16[400,768]{1,0:T(8,128)(2,1)} %img_proj_ref.3, bf16[512,768]{1,0:T(8,128)(2,1)} %txt_proj_ref.3), custom_call_target="tpu_custom_call" | custom-call | flops 358612992 | bytes 4000000 | tf_op jit(solution)/shard_map/project/pallas_call | solution.py:48
  3.7 9.5 %all-to-all-start = ((bf16[8,64,768]{2,1,0:T(8,128)(2,1)}), bf16[8,64,768]{2,1,0:T(8,128)(2,1)S(1)}, u32[]{:S(2)}, u32[]{:S(2)}) async-start(bf16[8,64,768]{2,1,0:T(8,128)(2,1)} %get-tuple-element.20), calls=%async_computation | async-start | bytes 1572864 | tf_op jit(solution)/shard_map/all_to_all | solution.py:170
  13.2 1.9 %collective-permute-start.1 = (bf16[912,256]{1,0:T(8,128)(2,1)S(1)}, bf16[912,256]{1,0:T(8,128)(2,1)S(1)}, u32[]{:S(2)}, u32[]{:S(2)}) collective-permute-start(bf16[912,256]{1,0:T(8,128)(2,1)S(1)} %copy-done.2), channel_id=1, source_target_pairs={{0,448},{64,128},{128,64},{192,256},{256,192},{320,384},{384,320},... | collective-permute-start | bytes 1400840 | tf_op jit(solution)/shard_map/ppermute | solution.py:34
  15.2 9.1 %all-to-all-done = bf16[8,64,768]{2,1,0:T(8,128)(2,1)S(1)} async-done(((bf16[8,64,768]{2,1,0:T(8,128)(2,1)}), bf16[8,64,768]{2,1,0:T(8,128)(2,1)S(1)}, u32[]{:S(2)}, u32[]{:S(2)}) %all-to-all-start) | async-done | bytes 786464 | tf_op jit(solution)/shard_map/all_to_all | solution.py:170
  24.6 1.9 %collective-permute-start = (bf16[32,768]{1,0:T(8,128)(2,1)S(1)}, bf16[32,768]{1,0:T(8,128)(2,1)S(1)}, u32[]{:S(2)}, u32[]{:S(2)}) collective-permute-start(bf16[32,768]{1,0:T(8,128)(2,1)S(1)} %get-tuple-element.42), channel_id=1, source_target_pairs={{0,8},{8,16},{16,24},{24,32},{32,40},{40,48},{48,56},{56,64},{64,7... | collective-permute-start | bytes 147464 | tf_op jit(solution)/shard_map/ppermute | solution.py:24
  28.1 5.6 %all-to-all-start.1 = ((bf16[8,32,768]{2,1,0:T(8,128)(2,1)}), bf16[8,32,768]{2,1,0:T(8,128)(2,1)S(1)}, u32[]{:S(2)}, u32[]{:S(2)}) async-start(bf16[8,32,768]{2,1,0:T(8,128)(2,1)} %broadcast_in_dim.18), calls=%async_computation.1 | async-start | bytes 786432 | tf_op jit(solution)/shard_map/all_to_all | solution.py:177
  34.4 1.6 %collective-permute-done = bf16[32,768]{1,0:T(8,128)(2,1)S(1)} collective-permute-done((bf16[32,768]{1,0:T(8,128)(2,1)S(1)}, bf16[32,768]{1,0:T(8,128)(2,1)S(1)}, u32[]{:S(2)}, u32[]{:S(2)}) %collective-permute-start) | collective-permute-done | bytes 49184 | tf_op jit(solution)/shard_map/ppermute | solution.py:24
  36.0 2.3 %collective-permute-start.2 = (bf16[64,768]{1,0:T(8,128)(2,1)S(1)}, bf16[64,768]{1,0:T(8,128)(2,1)S(1)}, u32[]{:S(2)}, u32[]{:S(2)}) collective-permute-start(bf16[64,768]{1,0:T(8,128)(2,1)S(1)} %pad_maximum_fusion.3), channel_id=1, source_target_pairs={{0,16},{8,24},{16,32},{24,40},{32,48},{40,56},{48,64},{56,72},{64,... | collective-permute-start | bytes 294920 | tf_op jit(solution)/shard_map/ppermute | solution.py:24
  38.3 4.5 %collective-permute-start.3 = (bf16[912,256]{1,0:T(8,128)(2,1)S(1)}, bf16[912,256]{1,0:T(8,128)(2,1)S(1)}, u32[]{:S(2)}, u32[]{:S(2)}) collective-permute-start(bf16[912,256]{1,0:T(8,128)(2,1)S(1)} %copy-done.2), channel_id=1, source_target_pairs={{0,128},{64,448},{128,256},{192,64},{256,384},{320,192},{384,0},{4... | collective-permute-start | bytes 1400840 | tf_op jit(solution)/shard_map/ppermute | solution.py:34
  42.9 6.1 %collective-permute-done.2 = bf16[64,768]{1,0:T(8,128)(2,1)S(1)} collective-permute-done((bf16[64,768]{1,0:T(8,128)(2,1)S(1)}, bf16[64,768]{1,0:T(8,128)(2,1)S(1)}, u32[]{:S(2)}, u32[]{:S(2)}) %collective-permute-start.2) | collective-permute-done | bytes 98336 | tf_op jit(solution)/shard_map/ppermute | solution.py:24
  49.5 6.0 %collective-permute-start.4 = (bf16[64,768]{1,0:T(8,128)(2,1)S(1)}, bf16[64,768]{1,0:T(8,128)(2,1)S(1)}, u32[]{:S(2)}, u32[]{:S(2)}) collective-permute-start(bf16[64,768]{1,0:T(8,128)(2,1)S(1)} %slice.36), channel_id=1, source_target_pairs={{0,496},{8,504},{16,0},{24,8},{32,16},{40,24},{48,32},{56,40},{64,... | collective-permute-start | bytes 294920 | tf_op jit(solution)/shard_map/ppermute | solution.py:24
  55.6 1.0 convolution_convert_fusion
  56.6 4.8 %all-to-all-start.2 = ((bf16[8,32,768]{2,1,0:T(8,128)(2,1)}), bf16[8,32,768]{2,1,0:T(8,128)(2,1)S(1)}, u32[]{:S(2)}, u32[]{:S(2)}) async-start(bf16[8,32,768]{2,1,0:T(8,128)(2,1)} %bitcast.5), calls=%async_computation.2 | async-start | bytes 786432 | tf_op jit(solution)/shard_map/all_to_all | solution.py:200
  61.4 6.1 %collective-permute-start.5 = (bf16[32,768]{1,0:T(8,128)(2,1)S(1)}, bf16[32,768]{1,0:T(8,128)(2,1)S(1)}, u32[]{:S(2)}, u32[]{:S(2)}) collective-permute-start(bf16[32,768]{1,0:T(8,128)(2,1)S(1)} %slice.37), channel_id=1, source_target_pairs={{0,504},{8,0},{16,8},{24,16},{32,24},{40,32},{48,40},{56,48},{64,5... | collective-permute-start | bytes 147464 | tf_op jit(solution)/shard_map/ppermute | solution.py:24
  67.7 1.4 %collective-permute-done.5 = bf16[32,768]{1,0:T(8,128)(2,1)S(1)} collective-permute-done((bf16[32,768]{1,0:T(8,128)(2,1)S(1)}, bf16[32,768]{1,0:T(8,128)(2,1)S(1)}, u32[]{:S(2)}, u32[]{:S(2)}) %collective-permute-start.5) | collective-permute-done | bytes 49184 | tf_op jit(solution)/shard_map/ppermute | solution.py:24
  70.4 0.8 reshape.118
  71.2 4.1 %all-to-all-start.3 = ((bf16[8,32,384]{2,1,0:T(8,128)(2,1)}), bf16[8,32,384]{2,1,0:T(8,128)(2,1)S(1)}, u32[]{:S(2)}, u32[]{:S(2)}) async-start(bf16[8,32,384]{2,1,0:T(8,128)(2,1)} %reshape.118), calls=%async_computation.3 | async-start | bytes 393216 | tf_op jit(solution)/shard_map/all_to_all | solution.py:212
  75.3 3.3 %collective-permute-start.6 = (bf16[64,768]{1,0:T(8,128)(2,1)S(1)}, bf16[64,768]{1,0:T(8,128)(2,1)S(1)}, u32[]{:S(2)}, u32[]{:S(2)}) collective-permute-start(bf16[64,768]{1,0:T(8,128)(2,1)S(1)} %get-tuple-element.25.own_ref), channel_id=1, source_target_pairs={{0,4},{4,0},{1,5},{5,1},{2,6},{6,2},{3,7},{7,3},{8,12},{12,8},{9,1... | collective-permute-start | bytes 294920 | tf_op jit(solution)/shard_map/ppermute | solution.py:38
  78.7 4.6 %collective-permute-done.6.high_ref = bf16[64,768]{1,0:T(8,128)(2,1)S(1)} collective-permute-done((bf16[64,768]{1,0:T(8,128)(2,1)S(1)}, bf16[64,768]{1,0:T(8,128)(2,1)S(1)}, u32[]{:S(2)}, u32[]{:S(2)}) %collective-permute-start.6) | collective-permute-done | bytes 98336 | tf_op jit(solution)/shard_map/ppermute | solution.py:38
  83.3 1.8 %all-to-all-done.3 = bf16[8,32,384]{2,1,0:T(8,128)(2,1)S(1)} async-done(((bf16[8,32,384]{2,1,0:T(8,128)(2,1)}), bf16[8,32,384]{2,1,0:T(8,128)(2,1)S(1)}, u32[]{:S(2)}, u32[]{:S(2)}) %all-to-all-start.3) | async-done | bytes 196640 | tf_op jit(solution)/shard_map/all_to_all | solution.py:212
  85.9 5.1 %all-to-all-start.4 = ((bf16[4,128,384]{2,1,0:T(8,128)(2,1)}), bf16[4,128,384]{2,1,0:T(8,128)(2,1)S(1)}, u32[]{:S(2)}, u32[]{:S(2)}) async-start(bf16[4,128,384]{2,1,0:T(8,128)(2,1)} %broadcast_in_dim.37), calls=%async_computation.4 | async-start | bytes 786432 | tf_op jit(solution)/shard_map/all_to_all | solution.py:225
  91.0 2.7 %collective-permute-start.10 = (bf16[912,256]{1,0:T(8,128)(2,1)S(1)}, bf16[912,256]{1,0:T(8,128)(2,1)S(1)}, u32[]{:S(2)}, u32[]{:S(2)}) collective-permute-start(bf16[912,256]{1,0:T(8,128)(2,1)S(1)} %collective-permute-done.1.refs_1_), channel_id=1, source_target_pairs={{0,128},{64,448},{128,256},{192,64},{256,384},{320,192},{384,0},{4... | collective-permute-start | bytes 1400840 | tf_op jit(solution)/shard_map/ppermute | solution.py:34
  93.8 2.6 %all-to-all-done.4.mine_ref = bf16[4,128,384]{2,1,0:T(8,128)(2,1)S(1)} async-done(((bf16[4,128,384]{2,1,0:T(8,128)(2,1)}), bf16[4,128,384]{2,1,0:T(8,128)(2,1)S(1)}, u32[]{:S(2)}, u32[]{:S(2)}) %all-to-all-start.4) | async-done | bytes 393248 | tf_op jit(solution)/shard_map/all_to_all | solution.py:225
  96.3 1.9 %collective-permute-start.9 = (bf16[4,128,384]{2,1,0:T(8,128)(2,1)S(1)}, bf16[4,128,384]{2,1,0:T(8,128)(2,1)S(1)}, u32[]{:S(2)}, u32[]{:S(2)}) collective-permute-start(bf16[4,128,384]{2,1,0:T(8,128)(2,1)S(1)} %all-to-all-done.4.mine_ref), channel_id=1, source_target_pairs={{0,1},{1,0},{2,3},{3,2},{4,5},{5,4},{6,7},{7,6},{8,9},{9,8},{10,11... | collective-permute-start | bytes 1179656 | tf_op jit(solution)/shard_map/ppermute | solution.py:38
  98.3 1.9 %collective-permute-start.7 = (bf16[128,768]{1,0:T(8,128)(2,1)S(1)}, bf16[128,768]{1,0:T(8,128)(2,1)S(1)}, u32[]{:S(2)}, u32[]{:S(2)}) collective-permute-start(bf16[128,768]{1,0:T(8,128)(2,1)S(1)} %pad_maximum_fusion.2), channel_id=1, source_target_pairs={{0,2},{2,0},{1,3},{3,1},{4,6},{6,4},{5,7},{7,5},{8,10},{10,8},{9,1... | collective-permute-start | bytes 589832 | tf_op jit(solution)/shard_map/ppermute | solution.py:38
  100.2 4.8 %collective-permute-done.10.refs_3_ = bf16[912,256]{1,0:T(8,128)(2,1)S(1)} collective-permute-done((bf16[912,256]{1,0:T(8,128)(2,1)S(1)}, bf16[912,256]{1,0:T(8,128)(2,1)S(1)}, u32[]{:S(2)}, u32[]{:S(2)}) %collective-permute-start.10) | collective-permute-done | bytes 466976 | tf_op jit(solution)/shard_map/ppermute | solution.py:34
  105.0 3.1 %project_grads.1 = bf16[16,48,256]{2,1,0:T(8,128)(2,1)} custom-call(s32[1]{0:T(128)} %bitcast.9.core_ref, bf16[4,128,384]{2,1,0:T(8,128)(2,1)S(1)} %all-to-all-done.4.mine_ref, bf16[4,128,384]{2,1,0:T(8,128)(2,1)S(1)} %collective-permute-done.9.other_ref, bf16[912,256]{1,0:T(8,128)(2,1)S(1)} %copy-done.2, ...), custom_call_target="tpu_custom_call" | custom-call | flops 358612992 | bytes 4000000 | tf_op jit(solution)/shard_map/project_grads/pallas_call | solution.py:48
  108.2 4.3 %all-to-all-start.5 = ((bf16[16,48,256]{2,1,0:T(8,128)(2,1)}), bf16[16,48,256]{2,1,0:T(8,128)(2,1)S(1)}, u32[]{:S(2)}, u32[]{:S(2)}) async-start(bf16[16,48,256]{2,1,0:T(8,128)(2,1)} %project_grads.1), calls=%async_computation.5 | async-start | bytes 786432 | tf_op jit(solution)/shard_map/all_to_all | solution.py:246
  112.5 1.9 %collective-permute-start.8 = (bf16[256,768]{1,0:T(8,128)(2,1)S(1)}, bf16[256,768]{1,0:T(8,128)(2,1)S(1)}, u32[]{:S(2)}, u32[]{:S(2)}) collective-permute-start(bf16[256,768]{1,0:T(8,128)(2,1)S(1)} %pad_maximum_fusion), channel_id=1, source_target_pairs={{0,1},{1,0},{2,3},{3,2},{4,5},{5,4},{6,7},{7,6},{8,9},{9,8},{10,11... | collective-permute-start | bytes 1179656 | tf_op jit(solution)/shard_map/ppermute | solution.py:38
  114.5 1.7 %collective-permute-done.8.core_ref = bf16[256,768]{1,0:T(8,128)(2,1)S(1)} collective-permute-done((bf16[256,768]{1,0:T(8,128)(2,1)S(1)}, bf16[256,768]{1,0:T(8,128)(2,1)S(1)}, u32[]{:S(2)}, u32[]{:S(2)}) %collective-permute-start.8) | collective-permute-done | bytes 393248 | tf_op jit(solution)/shard_map/ppermute | solution.py:38
  116.1 1.2 %feature_grads.1 = (bf16[400,256]{1,0:T(8,128)(2,1)}, bf16[256,512]{1,0:T(8,128)(2,1)}) custom-call(s32[1]{0:T(128)} %bitcast.member_ref, bf16[64,768]{1,0:T(8,128)(2,1)S(1)} %get-tuple-element.25.own_ref, bf16[64,768]{1,0:T(8,128)(2,1)S(1)} %collective-permute-done.6.high_ref, bf16[128,768]{1,0:T(8,128)(2,1)S(1)} %collective-permute-done.7.low_ref, ...), custom_call_target="tpu_custom_call" | custom-call | flops 358612992 | bytes 4000000 | tf_op jit(solution)/shard_map/feature_grads/pallas_call | solution.py:48
  117.4 4.8 %all-to-all-done.5.blocks_ref = bf16[16,48,256]{2,1,0:T(8,128)(2,1)S(1)} async-done(((bf16[16,48,256]{2,1,0:T(8,128)(2,1)}), bf16[16,48,256]{2,1,0:T(8,128)(2,1)S(1)}, u32[]{:S(2)}, u32[]{:S(2)}) %all-to-all-start.5) | async-done | bytes 393248 | tf_op jit(solution)/shard_map/all_to_all | solution.py:246
  (49 shorter events, 4.8 us)
Async XLA Ops:
  3.7 9.5 %copy-start.2 = (bf16[912,256]{1,0:T(8,128)(2,1)S(1)}, bf16[912,256]{1,0:T(8,128)(2,1)}, u32[]{:S(2)}) copy-start(bf16[912,256]{1,0:T(8,128)(2,1)} %get-tuple-element.23.refs_0_) | copy-start | bytes 1400836
  3.7 20.5 %all-to-all-start = ((bf16[8,64,768]{2,1,0:T(8,128)(2,1)}), bf16[8,64,768]{2,1,0:T(8,128)(2,1)S(1)}, u32[]{:S(2)}, u32[]{:S(2)}) async-start(bf16[8,64,768]{2,1,0:T(8,128)(2,1)} %get-tuple-element.20), calls=%async_computation | async-start | bytes 1572864 | tf_op jit(solution)/shard_map/all_to_all | solution.py:170
  13.2 22.8 %collective-permute-start.1 = (bf16[912,256]{1,0:T(8,128)(2,1)S(1)}, bf16[912,256]{1,0:T(8,128)(2,1)S(1)}, u32[]{:S(2)}, u32[]{:S(2)}) collective-permute-start(bf16[912,256]{1,0:T(8,128)(2,1)S(1)} %copy-done.2), channel_id=1, source_target_pairs={{0,448},{64,128},{128,64},{192,256},{256,192},{320,384},{384,320},... | collective-permute-start | bytes 1400840 | tf_op jit(solution)/shard_map/ppermute | solution.py:34
  24.6 11.4 %collective-permute-start = (bf16[32,768]{1,0:T(8,128)(2,1)S(1)}, bf16[32,768]{1,0:T(8,128)(2,1)S(1)}, u32[]{:S(2)}, u32[]{:S(2)}) collective-permute-start(bf16[32,768]{1,0:T(8,128)(2,1)S(1)} %get-tuple-element.42), channel_id=1, source_target_pairs={{0,8},{8,16},{16,24},{24,32},{32,40},{40,48},{48,56},{56,64},{64,7... | collective-permute-start | bytes 147464 | tf_op jit(solution)/shard_map/ppermute | solution.py:24
  28.1 20.8 %copy-start.3 = (s32[256]{0:T(256)S(1)}, s32[256]{0:T(256)}, u32[]{:S(2)}) copy-start(s32[256]{0:T(256)} %param.11) | copy-start | bytes 3076
  28.1 20.8 %all-to-all-start.1 = ((bf16[8,32,768]{2,1,0:T(8,128)(2,1)}), bf16[8,32,768]{2,1,0:T(8,128)(2,1)S(1)}, u32[]{:S(2)}, u32[]{:S(2)}) async-start(bf16[8,32,768]{2,1,0:T(8,128)(2,1)} %broadcast_in_dim.18), calls=%async_computation.1 | async-start | bytes 786432 | tf_op jit(solution)/shard_map/all_to_all | solution.py:177
  36.0 12.9 %collective-permute-start.2 = (bf16[64,768]{1,0:T(8,128)(2,1)S(1)}, bf16[64,768]{1,0:T(8,128)(2,1)S(1)}, u32[]{:S(2)}, u32[]{:S(2)}) collective-permute-start(bf16[64,768]{1,0:T(8,128)(2,1)S(1)} %pad_maximum_fusion.3), channel_id=1, source_target_pairs={{0,16},{8,24},{16,32},{24,40},{32,48},{40,56},{48,64},{56,72},{64,... | collective-permute-start | bytes 294920 | tf_op jit(solution)/shard_map/ppermute | solution.py:24
  38.3 30.9 %collective-permute-start.3 = (bf16[912,256]{1,0:T(8,128)(2,1)S(1)}, bf16[912,256]{1,0:T(8,128)(2,1)S(1)}, u32[]{:S(2)}, u32[]{:S(2)}) collective-permute-start(bf16[912,256]{1,0:T(8,128)(2,1)S(1)} %copy-done.2), channel_id=1, source_target_pairs={{0,128},{64,448},{128,256},{192,64},{256,384},{320,192},{384,0},{4... | collective-permute-start | bytes 1400840 | tf_op jit(solution)/shard_map/ppermute | solution.py:34
  49.5 11.8 %collective-permute-start.4 = (bf16[64,768]{1,0:T(8,128)(2,1)S(1)}, bf16[64,768]{1,0:T(8,128)(2,1)S(1)}, u32[]{:S(2)}, u32[]{:S(2)}) collective-permute-start(bf16[64,768]{1,0:T(8,128)(2,1)S(1)} %slice.36), channel_id=1, source_target_pairs={{0,496},{8,504},{16,0},{24,8},{32,16},{40,24},{48,32},{56,40},{64,... | collective-permute-start | bytes 294920 | tf_op jit(solution)/shard_map/ppermute | solution.py:24
  56.6 12.7 %all-to-all-start.2 = ((bf16[8,32,768]{2,1,0:T(8,128)(2,1)}), bf16[8,32,768]{2,1,0:T(8,128)(2,1)S(1)}, u32[]{:S(2)}, u32[]{:S(2)}) async-start(bf16[8,32,768]{2,1,0:T(8,128)(2,1)} %bitcast.5), calls=%async_computation.2 | async-start | bytes 786432 | tf_op jit(solution)/shard_map/all_to_all | solution.py:200
  61.4 7.8 %collective-permute-start.5 = (bf16[32,768]{1,0:T(8,128)(2,1)S(1)}, bf16[32,768]{1,0:T(8,128)(2,1)S(1)}, u32[]{:S(2)}, u32[]{:S(2)}) collective-permute-start(bf16[32,768]{1,0:T(8,128)(2,1)S(1)} %slice.37), channel_id=1, source_target_pairs={{0,504},{8,0},{16,8},{24,16},{32,24},{40,32},{48,40},{56,48},{64,5... | collective-permute-start | bytes 147464 | tf_op jit(solution)/shard_map/ppermute | solution.py:24
  71.2 13.9 %all-to-all-start.3 = ((bf16[8,32,384]{2,1,0:T(8,128)(2,1)}), bf16[8,32,384]{2,1,0:T(8,128)(2,1)S(1)}, u32[]{:S(2)}, u32[]{:S(2)}) async-start(bf16[8,32,384]{2,1,0:T(8,128)(2,1)} %reshape.118), calls=%async_computation.3 | async-start | bytes 393216 | tf_op jit(solution)/shard_map/all_to_all | solution.py:212
  75.3 8.0 %collective-permute-start.6 = (bf16[64,768]{1,0:T(8,128)(2,1)S(1)}, bf16[64,768]{1,0:T(8,128)(2,1)S(1)}, u32[]{:S(2)}, u32[]{:S(2)}) collective-permute-start(bf16[64,768]{1,0:T(8,128)(2,1)S(1)} %get-tuple-element.25.own_ref), channel_id=1, source_target_pairs={{0,4},{4,0},{1,5},{5,1},{2,6},{6,2},{3,7},{7,3},{8,12},{12,8},{9,1... | collective-permute-start | bytes 294920 | tf_op jit(solution)/shard_map/ppermute | solution.py:38
  85.9 10.4 %all-to-all-start.4 = ((bf16[4,128,384]{2,1,0:T(8,128)(2,1)}), bf16[4,128,384]{2,1,0:T(8,128)(2,1)S(1)}, u32[]{:S(2)}, u32[]{:S(2)}) async-start(bf16[4,128,384]{2,1,0:T(8,128)(2,1)} %broadcast_in_dim.37), calls=%async_computation.4 | async-start | bytes 786432 | tf_op jit(solution)/shard_map/all_to_all | solution.py:225
  91.0 14.0 %collective-permute-start.10 = (bf16[912,256]{1,0:T(8,128)(2,1)S(1)}, bf16[912,256]{1,0:T(8,128)(2,1)S(1)}, u32[]{:S(2)}, u32[]{:S(2)}) collective-permute-start(bf16[912,256]{1,0:T(8,128)(2,1)S(1)} %collective-permute-done.1.refs_1_), channel_id=1, source_target_pairs={{0,128},{64,448},{128,256},{192,64},{256,384},{320,192},{384,0},{4... | collective-permute-start | bytes 1400840 | tf_op jit(solution)/shard_map/ppermute | solution.py:34
  96.3 8.7 %collective-permute-start.9 = (bf16[4,128,384]{2,1,0:T(8,128)(2,1)S(1)}, bf16[4,128,384]{2,1,0:T(8,128)(2,1)S(1)}, u32[]{:S(2)}, u32[]{:S(2)}) collective-permute-start(bf16[4,128,384]{2,1,0:T(8,128)(2,1)S(1)} %all-to-all-done.4.mine_ref), channel_id=1, source_target_pairs={{0,1},{1,0},{2,3},{3,2},{4,5},{5,4},{6,7},{7,6},{8,9},{9,8},{10,11... | collective-permute-start | bytes 1179656 | tf_op jit(solution)/shard_map/ppermute | solution.py:38
  98.3 14.2 %collective-permute-start.7 = (bf16[128,768]{1,0:T(8,128)(2,1)S(1)}, bf16[128,768]{1,0:T(8,128)(2,1)S(1)}, u32[]{:S(2)}, u32[]{:S(2)}) collective-permute-start(bf16[128,768]{1,0:T(8,128)(2,1)S(1)} %pad_maximum_fusion.2), channel_id=1, source_target_pairs={{0,2},{2,0},{1,3},{3,1},{4,6},{6,4},{5,7},{7,5},{8,10},{10,8},{9,1... | collective-permute-start | bytes 589832 | tf_op jit(solution)/shard_map/ppermute | solution.py:38
  108.1 8.0 %copy-start = (bf16[512,768]{1,0:T(8,128)(2,1)S(1)}, bf16[512,768]{1,0:T(8,128)(2,1)}, u32[]{:S(2)}) copy-start(bf16[512,768]{1,0:T(8,128)(2,1)} %txt_proj_ref.3) | copy-start | bytes 2359300
  108.1 8.0 %copy-start.1 = (bf16[400,768]{1,0:T(8,128)(2,1)S(1)}, bf16[400,768]{1,0:T(8,128)(2,1)}, u32[]{:S(2)}) copy-start(bf16[400,768]{1,0:T(8,128)(2,1)} %img_proj_ref.3) | copy-start | bytes 1843204
  108.2 14.0 %all-to-all-start.5 = ((bf16[16,48,256]{2,1,0:T(8,128)(2,1)}), bf16[16,48,256]{2,1,0:T(8,128)(2,1)S(1)}, u32[]{:S(2)}, u32[]{:S(2)}) async-start(bf16[16,48,256]{2,1,0:T(8,128)(2,1)} %project_grads.1), calls=%async_computation.5 | async-start | bytes 786432 | tf_op jit(solution)/shard_map/all_to_all | solution.py:246
  112.5 3.6 %collective-permute-start.8 = (bf16[256,768]{1,0:T(8,128)(2,1)S(1)}, bf16[256,768]{1,0:T(8,128)(2,1)S(1)}, u32[]{:S(2)}, u32[]{:S(2)}) collective-permute-start(bf16[256,768]{1,0:T(8,128)(2,1)S(1)} %pad_maximum_fusion), channel_id=1, source_target_pairs={{0,1},{1,0},{2,3},{3,2},{4,5},{5,4},{6,7},{7,6},{8,9},{9,8},{10,11... | collective-permute-start | bytes 1179656 | tf_op jit(solution)/shard_map/ppermute | solution.py:38

commit v8 on v7

--- a/solution.py
+++ b/solution.py
@@ -69,6 +69,26 @@
         rows = slice(member * share, (member + 1) * share)
         parts_ref[member, :share] = img[rows]
         parts_ref[member, share:] = txt[rows]
+
+
+def row_grads_kernel(summed_ref, img_ref, txt_ref, last_ref, rows_ref, cols_ref):
+    share = last_ref.shape[0]
+    wide = cols_ref.shape[2] // 2
+    grad_img = img_ref[0].astype(F32)
+    for member in range(1, img_ref.shape[0]):
+        grad_img = grad_img + img_ref[member].astype(F32)
+    grad_txt = txt_ref[:share] + last_ref[...].astype(F32)
+    for tower, grad in enumerate((grad_img, grad_txt)):
+        rows = slice(tower * share, (tower + 1) * share)
+        summed = summed_ref[rows]
+        length = jnp.sqrt(jnp.sum(summed * summed, axis=1, keepdims=True) + NORM_EPS)
+        unit = summed / length
+        grad = (grad - unit * jnp.sum(unit * grad, axis=1, keepdims=True)) / length
+        grad = grad.astype(BF16)
+        rows_ref[rows] = grad
+        for block in range(cols_ref.shape[0]):
+            quarter = slice(block // 2 * wide, (block // 2 + 1) * wide)
+            cols_ref[block, :, tower * wide : (tower + 1) * wide] = grad[:, quarter]
 
 
 def wgrad_kernel(core_ref, mine_ref, other_ref, *refs):
@@ -168,6 +188,16 @@
     )
     second = along_y(pack, 1)
     parts = lax.all_to_all(parts, X, 0, 0, tiled=True)
+    offsets = jnp.arange(STEPS, dtype=jnp.int32)
+    col_ids = (
+        jnp.mod(anchor - offsets, blocks)[:, None] * rows
+        + member * share
+        + jnp.arange(share, dtype=jnp.int32)[None, :]
+    ).reshape(-1)
+    scale_value, bias_value = logit_scale[0], logit_bias[0]
+    parts, col_ids, scale_value, bias_value = lax.optimization_barrier(
+        (parts, col_ids, scale_value, bias_value)
+    )
     summed = jnp.sum(parts.astype(F32), axis=0)
     length = jnp.sqrt(jnp.sum(summed * summed, axis=1, keepdims=True) + NORM_EPS)
     unit = summed / length
@@ -181,13 +211,6 @@
     far = shifted(pair, 2)
     third = along_y(held, 2)
     cols = jnp.concatenate([pair, far])
-    offsets = jnp.arange(STEPS, dtype=jnp.int32)
-    col_ids = (
-        jnp.mod(anchor - offsets, blocks)[:, None] * rows
-        + member * share
-        + jnp.arange(share, dtype=jnp.int32)[None, :]
-    ).reshape(-1)
-    scale_value, bias_value = logit_scale[0], logit_bias[0]
     polarity = jnp.where(labels[:, None] == col_ids[None, :], 1.0, -1.0).astype(F32)
     logits = (
         scale_value * lax.dot_general(img_all, cols, ACROSS, preferred_element_type=F32)
@@ -201,14 +224,18 @@
     img_terms, third = lax.optimization_barrier((img_terms, third))
     two = txt_terms[: 2 * share] + back.astype(F32)
     last = shifted(two[share:].astype(BF16), -1)
-    grad_txt = two[:share] + last.astype(F32)
-    grad_img = jnp.sum(img_terms.astype(F32), axis=0)
-    grad = jnp.concatenate([grad_img, grad_txt])
-    grad_summed = ((grad - unit * jnp.sum(unit * grad, axis=1, keepdims=True)) / length).astype(BF16)
     wide = embed // quad
-    by_cols = grad_summed.reshape(2, share, quad, 1, wide).transpose(2, 3, 1, 0, 4)
-    by_cols = jnp.broadcast_to(by_cols, (quad, lax.axis_size("yp"), share, 2, wide))
-    by_cols = by_cols.reshape(lax.axis_size(Y), share, 2 * wide)
+    grad_summed, by_cols = call(
+        row_grads_kernel,
+        "row_grads",
+        (
+            jax.ShapeDtypeStruct((2 * share, embed), BF16),
+            jax.ShapeDtypeStruct((lax.axis_size(Y), share, 2 * wide), BF16),
+        ),
+        (summed, img_terms, two, last),
+        groups * share * embed,
+        vmem=VMEM // 4,
+    )
     by_cols = lax.all_to_all(by_cols, Y, 0, 0, tiled=True)
     pieces = [grad_summed, swapped(grad_summed, "xh")]
     by_cols, pieces = lax.optimization_barrier((by_cols, pieces))

time: 125 us -> 124 us (level)
  local copies, waits for them, and re-layouts: 3.4 us -> 1.72 us
    pallas_call x4 -> x5, Pallas kernels: 8.11 us -> 9.06 us  [call(): pl.pallas_call(kernel, out_shape=out_shape, in_specs=[pl.BlockSpec(memory...]
  transfers between devices with their start and end apart: 17 -> 17, of which waited for: 10 -> 11; matrix products, arithmetic and copies ran while one was open for 3% -> 2% of each run, Pallas kernels for 4% -> 4%
where the time goes in v8:
time: 124 us; the launch traced here: 122 us
  starting transfers between devices  67.6 us (55%)
  waiting for transfers between devices  38.9 us (31%)
  Pallas kernels  9.06 us (7%)
  between operations  2.23 us (2%)
  local copies, waits for them, and re-layouts  1.72 us (1%)
  matrix products  1.51 us (1%)
    ppermute x4, starting transfers between devices, shifted(): return lax.ppermute(value, DP, pairs)  16.2 us
    all_to_all x1, starting transfers between devices, on_device(): parts = lax.all_to_all(parts, X, 0, 0, tiled=True)  9.46 us
    ppermute x3, starting transfers between devices, along_y(): return lax.ppermute(value, Y, pairs)  9.09 us
    ppermute x4, starting transfers between devices, swapped(): return lax.ppermute(value, axis, [(0, 1), (1, 0)])  9.08 us
    pallas_call x5, Pallas kernels, call(): pl.pallas_call(kernel, out_shape=out_shape, in_specs=[pl.BlockSpec(memory...  9.06 us
    all_to_all x1, waiting for transfers between devices, on_device(): parts = lax.all_to_all(parts, X, 0, 0, tiled=True)  8.95 us
    ppermute x4, waiting for transfers between devices, shifted(): return lax.ppermute(value, DP, pairs)  8.83 us
    ppermute x4, waiting for transfers between devices, swapped(): return lax.ppermute(value, axis, [(0, 1), (1, 0)])  6.34 us
  transfers between devices with their start and end apart: 17, of which 11 were waited for; matrix products, arithmetic and copies ran while one was open for 2% of the time, Pallas kernels for 4%

profile of v8, /device:TPU:6, one launch (start us, length us, event | category | flops | bytes accessed | tf_op | source)
XLA Modules:
  0.0 121.6 jit_solution(10657717297588339311)
XLA Ops:
  0.6 3.1 %project.1 = (bf16[8,64,768]{2,1,0:T(8,128)(2,1)}, bf16[912,256]{1,0:T(8,128)(2,1)}) custom-call(bf16[400,256]{1,0:T(8,128)(2,1)} %bitcast.29, bf16[256,512]{1,0:T(8,128)(2,1)} %txt_ref.1, bf16[400,768]{1,0:T(8,128)(2,1)} %img_proj_ref.3, bf16[512,768]{1,0:T(8,128)(2,1)} %txt_proj_ref.3), custom_call_target="tpu_custom_call" | custom-call | flops 358612992 | bytes 4000000 | tf_op jit(solution)/shard_map/project/pallas_call | solution.py:48
  3.7 9.5 %all-to-all-start = ((bf16[8,64,768]{2,1,0:T(8,128)(2,1)}), bf16[8,64,768]{2,1,0:T(8,128)(2,1)S(1)}, u32[]{:S(2)}, u32[]{:S(2)}) async-start(bf16[8,64,768]{2,1,0:T(8,128)(2,1)} %get-tuple-element.26), calls=%async_computation | async-start | bytes 1572864 | tf_op jit(solution)/shard_map/all_to_all | solution.py:190
  13.2 1.9 %collective-permute-start.1 = (bf16[912,256]{1,0:T(8,128)(2,1)S(1)}, bf16[912,256]{1,0:T(8,128)(2,1)S(1)}, u32[]{:S(2)}, u32[]{:S(2)}) collective-permute-start(bf16[912,256]{1,0:T(8,128)(2,1)S(1)} %copy-done.2), channel_id=1, source_target_pairs={{0,448},{64,128},{128,64},{192,256},{256,192},{320,384},{384,320},... | collective-permute-start | bytes 1400840 | tf_op jit(solution)/shard_map/ppermute | solution.py:34
  15.3 9.0 %all-to-all-done = bf16[8,64,768]{2,1,0:T(8,128)(2,1)S(1)} async-done(((bf16[8,64,768]{2,1,0:T(8,128)(2,1)}), bf16[8,64,768]{2,1,0:T(8,128)(2,1)S(1)}, u32[]{:S(2)}, u32[]{:S(2)}) %all-to-all-start) | async-done | bytes 786464 | tf_op jit(solution)/shard_map/all_to_all | solution.py:190
  24.6 1.9 %collective-permute-start = (bf16[32,768]{1,0:T(8,128)(2,1)S(1)}, bf16[32,768]{1,0:T(8,128)(2,1)S(1)}, u32[]{:S(2)}, u32[]{:S(2)}) collective-permute-start(bf16[32,768]{1,0:T(8,128)(2,1)S(1)} %get-tuple-element.52), channel_id=1, source_target_pairs={{0,8},{8,16},{16,24},{24,32},{32,40},{40,48},{48,56},{56,64},{64,7... | collective-permute-start | bytes 147464 | tf_op jit(solution)/shard_map/ppermute | solution.py:24
  28.6 5.6 %all-to-all-start.1 = ((bf16[8,32,768]{2,1,0:T(8,128)(2,1)}), bf16[8,32,768]{2,1,0:T(8,128)(2,1)S(1)}, u32[]{:S(2)}, u32[]{:S(2)}) async-start(bf16[8,32,768]{2,1,0:T(8,128)(2,1)} %broadcast_in_dim.14), calls=%async_computation.1 | async-start | bytes 786432 | tf_op jit(solution)/shard_map/all_to_all | solution.py:207
  34.2 1.8 %collective-permute-done = bf16[32,768]{1,0:T(8,128)(2,1)S(1)} collective-permute-done((bf16[32,768]{1,0:T(8,128)(2,1)S(1)}, bf16[32,768]{1,0:T(8,128)(2,1)S(1)}, u32[]{:S(2)}, u32[]{:S(2)}) %collective-permute-start) | collective-permute-done | bytes 49184 | tf_op jit(solution)/shard_map/ppermute | solution.py:24
  36.0 2.1 %collective-permute-start.2 = (bf16[64,768]{1,0:T(8,128)(2,1)S(1)}, bf16[64,768]{1,0:T(8,128)(2,1)S(1)}, u32[]{:S(2)}, u32[]{:S(2)}) collective-permute-start(bf16[64,768]{1,0:T(8,128)(2,1)S(1)} %pad_maximum_fusion.2), channel_id=1, source_target_pairs={{0,16},{8,24},{16,32},{24,40},{32,48},{40,56},{48,64},{56,72},{64,... | collective-permute-start | bytes 294920 | tf_op jit(solution)/shard_map/ppermute | solution.py:24
  38.1 4.5 %collective-permute-start.3 = (bf16[912,256]{1,0:T(8,128)(2,1)S(1)}, bf16[912,256]{1,0:T(8,128)(2,1)S(1)}, u32[]{:S(2)}, u32[]{:S(2)}) collective-permute-start(bf16[912,256]{1,0:T(8,128)(2,1)S(1)} %copy-done.2), channel_id=1, source_target_pairs={{0,128},{64,448},{128,256},{192,64},{256,384},{320,192},{384,0},{4... | collective-permute-start | bytes 1400840 | tf_op jit(solution)/shard_map/ppermute | solution.py:34
  42.7 6.1 %collective-permute-done.2 = bf16[64,768]{1,0:T(8,128)(2,1)S(1)} collective-permute-done((bf16[64,768]{1,0:T(8,128)(2,1)S(1)}, bf16[64,768]{1,0:T(8,128)(2,1)S(1)}, u32[]{:S(2)}, u32[]{:S(2)}) %collective-permute-start.2) | collective-permute-done | bytes 98336 | tf_op jit(solution)/shard_map/ppermute | solution.py:24
  49.3 6.0 %collective-permute-start.4 = (bf16[64,768]{1,0:T(8,128)(2,1)S(1)}, bf16[64,768]{1,0:T(8,128)(2,1)S(1)}, u32[]{:S(2)}, u32[]{:S(2)}) collective-permute-start(bf16[64,768]{1,0:T(8,128)(2,1)S(1)} %slice.30), channel_id=1, source_target_pairs={{0,496},{8,504},{16,0},{24,8},{32,16},{40,24},{48,32},{56,40},{64,... | collective-permute-start | bytes 294920 | tf_op jit(solution)/shard_map/ppermute | solution.py:24
  55.4 1.0 convolution_convert_fusion
  56.4 4.8 %all-to-all-start.2 = ((bf16[8,32,768]{2,1,0:T(8,128)(2,1)}), bf16[8,32,768]{2,1,0:T(8,128)(2,1)S(1)}, u32[]{:S(2)}, u32[]{:S(2)}) async-start(bf16[8,32,768]{2,1,0:T(8,128)(2,1)} %bitcast.5), calls=%async_computation.2 | async-start | bytes 786432 | tf_op jit(solution)/shard_map/all_to_all | solution.py:223
  61.2 6.1 %collective-permute-start.5 = (bf16[32,768]{1,0:T(8,128)(2,1)S(1)}, bf16[32,768]{1,0:T(8,128)(2,1)S(1)}, u32[]{:S(2)}, u32[]{:S(2)}) collective-permute-start(bf16[32,768]{1,0:T(8,128)(2,1)S(1)} %slice.31), channel_id=1, source_target_pairs={{0,504},{8,0},{16,8},{24,16},{32,24},{40,32},{48,40},{56,48},{64,5... | collective-permute-start | bytes 147464 | tf_op jit(solution)/shard_map/ppermute | solution.py:24
  68.0 1.0 collective-permute-done.5.last_ref
  69.0 1.0 row_grads.1
  70.0 4.1 %all-to-all-start.3 = ((bf16[8,32,384]{2,1,0:T(8,128)(2,1)}), bf16[8,32,384]{2,1,0:T(8,128)(2,1)S(1)}, u32[]{:S(2)}, u32[]{:S(2)}) async-start(bf16[8,32,384]{2,1,0:T(8,128)(2,1)} %get-tuple-element.35), calls=%async_computation.3 | async-start | bytes 393216 | tf_op jit(solution)/shard_map/all_to_all | solution.py:239
  74.0 3.3 %collective-permute-start.6 = (bf16[64,768]{1,0:T(8,128)(2,1)S(1)}, bf16[64,768]{1,0:T(8,128)(2,1)S(1)}, u32[]{:S(2)}, u32[]{:S(2)}) collective-permute-start(bf16[64,768]{1,0:T(8,128)(2,1)S(1)} %get-tuple-element.37.own_ref), channel_id=1, source_target_pairs={{0,4},{4,0},{1,5},{5,1},{2,6},{6,2},{3,7},{7,3},{8,12},{12,8},{9,1... | collective-permute-start | bytes 294920 | tf_op jit(solution)/shard_map/ppermute | solution.py:38
  77.4 4.6 %collective-permute-done.6.high_ref = bf16[64,768]{1,0:T(8,128)(2,1)S(1)} collective-permute-done((bf16[64,768]{1,0:T(8,128)(2,1)S(1)}, bf16[64,768]{1,0:T(8,128)(2,1)S(1)}, u32[]{:S(2)}, u32[]{:S(2)}) %collective-permute-start.6) | collective-permute-done | bytes 98336 | tf_op jit(solution)/shard_map/ppermute | solution.py:38
  82.0 1.8 %all-to-all-done.3 = bf16[8,32,384]{2,1,0:T(8,128)(2,1)S(1)} async-done(((bf16[8,32,384]{2,1,0:T(8,128)(2,1)}), bf16[8,32,384]{2,1,0:T(8,128)(2,1)S(1)}, u32[]{:S(2)}, u32[]{:S(2)}) %all-to-all-start.3) | async-done | bytes 196640 | tf_op jit(solution)/shard_map/all_to_all | solution.py:239
  84.7 5.1 %all-to-all-start.4 = ((bf16[4,128,384]{2,1,0:T(8,128)(2,1)}), bf16[4,128,384]{2,1,0:T(8,128)(2,1)S(1)}, u32[]{:S(2)}, u32[]{:S(2)}) async-start(bf16[4,128,384]{2,1,0:T(8,128)(2,1)} %broadcast_in_dim.15), calls=%async_computation.4 | async-start | bytes 786432 | tf_op jit(solution)/shard_map/all_to_all | solution.py:252
  89.8 2.7 %collective-permute-start.10 = (bf16[912,256]{1,0:T(8,128)(2,1)S(1)}, bf16[912,256]{1,0:T(8,128)(2,1)S(1)}, u32[]{:S(2)}, u32[]{:S(2)}) collective-permute-start(bf16[912,256]{1,0:T(8,128)(2,1)S(1)} %collective-permute-done.1.refs_1_), channel_id=1, source_target_pairs={{0,128},{64,448},{128,256},{192,64},{256,384},{320,192},{384,0},{4... | collective-permute-start | bytes 1400840 | tf_op jit(solution)/shard_map/ppermute | solution.py:34
  92.5 2.6 %all-to-all-done.4.mine_ref = bf16[4,128,384]{2,1,0:T(8,128)(2,1)S(1)} async-done(((bf16[4,128,384]{2,1,0:T(8,128)(2,1)}), bf16[4,128,384]{2,1,0:T(8,128)(2,1)S(1)}, u32[]{:S(2)}, u32[]{:S(2)}) %all-to-all-start.4) | async-done | bytes 393248 | tf_op jit(solution)/shard_map/all_to_all | solution.py:252
  95.1 1.9 %collective-permute-start.9 = (bf16[4,128,384]{2,1,0:T(8,128)(2,1)S(1)}, bf16[4,128,384]{2,1,0:T(8,128)(2,1)S(1)}, u32[]{:S(2)}, u32[]{:S(2)}) collective-permute-start(bf16[4,128,384]{2,1,0:T(8,128)(2,1)S(1)} %all-to-all-done.4.mine_ref), channel_id=1, source_target_pairs={{0,1},{1,0},{2,3},{3,2},{4,5},{5,4},{6,7},{7,6},{8,9},{9,8},{10,11... | collective-permute-start | bytes 1179656 | tf_op jit(solution)/shard_map/ppermute | solution.py:38
  97.0 1.9 %collective-permute-start.7 = (bf16[128,768]{1,0:T(8,128)(2,1)S(1)}, bf16[128,768]{1,0:T(8,128)(2,1)S(1)}, u32[]{:S(2)}, u32[]{:S(2)}) collective-permute-start(bf16[128,768]{1,0:T(8,128)(2,1)S(1)} %pad_maximum_fusion.1), channel_id=1, source_target_pairs={{0,2},{2,0},{1,3},{3,1},{4,6},{6,4},{5,7},{7,5},{8,10},{10,8},{9,1... | collective-permute-start | bytes 589832 | tf_op jit(solution)/shard_map/ppermute | solution.py:38
  99.0 4.8 %collective-permute-done.10.refs_3_ = bf16[912,256]{1,0:T(8,128)(2,1)S(1)} collective-permute-done((bf16[912,256]{1,0:T(8,128)(2,1)S(1)}, bf16[912,256]{1,0:T(8,128)(2,1)S(1)}, u32[]{:S(2)}, u32[]{:S(2)}) %collective-permute-start.10) | collective-permute-done | bytes 466976 | tf_op jit(solution)/shard_map/ppermute | solution.py:34
  103.8 3.1 %project_grads.1 = bf16[16,48,256]{2,1,0:T(8,128)(2,1)} custom-call(s32[1]{0:T(128)} %bitcast.7.core_ref, bf16[4,128,384]{2,1,0:T(8,128)(2,1)S(1)} %all-to-all-done.4.mine_ref, bf16[4,128,384]{2,1,0:T(8,128)(2,1)S(1)} %collective-permute-done.9.other_ref, bf16[912,256]{1,0:T(8,128)(2,1)S(1)} %copy-done.2, ...), custom_call_target="tpu_custom_call" | custom-call | flops 358612992 | bytes 4000000 | tf_op jit(solution)/shard_map/project_grads/pallas_call | solution.py:48
  106.9 4.3 %all-to-all-start.5 = ((bf16[16,48,256]{2,1,0:T(8,128)(2,1)}), bf16[16,48,256]{2,1,0:T(8,128)(2,1)S(1)}, u32[]{:S(2)}, u32[]{:S(2)}) async-start(bf16[16,48,256]{2,1,0:T(8,128)(2,1)} %project_grads.1), calls=%async_computation.5 | async-start | bytes 786432 | tf_op jit(solution)/shard_map/all_to_all | solution.py:273
  111.2 1.9 %collective-permute-start.8 = (bf16[256,768]{1,0:T(8,128)(2,1)S(1)}, bf16[256,768]{1,0:T(8,128)(2,1)S(1)}, u32[]{:S(2)}, u32[]{:S(2)}) collective-permute-start(bf16[256,768]{1,0:T(8,128)(2,1)S(1)} %pad_maximum_fusion), channel_id=1, source_target_pairs={{0,1},{1,0},{2,3},{3,2},{4,5},{5,4},{6,7},{7,6},{8,9},{9,8},{10,11... | collective-permute-start | bytes 1179656 | tf_op jit(solution)/shard_map/ppermute | solution.py:38
  113.2 1.7 %collective-permute-done.8.core_ref = bf16[256,768]{1,0:T(8,128)(2,1)S(1)} collective-permute-done((bf16[256,768]{1,0:T(8,128)(2,1)S(1)}, bf16[256,768]{1,0:T(8,128)(2,1)S(1)}, u32[]{:S(2)}, u32[]{:S(2)}) %collective-permute-start.8) | collective-permute-done | bytes 393248 | tf_op jit(solution)/shard_map/ppermute | solution.py:38
  114.9 1.3 %feature_grads.1 = (bf16[400,256]{1,0:T(8,128)(2,1)}, bf16[256,512]{1,0:T(8,128)(2,1)}) custom-call(s32[1]{0:T(128)} %bitcast.member_ref, bf16[64,768]{1,0:T(8,128)(2,1)S(1)} %get-tuple-element.37.own_ref, bf16[64,768]{1,0:T(8,128)(2,1)S(1)} %collective-permute-done.6.high_ref, bf16[128,768]{1,0:T(8,128)(2,1)S(1)} %collective-permute-done.7.low_ref, ...), custom_call_target="tpu_custom_call" | custom-call | flops 358612992 | bytes 4000000 | tf_op jit(solution)/shard_map/feature_grads/pallas_call | solution.py:48
  116.1 4.8 %all-to-all-done.5.blocks_ref = bf16[16,48,256]{2,1,0:T(8,128)(2,1)S(1)} async-done(((bf16[16,48,256]{2,1,0:T(8,128)(2,1)}), bf16[16,48,256]{2,1,0:T(8,128)(2,1)S(1)}, u32[]{:S(2)}, u32[]{:S(2)}) %all-to-all-start.5) | async-done | bytes 393248 | tf_op jit(solution)/shard_map/all_to_all | solution.py:273
  (38 shorter events, 4.2 us)
Async XLA Ops:
  3.7 9.5 %copy-start.2 = (bf16[912,256]{1,0:T(8,128)(2,1)S(1)}, bf16[912,256]{1,0:T(8,128)(2,1)}, u32[]{:S(2)}) copy-start(bf16[912,256]{1,0:T(8,128)(2,1)} %get-tuple-element.33.refs_0_) | copy-start | bytes 1400836
  3.7 20.5 %all-to-all-start = ((bf16[8,64,768]{2,1,0:T(8,128)(2,1)}), bf16[8,64,768]{2,1,0:T(8,128)(2,1)S(1)}, u32[]{:S(2)}, u32[]{:S(2)}) async-start(bf16[8,64,768]{2,1,0:T(8,128)(2,1)} %get-tuple-element.26), calls=%async_computation | async-start | bytes 1572864 | tf_op jit(solution)/shard_map/all_to_all | solution.py:190
  13.2 22.8 %collective-permute-start.1 = (bf16[912,256]{1,0:T(8,128)(2,1)S(1)}, bf16[912,256]{1,0:T(8,128)(2,1)S(1)}, u32[]{:S(2)}, u32[]{:S(2)}) collective-permute-start(bf16[912,256]{1,0:T(8,128)(2,1)S(1)} %copy-done.2), channel_id=1, source_target_pairs={{0,448},{64,128},{128,64},{192,256},{256,192},{320,384},{384,320},... | collective-permute-start | bytes 1400840 | tf_op jit(solution)/shard_map/ppermute | solution.py:34
  24.6 11.4 %collective-permute-start = (bf16[32,768]{1,0:T(8,128)(2,1)S(1)}, bf16[32,768]{1,0:T(8,128)(2,1)S(1)}, u32[]{:S(2)}, u32[]{:S(2)}) collective-permute-start(bf16[32,768]{1,0:T(8,128)(2,1)S(1)} %get-tuple-element.52), channel_id=1, source_target_pairs={{0,8},{8,16},{16,24},{24,32},{32,40},{40,48},{48,56},{56,64},{64,7... | collective-permute-start | bytes 147464 | tf_op jit(solution)/shard_map/ppermute | solution.py:24
  28.6 20.2 %copy-start.3 = (s32[256]{0:T(256)S(1)}, s32[256]{0:T(256)}, u32[]{:S(2)}) copy-start(s32[256]{0:T(256)} %param.11) | copy-start | bytes 3076
  28.6 20.2 %all-to-all-start.1 = ((bf16[8,32,768]{2,1,0:T(8,128)(2,1)}), bf16[8,32,768]{2,1,0:T(8,128)(2,1)S(1)}, u32[]{:S(2)}, u32[]{:S(2)}) async-start(bf16[8,32,768]{2,1,0:T(8,128)(2,1)} %broadcast_in_dim.14), calls=%async_computation.1 | async-start | bytes 786432 | tf_op jit(solution)/shard_map/all_to_all | solution.py:207
  36.0 12.7 %collective-permute-start.2 = (bf16[64,768]{1,0:T(8,128)(2,1)S(1)}, bf16[64,768]{1,0:T(8,128)(2,1)S(1)}, u32[]{:S(2)}, u32[]{:S(2)}) collective-permute-start(bf16[64,768]{1,0:T(8,128)(2,1)S(1)} %pad_maximum_fusion.2), channel_id=1, source_target_pairs={{0,16},{8,24},{16,32},{24,40},{32,48},{40,56},{48,64},{56,72},{64,... | collective-permute-start | bytes 294920 | tf_op jit(solution)/shard_map/ppermute | solution.py:24
  38.1 29.1 %collective-permute-start.3 = (bf16[912,256]{1,0:T(8,128)(2,1)S(1)}, bf16[912,256]{1,0:T(8,128)(2,1)S(1)}, u32[]{:S(2)}, u32[]{:S(2)}) collective-permute-start(bf16[912,256]{1,0:T(8,128)(2,1)S(1)} %copy-done.2), channel_id=1, source_target_pairs={{0,128},{64,448},{128,256},{192,64},{256,384},{320,192},{384,0},{4... | collective-permute-start | bytes 1400840 | tf_op jit(solution)/shard_map/ppermute | solution.py:34
  49.3 11.8 %collective-permute-start.4 = (bf16[64,768]{1,0:T(8,128)(2,1)S(1)}, bf16[64,768]{1,0:T(8,128)(2,1)S(1)}, u32[]{:S(2)}, u32[]{:S(2)}) collective-permute-start(bf16[64,768]{1,0:T(8,128)(2,1)S(1)} %slice.30), channel_id=1, source_target_pairs={{0,496},{8,504},{16,0},{24,8},{32,16},{40,24},{48,32},{56,40},{64,... | collective-permute-start | bytes 294920 | tf_op jit(solution)/shard_map/ppermute | solution.py:24
  56.4 11.7 %all-to-all-start.2 = ((bf16[8,32,768]{2,1,0:T(8,128)(2,1)}), bf16[8,32,768]{2,1,0:T(8,128)(2,1)S(1)}, u32[]{:S(2)}, u32[]{:S(2)}) async-start(bf16[8,32,768]{2,1,0:T(8,128)(2,1)} %bitcast.5), calls=%async_computation.2 | async-start | bytes 786432 | tf_op jit(solution)/shard_map/all_to_all | solution.py:223
  61.2 7.8 %collective-permute-start.5 = (bf16[32,768]{1,0:T(8,128)(2,1)S(1)}, bf16[32,768]{1,0:T(8,128)(2,1)S(1)}, u32[]{:S(2)}, u32[]{:S(2)}) collective-permute-start(bf16[32,768]{1,0:T(8,128)(2,1)S(1)} %slice.31), channel_id=1, source_target_pairs={{0,504},{8,0},{16,8},{24,16},{32,24},{40,32},{48,40},{56,48},{64,5... | collective-permute-start | bytes 147464 | tf_op jit(solution)/shard_map/ppermute | solution.py:24
  70.0 13.9 %all-to-all-start.3 = ((bf16[8,32,384]{2,1,0:T(8,128)(2,1)}), bf16[8,32,384]{2,1,0:T(8,128)(2,1)S(1)}, u32[]{:S(2)}, u32[]{:S(2)}) async-start(bf16[8,32,384]{2,1,0:T(8,128)(2,1)} %get-tuple-element.35), calls=%async_computation.3 | async-start | bytes 393216 | tf_op jit(solution)/shard_map/all_to_all | solution.py:239
  74.0 8.0 %collective-permute-start.6 = (bf16[64,768]{1,0:T(8,128)(2,1)S(1)}, bf16[64,768]{1,0:T(8,128)(2,1)S(1)}, u32[]{:S(2)}, u32[]{:S(2)}) collective-permute-start(bf16[64,768]{1,0:T(8,128)(2,1)S(1)} %get-tuple-element.37.own_ref), channel_id=1, source_target_pairs={{0,4},{4,0},{1,5},{5,1},{2,6},{6,2},{3,7},{7,3},{8,12},{12,8},{9,1... | collective-permute-start | bytes 294920 | tf_op jit(solution)/shard_map/ppermute | solution.py:38
  84.7 10.4 %all-to-all-start.4 = ((bf16[4,128,384]{2,1,0:T(8,128)(2,1)}), bf16[4,128,384]{2,1,0:T(8,128)(2,1)S(1)}, u32[]{:S(2)}, u32[]{:S(2)}) async-start(bf16[4,128,384]{2,1,0:T(8,128)(2,1)} %broadcast_in_dim.15), calls=%async_computation.4 | async-start | bytes 786432 | tf_op jit(solution)/shard_map/all_to_all | solution.py:252
  89.8 14.0 %collective-permute-start.10 = (bf16[912,256]{1,0:T(8,128)(2,1)S(1)}, bf16[912,256]{1,0:T(8,128)(2,1)S(1)}, u32[]{:S(2)}, u32[]{:S(2)}) collective-permute-start(bf16[912,256]{1,0:T(8,128)(2,1)S(1)} %collective-permute-done.1.refs_1_), channel_id=1, source_target_pairs={{0,128},{64,448},{128,256},{192,64},{256,384},{320,192},{384,0},{4... | collective-permute-start | bytes 1400840 | tf_op jit(solution)/shard_map/ppermute | solution.py:34
  95.1 8.7 %collective-permute-start.9 = (bf16[4,128,384]{2,1,0:T(8,128)(2,1)S(1)}, bf16[4,128,384]{2,1,0:T(8,128)(2,1)S(1)}, u32[]{:S(2)}, u32[]{:S(2)}) collective-permute-start(bf16[4,128,384]{2,1,0:T(8,128)(2,1)S(1)} %all-to-all-done.4.mine_ref), channel_id=1, source_target_pairs={{0,1},{1,0},{2,3},{3,2},{4,5},{5,4},{6,7},{7,6},{8,9},{9,8},{10,11... | collective-permute-start | bytes 1179656 | tf_op jit(solution)/shard_map/ppermute | solution.py:38
  97.0 14.2 %collective-permute-start.7 = (bf16[128,768]{1,0:T(8,128)(2,1)S(1)}, bf16[128,768]{1,0:T(8,128)(2,1)S(1)}, u32[]{:S(2)}, u32[]{:S(2)}) collective-permute-start(bf16[128,768]{1,0:T(8,128)(2,1)S(1)} %pad_maximum_fusion.1), channel_id=1, source_target_pairs={{0,2},{2,0},{1,3},{3,1},{4,6},{6,4},{5,7},{7,5},{8,10},{10,8},{9,1... | collective-permute-start | bytes 589832 | tf_op jit(solution)/shard_map/ppermute | solution.py:38
  106.9 8.0 %copy-start = (bf16[512,768]{1,0:T(8,128)(2,1)S(1)}, bf16[512,768]{1,0:T(8,128)(2,1)}, u32[]{:S(2)}) copy-start(bf16[512,768]{1,0:T(8,128)(2,1)} %txt_proj_ref.3) | copy-start | bytes 2359300
  106.9 8.0 %copy-start.1 = (bf16[400,768]{1,0:T(8,128)(2,1)S(1)}, bf16[400,768]{1,0:T(8,128)(2,1)}, u32[]{:S(2)}) copy-start(bf16[400,768]{1,0:T(8,128)(2,1)} %img_proj_ref.3) | copy-start | bytes 1843204
  106.9 14.0 %all-to-all-start.5 = ((bf16[16,48,256]{2,1,0:T(8,128)(2,1)}), bf16[16,48,256]{2,1,0:T(8,128)(2,1)S(1)}, u32[]{:S(2)}, u32[]{:S(2)}) async-start(bf16[16,48,256]{2,1,0:T(8,128)(2,1)} %project_grads.1), calls=%async_computation.5 | async-start | bytes 786432 | tf_op jit(solution)/shard_map/all_to_all | solution.py:273
  111.2 3.6 %collective-permute-start.8 = (bf16[256,768]{1,0:T(8,128)(2,1)S(1)}, bf16[256,768]{1,0:T(8,128)(2,1)S(1)}, u32[]{:S(2)}, u32[]{:S(2)}) collective-permute-start(bf16[256,768]{1,0:T(8,128)(2,1)S(1)} %pad_maximum_fusion), channel_id=1, source_target_pairs={{0,1},{1,0},{2,3},{3,2},{4,5},{5,4},{6,7},{7,6},{8,9},{9,8},{10,11... | collective-permute-start | bytes 1179656 | tf_op jit(solution)/shard_map/ppermute | solution.py:38

commit v9 on v8

--- a/solution.py
+++ b/solution.py
@@ -103,22 +103,25 @@
     d_all = far[0].shape[0]
     d_txt = 2 * HALF
     d_img = d_all - d_txt
-    sums = [None] * 3
-    for step, copy in enumerate(copies):
-        line_ref = lines.at[step]
+    for step in range(len(copies)):
         for chip in range(chips):
             for ref, core in ((mine_ref, core_ref[0]), (other_ref, 1 - core_ref[0])):
                 row = pl.multiple_of((2 * chip + core) * share, share)
                 cols_ref[step, pl.ds(row, share)] = ref[chip, step * share : (step + 1) * share]
-        cols = cols_ref[step].T
+    cols = jnp.concatenate([cols_ref[step].T for step in range(len(copies))], axis=1)
+    img_cols, txt_cols = cols[: wide // 2], cols[wide // 2 :]
+    for copy in copies:
         copy.wait()
-        img_cols, txt_cols = cols[: wide // 2], cols[wide // 2 :]
-        terms = [
-            jnp.dot(txt_cols, line_ref[:HALF], preferred_element_type=F32),
-            jnp.dot(txt_cols, line_ref[HALF:d_txt], preferred_element_type=F32),
-            lax.dot_general(img_cols, line_ref[d_txt:], ACROSS, preferred_element_type=F32),
-        ]
-        sums = [term if total is None else total + term for total, term in zip(sums, terms)]
+    sums = [
+        jnp.dot(
+            txt_cols,
+            lines[:, half * HALF : (half + 1) * HALF].reshape(cols.shape[1], HALF),
+            preferred_element_type=F32,
+        )
+        for half in range(2)
+    ]
+    img_lines = jnp.concatenate([lines[step, d_txt:] for step in range(len(copies))], axis=1)
+    sums.append(lax.dot_general(img_cols, img_lines, ACROSS, preferred_element_type=F32))
     peers, height, _ = out_ref.shape
     take = height // 4
     for peer in range(peers):
@@ -188,7 +191,7 @@
     )
     second = along_y(pack, 1)
     parts = lax.all_to_all(parts, X, 0, 0, tiled=True)
-    offsets = jnp.arange(STEPS, dtype=jnp.int32)
+    offsets = jnp.array([0, 2, 1, 3], jnp.int32)
     col_ids = (
         jnp.mod(anchor - offsets, blocks)[:, None] * rows
         + member * share
@@ -210,7 +213,7 @@
     pair, second, held = lax.optimization_barrier((pair, second, pack))
     far = shifted(pair, 2)
     third = along_y(held, 2)
-    cols = jnp.concatenate([pair, far])
+    cols = jnp.concatenate([txt_own, far[:share], near, far[share:]])
     polarity = jnp.where(labels[:, None] == col_ids[None, :], 1.0, -1.0).astype(F32)
     logits = (
         scale_value * lax.dot_general(img_all, cols, ACROSS, preferred_element_type=F32)
@@ -219,11 +222,11 @@
     weights = (-scale_value * polarity * jax.nn.sigmoid(-polarity * logits) / rows).astype(BF16)
     txt_terms = lax.dot_general(weights, img_all, DOWN, preferred_element_type=F32)
     img_terms = jnp.dot(weights, cols, preferred_element_type=F32).astype(BF16)
-    back = shifted(txt_terms[2 * share :].astype(BF16), -2)
+    back = shifted(txt_terms[2 * share :].astype(BF16), -1)
     img_terms = lax.all_to_all(img_terms.reshape(groups, share, embed), X, 0, 0, tiled=True)
     img_terms, third = lax.optimization_barrier((img_terms, third))
     two = txt_terms[: 2 * share] + back.astype(F32)
-    last = shifted(two[share:].astype(BF16), -1)
+    last = shifted(two[share:].astype(BF16), -2)
     wide = embed // quad
     grad_summed, by_cols = call(
         row_grads_kernel,

time: 124 us -> 121 us (0.976)
  starting transfers between devices: 67.6 us -> 63.4 us
  waiting for transfers between devices: 38.9 us -> 41 us
    ppermute x4, starting transfers between devices: 16.2 us -> 11.7 us  [shifted(): return lax.ppermute(value, DP, pairs)]
    all_to_all x1, waiting for transfers between devices: 0.75 us -> 3.4 us  [on_device(): lax.all_to_all(img_terms.reshape(groups, share, embed), X, 0, 0, tiled=True)]
where the time goes in v9:
time: 121 us; the launch traced here: 119 us
  starting transfers between devices  63.4 us (52%)
  waiting for transfers between devices  41 us (34%)
  Pallas kernels  8.93 us (7%)
  between operations  2.24 us (2%)
  local copies, waits for them, and re-layouts  1.74 us (1%)
  matrix products  1.52 us (1%)
    ppermute x4, starting transfers between devices, shifted(): return lax.ppermute(value, DP, pairs)  11.7 us
    all_to_all x1, starting transfers between devices, on_device(): parts = lax.all_to_all(parts, X, 0, 0, tiled=True)  9.46 us
    ppermute x4, starting transfers between devices, swapped(): return lax.ppermute(value, axis, [(0, 1), (1, 0)])  9.11 us
    all_to_all x1, waiting for transfers between devices, on_device(): parts = lax.all_to_all(parts, X, 0, 0, tiled=True)  8.94 us
    pallas_call x5, Pallas kernels, call(): pl.pallas_call(kernel, out_shape=out_shape, in_specs=[pl.BlockSpec(memory...  8.93 us
    ppermute x4, waiting for transfers between devices, shifted(): return lax.ppermute(value, DP, pairs)  8.32 us
    ppermute x3, starting transfers between devices, along_y(): return lax.ppermute(value, Y, pairs)  7.93 us
    ppermute x4, waiting for transfers between devices, swapped(): return lax.ppermute(value, axis, [(0, 1), (1, 0)])  6.32 us
  transfers between devices with their start and end apart: 17, of which 11 were waited for; matrix products, arithmetic and copies ran while one was open for 2% of the time, Pallas kernels for 4%

profile of v9, /device:TPU:6, one launch (start us, length us, event | category | flops | bytes accessed | tf_op | source)
XLA Modules:
  0.0 119.2 jit_solution(16078151457192794915)
XLA Ops:
  0.6 3.1 %project.1 = (bf16[8,64,768]{2,1,0:T(8,128)(2,1)}, bf16[912,256]{1,0:T(8,128)(2,1)}) custom-call(bf16[400,256]{1,0:T(8,128)(2,1)} %bitcast.27, bf16[256,512]{1,0:T(8,128)(2,1)} %txt_ref.1, bf16[400,768]{1,0:T(8,128)(2,1)} %img_proj_ref.3, bf16[512,768]{1,0:T(8,128)(2,1)} %txt_proj_ref.3), custom_call_target="tpu_custom_call" | custom-call | flops 358612992 | bytes 4000000 | tf_op jit(solution)/shard_map/project/pallas_call | solution.py:48
  3.7 9.5 %all-to-all-start = ((bf16[8,64,768]{2,1,0:T(8,128)(2,1)}), bf16[8,64,768]{2,1,0:T(8,128)(2,1)S(1)}, u32[]{:S(2)}, u32[]{:S(2)}) async-start(bf16[8,64,768]{2,1,0:T(8,128)(2,1)} %get-tuple-element.26), calls=%async_computation | async-start | bytes 1572864 | tf_op jit(solution)/shard_map/all_to_all | solution.py:193
  13.2 1.9 %collective-permute-start.1 = (bf16[912,256]{1,0:T(8,128)(2,1)S(1)}, bf16[912,256]{1,0:T(8,128)(2,1)S(1)}, u32[]{:S(2)}, u32[]{:S(2)}) collective-permute-start(bf16[912,256]{1,0:T(8,128)(2,1)S(1)} %copy-done.2), channel_id=1, source_target_pairs={{0,448},{64,128},{128,64},{192,256},{256,192},{320,384},{384,320},... | collective-permute-start | bytes 1400840 | tf_op jit(solution)/shard_map/ppermute | solution.py:34
  15.3 8.9 %all-to-all-done = bf16[8,64,768]{2,1,0:T(8,128)(2,1)S(1)} async-done(((bf16[8,64,768]{2,1,0:T(8,128)(2,1)}), bf16[8,64,768]{2,1,0:T(8,128)(2,1)S(1)}, u32[]{:S(2)}, u32[]{:S(2)}) %all-to-all-start) | async-done | bytes 786464 | tf_op jit(solution)/shard_map/all_to_all | solution.py:193
  24.6 1.9 %collective-permute-start = (bf16[32,768]{1,0:T(8,128)(2,1)S(1)}, bf16[32,768]{1,0:T(8,128)(2,1)S(1)}, u32[]{:S(2)}, u32[]{:S(2)}) collective-permute-start(bf16[32,768]{1,0:T(8,128)(2,1)S(1)} %get-tuple-element.54), channel_id=1, source_target_pairs={{0,8},{8,16},{16,24},{24,32},{32,40},{40,48},{48,56},{56,64},{64,7... | collective-permute-start | bytes 147464 | tf_op jit(solution)/shard_map/ppermute | solution.py:24
  27.3 5.5 %all-to-all-start.1 = ((bf16[8,32,768]{2,1,0:T(8,128)(2,1)}), bf16[8,32,768]{2,1,0:T(8,128)(2,1)S(1)}, u32[]{:S(2)}, u32[]{:S(2)}) async-start(bf16[8,32,768]{2,1,0:T(8,128)(2,1)} %broadcast_in_dim.14), calls=%async_computation.1 | async-start | bytes 786432 | tf_op jit(solution)/shard_map/all_to_all | solution.py:210
  32.8 3.2 %collective-permute-done = bf16[32,768]{1,0:T(8,128)(2,1)S(1)} collective-permute-done((bf16[32,768]{1,0:T(8,128)(2,1)S(1)}, bf16[32,768]{1,0:T(8,128)(2,1)S(1)}, u32[]{:S(2)}, u32[]{:S(2)}) %collective-permute-start) | collective-permute-done | bytes 49184 | tf_op jit(solution)/shard_map/ppermute | solution.py:24
  36.0 1.9 %collective-permute-start.2 = (bf16[64,768]{1,0:T(8,128)(2,1)S(1)}, bf16[64,768]{1,0:T(8,128)(2,1)S(1)}, u32[]{:S(2)}, u32[]{:S(2)}) collective-permute-start(bf16[64,768]{1,0:T(8,128)(2,1)S(1)} %pad_maximum_fusion.3), channel_id=1, source_target_pairs={{0,16},{8,24},{16,32},{24,40},{32,48},{40,56},{48,64},{56,72},{64,... | collective-permute-start | bytes 294920 | tf_op jit(solution)/shard_map/ppermute | solution.py:24
  39.2 3.3 %collective-permute-start.3 = (bf16[912,256]{1,0:T(8,128)(2,1)S(1)}, bf16[912,256]{1,0:T(8,128)(2,1)S(1)}, u32[]{:S(2)}, u32[]{:S(2)}) collective-permute-start(bf16[912,256]{1,0:T(8,128)(2,1)S(1)} %copy-done.2), channel_id=1, source_target_pairs={{0,128},{64,448},{128,256},{192,64},{256,384},{320,192},{384,0},{4... | collective-permute-start | bytes 1400840 | tf_op jit(solution)/shard_map/ppermute | solution.py:34
  42.5 4.9 %collective-permute-done.2 = bf16[64,768]{1,0:T(8,128)(2,1)S(1)} collective-permute-done((bf16[64,768]{1,0:T(8,128)(2,1)S(1)}, bf16[64,768]{1,0:T(8,128)(2,1)S(1)}, u32[]{:S(2)}, u32[]{:S(2)}) %collective-permute-start.2) | collective-permute-done | bytes 98336 | tf_op jit(solution)/shard_map/ppermute | solution.py:24
  48.0 4.5 %collective-permute-start.4 = (bf16[64,768]{1,0:T(8,128)(2,1)S(1)}, bf16[64,768]{1,0:T(8,128)(2,1)S(1)}, u32[]{:S(2)}, u32[]{:S(2)}) collective-permute-start(bf16[64,768]{1,0:T(8,128)(2,1)S(1)} %slice.40), channel_id=1, source_target_pairs={{0,504},{8,0},{16,8},{24,16},{32,24},{40,32},{48,40},{56,48},{64,5... | collective-permute-start | bytes 294920 | tf_op jit(solution)/shard_map/ppermute | solution.py:24
  52.5 1.0 convolution_convert_fusion
  53.5 4.8 %all-to-all-start.2 = ((bf16[8,32,768]{2,1,0:T(8,128)(2,1)}), bf16[8,32,768]{2,1,0:T(8,128)(2,1)S(1)}, u32[]{:S(2)}, u32[]{:S(2)}) async-start(bf16[8,32,768]{2,1,0:T(8,128)(2,1)} %bitcast.5), calls=%async_computation.2 | async-start | bytes 786432 | tf_op jit(solution)/shard_map/all_to_all | solution.py:226
  58.3 3.4 %collective-permute-start.5 = (bf16[32,768]{1,0:T(8,128)(2,1)S(1)}, bf16[32,768]{1,0:T(8,128)(2,1)S(1)}, u32[]{:S(2)}, u32[]{:S(2)}) collective-permute-start(bf16[32,768]{1,0:T(8,128)(2,1)S(1)} %slice.41), channel_id=1, source_target_pairs={{0,496},{8,504},{16,0},{24,8},{32,16},{40,24},{48,32},{56,40},{64,... | collective-permute-start | bytes 147464 | tf_op jit(solution)/shard_map/ppermute | solution.py:24
  61.7 3.4 %all-to-all-done.2.img_ref = bf16[8,32,768]{2,1,0:T(8,128)(2,1)S(1)} async-done(((bf16[8,32,768]{2,1,0:T(8,128)(2,1)}), bf16[8,32,768]{2,1,0:T(8,128)(2,1)S(1)}, u32[]{:S(2)}, u32[]{:S(2)}) %all-to-all-start.2) | async-done | bytes 393248 | tf_op jit(solution)/shard_map/all_to_all | solution.py:226
  65.4 1.0 row_grads.1
  66.4 4.3 %all-to-all-start.3 = ((bf16[8,32,384]{2,1,0:T(8,128)(2,1)}), bf16[8,32,384]{2,1,0:T(8,128)(2,1)S(1)}, u32[]{:S(2)}, u32[]{:S(2)}) async-start(bf16[8,32,384]{2,1,0:T(8,128)(2,1)} %get-tuple-element.35), calls=%async_computation.3 | async-start | bytes 393216 | tf_op jit(solution)/shard_map/all_to_all | solution.py:242
  70.7 3.4 %collective-permute-start.6 = (bf16[64,768]{1,0:T(8,128)(2,1)S(1)}, bf16[64,768]{1,0:T(8,128)(2,1)S(1)}, u32[]{:S(2)}, u32[]{:S(2)}) collective-permute-start(bf16[64,768]{1,0:T(8,128)(2,1)S(1)} %get-tuple-element.37.own_ref), channel_id=1, source_target_pairs={{0,4},{4,0},{1,5},{5,1},{2,6},{6,2},{3,7},{7,3},{8,12},{12,8},{9,1... | collective-permute-start | bytes 294920 | tf_op jit(solution)/shard_map/ppermute | solution.py:38
  74.0 4.6 %collective-permute-done.6.high_ref = bf16[64,768]{1,0:T(8,128)(2,1)S(1)} collective-permute-done((bf16[64,768]{1,0:T(8,128)(2,1)S(1)}, bf16[64,768]{1,0:T(8,128)(2,1)S(1)}, u32[]{:S(2)}, u32[]{:S(2)}) %collective-permute-start.6) | collective-permute-done | bytes 98336 | tf_op jit(solution)/shard_map/ppermute | solution.py:38
  78.7 1.8 %all-to-all-done.3 = bf16[8,32,384]{2,1,0:T(8,128)(2,1)S(1)} async-done(((bf16[8,32,384]{2,1,0:T(8,128)(2,1)}), bf16[8,32,384]{2,1,0:T(8,128)(2,1)S(1)}, u32[]{:S(2)}, u32[]{:S(2)}) %all-to-all-start.3) | async-done | bytes 196640 | tf_op jit(solution)/shard_map/all_to_all | solution.py:242
  81.3 5.1 %all-to-all-start.4 = ((bf16[4,128,384]{2,1,0:T(8,128)(2,1)}), bf16[4,128,384]{2,1,0:T(8,128)(2,1)S(1)}, u32[]{:S(2)}, u32[]{:S(2)}) async-start(bf16[4,128,384]{2,1,0:T(8,128)(2,1)} %broadcast_in_dim.15), calls=%async_computation.4 | async-start | bytes 786432 | tf_op jit(solution)/shard_map/all_to_all | solution.py:255
  86.4 2.7 %collective-permute-start.10 = (bf16[912,256]{1,0:T(8,128)(2,1)S(1)}, bf16[912,256]{1,0:T(8,128)(2,1)S(1)}, u32[]{:S(2)}, u32[]{:S(2)}) collective-permute-start(bf16[912,256]{1,0:T(8,128)(2,1)S(1)} %collective-permute-done.1.refs_1_), channel_id=1, source_target_pairs={{0,128},{64,448},{128,256},{192,64},{256,384},{320,192},{384,0},{4... | collective-permute-start | bytes 1400840 | tf_op jit(solution)/shard_map/ppermute | solution.py:34
  89.1 2.6 %all-to-all-done.4.mine_ref = bf16[4,128,384]{2,1,0:T(8,128)(2,1)S(1)} async-done(((bf16[4,128,384]{2,1,0:T(8,128)(2,1)}), bf16[4,128,384]{2,1,0:T(8,128)(2,1)S(1)}, u32[]{:S(2)}, u32[]{:S(2)}) %all-to-all-start.4) | async-done | bytes 393248 | tf_op jit(solution)/shard_map/all_to_all | solution.py:255
  91.7 1.9 %collective-permute-start.9 = (bf16[4,128,384]{2,1,0:T(8,128)(2,1)S(1)}, bf16[4,128,384]{2,1,0:T(8,128)(2,1)S(1)}, u32[]{:S(2)}, u32[]{:S(2)}) collective-permute-start(bf16[4,128,384]{2,1,0:T(8,128)(2,1)S(1)} %all-to-all-done.4.mine_ref), channel_id=1, source_target_pairs={{0,1},{1,0},{2,3},{3,2},{4,5},{5,4},{6,7},{7,6},{8,9},{9,8},{10,11... | collective-permute-start | bytes 1179656 | tf_op jit(solution)/shard_map/ppermute | solution.py:38
  93.6 1.9 %collective-permute-start.7 = (bf16[128,768]{1,0:T(8,128)(2,1)S(1)}, bf16[128,768]{1,0:T(8,128)(2,1)S(1)}, u32[]{:S(2)}, u32[]{:S(2)}) collective-permute-start(bf16[128,768]{1,0:T(8,128)(2,1)S(1)} %pad_maximum_fusion.2), channel_id=1, source_target_pairs={{0,2},{2,0},{1,3},{3,1},{4,6},{6,4},{5,7},{7,5},{8,10},{10,8},{9,1... | collective-permute-start | bytes 589832 | tf_op jit(solution)/shard_map/ppermute | solution.py:38
  95.6 4.8 %collective-permute-done.10.refs_3_ = bf16[912,256]{1,0:T(8,128)(2,1)S(1)} collective-permute-done((bf16[912,256]{1,0:T(8,128)(2,1)S(1)}, bf16[912,256]{1,0:T(8,128)(2,1)S(1)}, u32[]{:S(2)}, u32[]{:S(2)}) %collective-permute-start.10) | collective-permute-done | bytes 466976 | tf_op jit(solution)/shard_map/ppermute | solution.py:34
  100.4 3.0 %project_grads.1 = bf16[16,48,256]{2,1,0:T(8,128)(2,1)} custom-call(s32[1]{0:T(128)} %bitcast.7.core_ref, bf16[4,128,384]{2,1,0:T(8,128)(2,1)S(1)} %all-to-all-done.4.mine_ref, bf16[4,128,384]{2,1,0:T(8,128)(2,1)S(1)} %collective-permute-done.9.other_ref, bf16[912,256]{1,0:T(8,128)(2,1)S(1)} %copy-done.2, ...), custom_call_target="tpu_custom_call" | custom-call | flops 358612992 | bytes 4000000 | tf_op jit(solution)/shard_map/project_grads/pallas_call | solution.py:48
  103.4 5.5 %all-to-all-start.5 = ((bf16[16,48,256]{2,1,0:T(8,128)(2,1)}), bf16[16,48,256]{2,1,0:T(8,128)(2,1)S(1)}, u32[]{:S(2)}, u32[]{:S(2)}) async-start(bf16[16,48,256]{2,1,0:T(8,128)(2,1)} %project_grads.1), calls=%async_computation.5 | async-start | bytes 786432 | tf_op jit(solution)/shard_map/all_to_all | solution.py:276
  108.9 1.9 %collective-permute-start.8 = (bf16[256,768]{1,0:T(8,128)(2,1)S(1)}, bf16[256,768]{1,0:T(8,128)(2,1)S(1)}, u32[]{:S(2)}, u32[]{:S(2)}) collective-permute-start(bf16[256,768]{1,0:T(8,128)(2,1)S(1)} %pad_maximum_fusion), channel_id=1, source_target_pairs={{0,1},{1,0},{2,3},{3,2},{4,5},{5,4},{6,7},{7,6},{8,9},{9,8},{10,11... | collective-permute-start | bytes 1179656 | tf_op jit(solution)/shard_map/ppermute | solution.py:38
  110.8 1.7 %collective-permute-done.8.core_ref = bf16[256,768]{1,0:T(8,128)(2,1)S(1)} collective-permute-done((bf16[256,768]{1,0:T(8,128)(2,1)S(1)}, bf16[256,768]{1,0:T(8,128)(2,1)S(1)}, u32[]{:S(2)}, u32[]{:S(2)}) %collective-permute-start.8) | collective-permute-done | bytes 393248 | tf_op jit(solution)/shard_map/ppermute | solution.py:38
  112.5 1.2 %feature_grads.1 = (bf16[400,256]{1,0:T(8,128)(2,1)}, bf16[256,512]{1,0:T(8,128)(2,1)}) custom-call(s32[1]{0:T(128)} %bitcast.member_ref, bf16[64,768]{1,0:T(8,128)(2,1)S(1)} %get-tuple-element.37.own_ref, bf16[64,768]{1,0:T(8,128)(2,1)S(1)} %collective-permute-done.6.high_ref, bf16[128,768]{1,0:T(8,128)(2,1)S(1)} %collective-permute-done.7.low_ref, ...), custom_call_target="tpu_custom_call" | custom-call | flops 358612992 | bytes 4000000 | tf_op jit(solution)/shard_map/feature_grads/pallas_call | solution.py:48
  113.8 4.8 %all-to-all-done.5.blocks_ref = bf16[16,48,256]{2,1,0:T(8,128)(2,1)S(1)} async-done(((bf16[16,48,256]{2,1,0:T(8,128)(2,1)}), bf16[16,48,256]{2,1,0:T(8,128)(2,1)S(1)}, u32[]{:S(2)}, u32[]{:S(2)}) %all-to-all-start.5) | async-done | bytes 393248 | tf_op jit(solution)/shard_map/all_to_all | solution.py:276
  (39 shorter events, 3.7 us)
Async XLA Ops:
  3.7 9.5 %copy-start.2 = (bf16[912,256]{1,0:T(8,128)(2,1)S(1)}, bf16[912,256]{1,0:T(8,128)(2,1)}, u32[]{:S(2)}) copy-start(bf16[912,256]{1,0:T(8,128)(2,1)} %get-tuple-element.33.refs_0_) | copy-start | bytes 1400836
  3.7 11.4 %copy-start.3 = (s32[4]{0:T(128)S(1)}, s32[4]{0:T(128)}, u32[]{:S(2)}) copy-start(s32[4]{0:T(128)} %constant.81) | copy-start | bytes 52
  3.7 20.5 %all-to-all-start = ((bf16[8,64,768]{2,1,0:T(8,128)(2,1)}), bf16[8,64,768]{2,1,0:T(8,128)(2,1)S(1)}, u32[]{:S(2)}, u32[]{:S(2)}) async-start(bf16[8,64,768]{2,1,0:T(8,128)(2,1)} %get-tuple-element.26), calls=%async_computation | async-start | bytes 1572864 | tf_op jit(solution)/shard_map/all_to_all | solution.py:193
  13.2 22.8 %collective-permute-start.1 = (bf16[912,256]{1,0:T(8,128)(2,1)S(1)}, bf16[912,256]{1,0:T(8,128)(2,1)S(1)}, u32[]{:S(2)}, u32[]{:S(2)}) collective-permute-start(bf16[912,256]{1,0:T(8,128)(2,1)S(1)} %copy-done.2), channel_id=1, source_target_pairs={{0,448},{64,128},{128,64},{192,256},{256,192},{320,384},{384,320},... | collective-permute-start | bytes 1400840 | tf_op jit(solution)/shard_map/ppermute | solution.py:34
  24.6 11.4 %collective-permute-start = (bf16[32,768]{1,0:T(8,128)(2,1)S(1)}, bf16[32,768]{1,0:T(8,128)(2,1)S(1)}, u32[]{:S(2)}, u32[]{:S(2)}) collective-permute-start(bf16[32,768]{1,0:T(8,128)(2,1)S(1)} %get-tuple-element.54), channel_id=1, source_target_pairs={{0,8},{8,16},{16,24},{24,32},{32,40},{40,48},{48,56},{56,64},{64,7... | collective-permute-start | bytes 147464 | tf_op jit(solution)/shard_map/ppermute | solution.py:24
  26.5 20.9 %copy-start.4 = (s32[256]{0:T(256)S(1)}, s32[256]{0:T(256)}, u32[]{:S(2)}) copy-start(s32[256]{0:T(256)} %param.12) | copy-start | bytes 3076
  27.3 20.1 %all-to-all-start.1 = ((bf16[8,32,768]{2,1,0:T(8,128)(2,1)}), bf16[8,32,768]{2,1,0:T(8,128)(2,1)S(1)}, u32[]{:S(2)}, u32[]{:S(2)}) async-start(bf16[8,32,768]{2,1,0:T(8,128)(2,1)} %broadcast_in_dim.14), calls=%async_computation.1 | async-start | bytes 786432 | tf_op jit(solution)/shard_map/all_to_all | solution.py:210
  36.0 11.4 %collective-permute-start.2 = (bf16[64,768]{1,0:T(8,128)(2,1)S(1)}, bf16[64,768]{1,0:T(8,128)(2,1)S(1)}, u32[]{:S(2)}, u32[]{:S(2)}) collective-permute-start(bf16[64,768]{1,0:T(8,128)(2,1)S(1)} %pad_maximum_fusion.3), channel_id=1, source_target_pairs={{0,16},{8,24},{16,32},{24,40},{32,48},{40,56},{48,64},{56,72},{64,... | collective-permute-start | bytes 294920 | tf_op jit(solution)/shard_map/ppermute | solution.py:24
  39.2 22.5 %collective-permute-start.3 = (bf16[912,256]{1,0:T(8,128)(2,1)S(1)}, bf16[912,256]{1,0:T(8,128)(2,1)S(1)}, u32[]{:S(2)}, u32[]{:S(2)}) collective-permute-start(bf16[912,256]{1,0:T(8,128)(2,1)S(1)} %copy-done.2), channel_id=1, source_target_pairs={{0,128},{64,448},{128,256},{192,64},{256,384},{320,192},{384,0},{4... | collective-permute-start | bytes 1400840 | tf_op jit(solution)/shard_map/ppermute | solution.py:34
  48.0 10.3 %collective-permute-start.4 = (bf16[64,768]{1,0:T(8,128)(2,1)S(1)}, bf16[64,768]{1,0:T(8,128)(2,1)S(1)}, u32[]{:S(2)}, u32[]{:S(2)}) collective-permute-start(bf16[64,768]{1,0:T(8,128)(2,1)S(1)} %slice.40), channel_id=1, source_target_pairs={{0,504},{8,0},{16,8},{24,16},{32,24},{40,32},{48,40},{56,48},{64,5... | collective-permute-start | bytes 294920 | tf_op jit(solution)/shard_map/ppermute | solution.py:24
  53.5 11.7 %all-to-all-start.2 = ((bf16[8,32,768]{2,1,0:T(8,128)(2,1)}), bf16[8,32,768]{2,1,0:T(8,128)(2,1)S(1)}, u32[]{:S(2)}, u32[]{:S(2)}) async-start(bf16[8,32,768]{2,1,0:T(8,128)(2,1)} %bitcast.5), calls=%async_computation.2 | async-start | bytes 786432 | tf_op jit(solution)/shard_map/all_to_all | solution.py:226
  58.3 7.1 %collective-permute-start.5 = (bf16[32,768]{1,0:T(8,128)(2,1)S(1)}, bf16[32,768]{1,0:T(8,128)(2,1)S(1)}, u32[]{:S(2)}, u32[]{:S(2)}) collective-permute-start(bf16[32,768]{1,0:T(8,128)(2,1)S(1)} %slice.41), channel_id=1, source_target_pairs={{0,496},{8,504},{16,0},{24,8},{32,16},{40,24},{48,32},{56,40},{64,... | collective-permute-start | bytes 147464 | tf_op jit(solution)/shard_map/ppermute | solution.py:24
  66.4 14.1 %all-to-all-start.3 = ((bf16[8,32,384]{2,1,0:T(8,128)(2,1)}), bf16[8,32,384]{2,1,0:T(8,128)(2,1)S(1)}, u32[]{:S(2)}, u32[]{:S(2)}) async-start(bf16[8,32,384]{2,1,0:T(8,128)(2,1)} %get-tuple-element.35), calls=%async_computation.3 | async-start | bytes 393216 | tf_op jit(solution)/shard_map/all_to_all | solution.py:242
  70.7 8.0 %collective-permute-start.6 = (bf16[64,768]{1,0:T(8,128)(2,1)S(1)}, bf16[64,768]{1,0:T(8,128)(2,1)S(1)}, u32[]{:S(2)}, u32[]{:S(2)}) collective-permute-start(bf16[64,768]{1,0:T(8,128)(2,1)S(1)} %get-tuple-element.37.own_ref), channel_id=1, source_target_pairs={{0,4},{4,0},{1,5},{5,1},{2,6},{6,2},{3,7},{7,3},{8,12},{12,8},{9,1... | collective-permute-start | bytes 294920 | tf_op jit(solution)/shard_map/ppermute | solution.py:38
  81.3 10.4 %all-to-all-start.4 = ((bf16[4,128,384]{2,1,0:T(8,128)(2,1)}), bf16[4,128,384]{2,1,0:T(8,128)(2,1)S(1)}, u32[]{:S(2)}, u32[]{:S(2)}) async-start(bf16[4,128,384]{2,1,0:T(8,128)(2,1)} %broadcast_in_dim.15), calls=%async_computation.4 | async-start | bytes 786432 | tf_op jit(solution)/shard_map/all_to_all | solution.py:255
  86.4 14.0 %collective-permute-start.10 = (bf16[912,256]{1,0:T(8,128)(2,1)S(1)}, bf16[912,256]{1,0:T(8,128)(2,1)S(1)}, u32[]{:S(2)}, u32[]{:S(2)}) collective-permute-start(bf16[912,256]{1,0:T(8,128)(2,1)S(1)} %collective-permute-done.1.refs_1_), channel_id=1, source_target_pairs={{0,128},{64,448},{128,256},{192,64},{256,384},{320,192},{384,0},{4... | collective-permute-start | bytes 1400840 | tf_op jit(solution)/shard_map/ppermute | solution.py:34
  91.7 8.7 %collective-permute-start.9 = (bf16[4,128,384]{2,1,0:T(8,128)(2,1)S(1)}, bf16[4,128,384]{2,1,0:T(8,128)(2,1)S(1)}, u32[]{:S(2)}, u32[]{:S(2)}) collective-permute-start(bf16[4,128,384]{2,1,0:T(8,128)(2,1)S(1)} %all-to-all-done.4.mine_ref), channel_id=1, source_target_pairs={{0,1},{1,0},{2,3},{3,2},{4,5},{5,4},{6,7},{7,6},{8,9},{9,8},{10,11... | collective-permute-start | bytes 1179656 | tf_op jit(solution)/shard_map/ppermute | solution.py:38
  93.6 15.2 %collective-permute-start.7 = (bf16[128,768]{1,0:T(8,128)(2,1)S(1)}, bf16[128,768]{1,0:T(8,128)(2,1)S(1)}, u32[]{:S(2)}, u32[]{:S(2)}) collective-permute-start(bf16[128,768]{1,0:T(8,128)(2,1)S(1)} %pad_maximum_fusion.2), channel_id=1, source_target_pairs={{0,2},{2,0},{1,3},{3,1},{4,6},{6,4},{5,7},{7,5},{8,10},{10,8},{9,1... | collective-permute-start | bytes 589832 | tf_op jit(solution)/shard_map/ppermute | solution.py:38
  103.4 9.1 %copy-start = (bf16[512,768]{1,0:T(8,128)(2,1)S(1)}, bf16[512,768]{1,0:T(8,128)(2,1)}, u32[]{:S(2)}) copy-start(bf16[512,768]{1,0:T(8,128)(2,1)} %txt_proj_ref.3) | copy-start | bytes 2359300
  103.4 9.1 %copy-start.1 = (bf16[400,768]{1,0:T(8,128)(2,1)S(1)}, bf16[400,768]{1,0:T(8,128)(2,1)}, u32[]{:S(2)}) copy-start(bf16[400,768]{1,0:T(8,128)(2,1)} %img_proj_ref.3) | copy-start | bytes 1843204
  103.4 15.2 %all-to-all-start.5 = ((bf16[16,48,256]{2,1,0:T(8,128)(2,1)}), bf16[16,48,256]{2,1,0:T(8,128)(2,1)S(1)}, u32[]{:S(2)}, u32[]{:S(2)}) async-start(bf16[16,48,256]{2,1,0:T(8,128)(2,1)} %project_grads.1), calls=%async_computation.5 | async-start | bytes 786432 | tf_op jit(solution)/shard_map/all_to_all | solution.py:276
  108.9 3.6 %collective-permute-start.8 = (bf16[256,768]{1,0:T(8,128)(2,1)S(1)}, bf16[256,768]{1,0:T(8,128)(2,1)S(1)}, u32[]{:S(2)}, u32[]{:S(2)}) collective-permute-start(bf16[256,768]{1,0:T(8,128)(2,1)S(1)} %pad_maximum_fusion), channel_id=1, source_target_pairs={{0,1},{1,0},{2,3},{3,2},{4,5},{5,4},{6,7},{7,6},{8,9},{9,8},{10,11... | collective-permute-start | bytes 1179656 | tf_op jit(solution)/shard_map/ppermute | solution.py:38

commit v10 on v9

--- a/solution.py
+++ b/solution.py
@@ -56,8 +56,10 @@
     )(*args)
 
 
-def project_kernel(img_t_ref, txt_ref, img_proj_ref, txt_proj_ref, parts_ref, pack_ref):
+def project_kernel(scale_ref, bias_ref, img_t_ref, txt_ref, img_proj_ref, txt_proj_ref, parts_ref, pack_ref, scalars_ref):
     groups, share = parts_ref.shape[0], parts_ref.shape[1] // 2
+    scalars_ref[:1] = jnp.full((1, scalars_ref.shape[1]), scale_ref[0], F32)
+    scalars_ref[1:] = jnp.full((1, scalars_ref.shape[1]), bias_ref[0], F32)
     d_txt = txt_ref.shape[1]
     for half in range(d_txt // HALF):
         pack_ref[half * HALF : (half + 1) * HALF] = txt_ref[:, half * HALF : (half + 1) * HALF]
@@ -179,15 +181,17 @@
     d_img, d_txt = image_feats.shape[1], text_feats.shape[1]
     embed = image_proj.shape[1]
     chips = lax.axis_size(CHIPS)
-    parts, pack = call(
+    parts, pack, scalars = call(
         project_kernel,
         "project",
         (
             jax.ShapeDtypeStruct((groups, 2 * share, embed), BF16),
             jax.ShapeDtypeStruct((d_txt + d_img, HALF), BF16),
+            jax.ShapeDtypeStruct((2, STEPS * share), F32),
         ),
-        (image_feats.T, text_feats, image_proj, text_proj),
+        (logit_scale, logit_bias, image_feats.T, text_feats, image_proj, text_proj),
         2 * rows * (d_img + d_txt) * embed,
+        scalars=2,
     )
     second = along_y(pack, 1)
     parts = lax.all_to_all(parts, X, 0, 0, tiled=True)
@@ -197,10 +201,8 @@
         + member * share
         + jnp.arange(share, dtype=jnp.int32)[None, :]
     ).reshape(-1)
-    scale_value, bias_value = logit_scale[0], logit_bias[0]
-    parts, col_ids, scale_value, bias_value = lax.optimization_barrier(
-        (parts, col_ids, scale_value, bias_value)
-    )
+    scale_value, bias_value = scalars[:1], scalars[1:]
+    parts, col_ids = lax.optimization_barrier((parts, col_ids))
     summed = jnp.sum(parts.astype(F32), axis=0)
     length = jnp.sqrt(jnp.sum(summed * summed, axis=1, keepdims=True) + NORM_EPS)
     unit = summed / length
@@ -210,11 +212,12 @@
     img_all = lax.all_to_all(img_all, X, 0, 0, tiled=True).reshape(rows, embed)
     near = shifted(txt_own, 1)
     pair = jnp.concatenate([txt_own, near])
-    pair, second, held = lax.optimization_barrier((pair, second, pack))
+    pair, second, held, col_ids = lax.optimization_barrier((pair, second, pack, col_ids))
     far = shifted(pair, 2)
+    polarity = jnp.where(labels[:, None] == col_ids[None, :], 1.0, -1.0).astype(F32)
+    held, polarity = lax.optimization_barrier((held, polarity))
     third = along_y(held, 2)
     cols = jnp.concatenate([txt_own, far[:share], near, far[share:]])
-    polarity = jnp.where(labels[:, None] == col_ids[None, :], 1.0, -1.0).astype(F32)
     logits = (
         scale_value * lax.dot_general(img_all, cols, ACROSS, preferred_element_type=F32)
         + bias_value

time: 121 us -> 128 us (1.058)
  starting transfers between devices: 63.4 us -> 67.2 us
  waiting for transfers between devices: 41 us -> 43.8 us
    all_to_all x1, starting transfers between devices: 4.79 us -> 12.2 us  [on_device(): lax.all_to_all(img_terms.reshape(groups, share, embed), X, 0, 0, tiled=True)]
    all_to_all x1, starting transfers between devices: 5.45 us -> 3.7 us  [on_device(): wgrad = lax.all_to_all(wgrad, ('yp', 'z'), 0, 0, tiled=True)]
    ppermute x4, starting transfers between devices: 11.7 us -> 10.3 us  [shifted(): return lax.ppermute(value, DP, pairs)]
    all_to_all x1, waiting for transfers between devices: 3.4 us -> 4.87 us  [on_device(): lax.all_to_all(img_terms.reshape(groups, share, embed), X, 0, 0, tiled=True)]
  transfers between devices with their start and end apart: 17 -> 17, of which waited for: 11 -> 11; matrix products, arithmetic and copies ran while one was open for 2% -> 2% of each run, Pallas kernels for 4% -> 3%
where the time goes in v10:
time: 128 us; the launch traced here: 126 us
  starting transfers between devices  67.2 us (52%)
  waiting for transfers between devices  43.8 us (34%)
  Pallas kernels  8.93 us (7%)
  between operations  2.27 us (2%)
  local copies, waits for them, and re-layouts  1.74 us (1%)
  matrix products  1.51 us (1%)
    all_to_all x1, starting transfers between devices, on_device(): lax.all_to_all(img_terms.reshape(groups, share, embed), X, 0, 0, tiled=True)  12.2 us
    ppermute x4, starting transfers between devices, shifted(): return lax.ppermute(value, DP, pairs)  10.3 us
    ppermute x4, starting transfers between devices, swapped(): return lax.ppermute(value, axis, [(0, 1), (1, 0)])  9.69 us
    all_to_all x1, starting transfers between devices, on_device(): parts = lax.all_to_all(parts, X, 0, 0, tiled=True)  9.46 us
    ppermute x4, waiting for transfers between devices, shifted(): return lax.ppermute(value, DP, pairs)  9.28 us
    all_to_all x1, waiting for transfers between devices, on_device(): parts = lax.all_to_all(parts, X, 0, 0, tiled=True)  8.94 us
    pallas_call x5, Pallas kernels, call(): pl.pallas_call(kernel, out_shape=out_shape, in_specs=[pl.BlockSpec(memory...  8.93 us
    ppermute x3, starting transfers between devices, along_y(): return lax.ppermute(value, Y, pairs)  7.48 us
  transfers between devices with their start and end apart: 17, of which 11 were waited for; matrix products, arithmetic and copies ran while one was open for 2% of the time, Pallas kernels for 3%

profile of v10, /device:TPU:6, one launch (start us, length us, event | category | flops | bytes accessed | tf_op | source)
XLA Modules:
  0.0 126.1 jit_solution(8218001033293153572)
XLA Ops:
  1.9 3.1 %project.1 = (bf16[8,64,768]{2,1,0:T(8,128)(2,1)}, bf16[912,256]{1,0:T(8,128)(2,1)}, f32[2,128]{1,0:T(2,128)}) custom-call(f32[1]{0:T(128)S(6)} %copy.12.scale_ref, f32[1]{0:T(128)S(6)} %copy.13.bias_ref, bf16[400,256]{1,0:T(8,128)(2,1)} %bitcast.28, bf16[256,512]{1,0:T(8,128)(2,1)} %txt_ref.1, bf16[400,768]{1,0:T(8,128)(2,1)} %img_proj_ref.3, ...), custom_call_target="tpu_custom_call" | custom-call | flops 358612992 | bytes 4000000 | tf_op jit(solution)/shard_map/project/pallas_call | solution.py:48
  5.0 9.5 %all-to-all-start = ((bf16[8,64,768]{2,1,0:T(8,128)(2,1)}), bf16[8,64,768]{2,1,0:T(8,128)(2,1)S(1)}, u32[]{:S(2)}, u32[]{:S(2)}) async-start(bf16[8,64,768]{2,1,0:T(8,128)(2,1)} %get-tuple-element.28), calls=%async_computation | async-start | bytes 1572864 | tf_op jit(solution)/shard_map/all_to_all | solution.py:197
  14.5 1.9 %collective-permute-start.1 = (bf16[912,256]{1,0:T(8,128)(2,1)S(1)}, bf16[912,256]{1,0:T(8,128)(2,1)S(1)}, u32[]{:S(2)}, u32[]{:S(2)}) collective-permute-start(bf16[912,256]{1,0:T(8,128)(2,1)S(1)} %copy-done.2), channel_id=1, source_target_pairs={{0,448},{64,128},{128,64},{192,256},{256,192},{320,384},{384,320},... | collective-permute-start | bytes 1400840 | tf_op jit(solution)/shard_map/ppermute | solution.py:34
  16.6 8.9 %all-to-all-done = bf16[8,64,768]{2,1,0:T(8,128)(2,1)S(1)} async-done(((bf16[8,64,768]{2,1,0:T(8,128)(2,1)}), bf16[8,64,768]{2,1,0:T(8,128)(2,1)S(1)}, u32[]{:S(2)}, u32[]{:S(2)}) %all-to-all-start) | async-done | bytes 786464 | tf_op jit(solution)/shard_map/all_to_all | solution.py:197
  25.9 1.9 %collective-permute-start = (bf16[32,768]{1,0:T(8,128)(2,1)S(1)}, bf16[32,768]{1,0:T(8,128)(2,1)S(1)}, u32[]{:S(2)}, u32[]{:S(2)}) collective-permute-start(bf16[32,768]{1,0:T(8,128)(2,1)S(1)} %get-tuple-element.58), channel_id=1, source_target_pairs={{0,8},{8,16},{16,24},{24,32},{32,40},{40,48},{48,56},{56,64},{64,7... | collective-permute-start | bytes 147464 | tf_op jit(solution)/shard_map/ppermute | solution.py:24
  28.6 5.5 %all-to-all-start.1 = ((bf16[8,32,768]{2,1,0:T(8,128)(2,1)}), bf16[8,32,768]{2,1,0:T(8,128)(2,1)S(1)}, u32[]{:S(2)}, u32[]{:S(2)}) async-start(bf16[8,32,768]{2,1,0:T(8,128)(2,1)} %broadcast_in_dim.14), calls=%async_computation.1 | async-start | bytes 786432 | tf_op jit(solution)/shard_map/all_to_all | solution.py:212
  34.1 3.2 %collective-permute-done = bf16[32,768]{1,0:T(8,128)(2,1)S(1)} collective-permute-done((bf16[32,768]{1,0:T(8,128)(2,1)S(1)}, bf16[32,768]{1,0:T(8,128)(2,1)S(1)}, u32[]{:S(2)}, u32[]{:S(2)}) %collective-permute-start) | collective-permute-done | bytes 49184 | tf_op jit(solution)/shard_map/ppermute | solution.py:24
  37.3 1.9 %collective-permute-start.2 = (bf16[64,768]{1,0:T(8,128)(2,1)S(1)}, bf16[64,768]{1,0:T(8,128)(2,1)S(1)}, u32[]{:S(2)}, u32[]{:S(2)}) collective-permute-start(bf16[64,768]{1,0:T(8,128)(2,1)S(1)} %pad_maximum_fusion.3), channel_id=1, source_target_pairs={{0,16},{8,24},{16,32},{24,40},{32,48},{40,56},{48,64},{56,72},{64,... | collective-permute-start | bytes 294920 | tf_op jit(solution)/shard_map/ppermute | solution.py:24
  39.4 3.3 %collective-permute-start.3 = (bf16[912,256]{1,0:T(8,128)(2,1)S(1)}, bf16[912,256]{1,0:T(8,128)(2,1)S(1)}, u32[]{:S(2)}, u32[]{:S(2)}) collective-permute-start(bf16[912,256]{1,0:T(8,128)(2,1)S(1)} %copy-done.2), channel_id=1, source_target_pairs={{0,128},{64,448},{128,256},{192,64},{256,384},{320,192},{384,0},{4... | collective-permute-start | bytes 1400840 | tf_op jit(solution)/shard_map/ppermute | solution.py:34
  42.7 6.0 %collective-permute-done.2 = bf16[64,768]{1,0:T(8,128)(2,1)S(1)} collective-permute-done((bf16[64,768]{1,0:T(8,128)(2,1)S(1)}, bf16[64,768]{1,0:T(8,128)(2,1)S(1)}, u32[]{:S(2)}, u32[]{:S(2)}) %collective-permute-start.2) | collective-permute-done | bytes 98336 | tf_op jit(solution)/shard_map/ppermute | solution.py:24
  49.3 4.5 %collective-permute-start.4 = (bf16[64,768]{1,0:T(8,128)(2,1)S(1)}, bf16[64,768]{1,0:T(8,128)(2,1)S(1)}, u32[]{:S(2)}, u32[]{:S(2)}) collective-permute-start(bf16[64,768]{1,0:T(8,128)(2,1)S(1)} %slice.51), channel_id=1, source_target_pairs={{0,504},{8,0},{16,8},{24,16},{32,24},{40,32},{48,40},{56,48},{64,5... | collective-permute-start | bytes 294920 | tf_op jit(solution)/shard_map/ppermute | solution.py:24
  53.8 1.0 convolution_convert_fusion
  54.8 12.2 %all-to-all-start.2 = ((bf16[8,32,768]{2,1,0:T(8,128)(2,1)}), bf16[8,32,768]{2,1,0:T(8,128)(2,1)S(1)}, u32[]{:S(2)}, u32[]{:S(2)}) async-start(bf16[8,32,768]{2,1,0:T(8,128)(2,1)} %bitcast.6), calls=%async_computation.2 | async-start | bytes 786432 | tf_op jit(solution)/shard_map/all_to_all | solution.py:229
  67.0 1.9 %collective-permute-start.5 = (bf16[32,768]{1,0:T(8,128)(2,1)S(1)}, bf16[32,768]{1,0:T(8,128)(2,1)S(1)}, u32[]{:S(2)}, u32[]{:S(2)}) collective-permute-start(bf16[32,768]{1,0:T(8,128)(2,1)S(1)} %slice.52), channel_id=1, source_target_pairs={{0,496},{8,504},{16,0},{24,8},{32,16},{40,24},{48,32},{56,40},{64,... | collective-permute-start | bytes 147464 | tf_op jit(solution)/shard_map/ppermute | solution.py:24
  69.0 4.9 %all-to-all-done.2.img_ref = bf16[8,32,768]{2,1,0:T(8,128)(2,1)S(1)} async-done(((bf16[8,32,768]{2,1,0:T(8,128)(2,1)}), bf16[8,32,768]{2,1,0:T(8,128)(2,1)S(1)}, u32[]{:S(2)}, u32[]{:S(2)}) %all-to-all-start.2) | async-done | bytes 393248 | tf_op jit(solution)/shard_map/all_to_all | solution.py:229
  73.9 1.0 row_grads.1
  74.9 3.4 %all-to-all-start.3 = ((bf16[8,32,384]{2,1,0:T(8,128)(2,1)}), bf16[8,32,384]{2,1,0:T(8,128)(2,1)S(1)}, u32[]{:S(2)}, u32[]{:S(2)}) async-start(bf16[8,32,384]{2,1,0:T(8,128)(2,1)} %get-tuple-element.39), calls=%async_computation.3 | async-start | bytes 393216 | tf_op jit(solution)/shard_map/all_to_all | solution.py:245
  78.3 3.9 %collective-permute-start.6 = (bf16[64,768]{1,0:T(8,128)(2,1)S(1)}, bf16[64,768]{1,0:T(8,128)(2,1)S(1)}, u32[]{:S(2)}, u32[]{:S(2)}) collective-permute-start(bf16[64,768]{1,0:T(8,128)(2,1)S(1)} %get-tuple-element.41.own_ref), channel_id=1, source_target_pairs={{0,4},{4,0},{1,5},{5,1},{2,6},{6,2},{3,7},{7,3},{8,12},{12,8},{9,1... | collective-permute-start | bytes 294920 | tf_op jit(solution)/shard_map/ppermute | solution.py:38
  82.2 4.1 %collective-permute-done.6.high_ref = bf16[64,768]{1,0:T(8,128)(2,1)S(1)} collective-permute-done((bf16[64,768]{1,0:T(8,128)(2,1)S(1)}, bf16[64,768]{1,0:T(8,128)(2,1)S(1)}, u32[]{:S(2)}, u32[]{:S(2)}) %collective-permute-start.6) | collective-permute-done | bytes 98336 | tf_op jit(solution)/shard_map/ppermute | solution.py:38
  86.3 2.4 %all-to-all-done.3 = bf16[8,32,384]{2,1,0:T(8,128)(2,1)S(1)} async-done(((bf16[8,32,384]{2,1,0:T(8,128)(2,1)}), bf16[8,32,384]{2,1,0:T(8,128)(2,1)S(1)}, u32[]{:S(2)}, u32[]{:S(2)}) %all-to-all-start.3) | async-done | bytes 196640 | tf_op jit(solution)/shard_map/all_to_all | solution.py:245
  89.5 5.5 %all-to-all-start.4 = ((bf16[4,128,384]{2,1,0:T(8,128)(2,1)}), bf16[4,128,384]{2,1,0:T(8,128)(2,1)S(1)}, u32[]{:S(2)}, u32[]{:S(2)}) async-start(bf16[4,128,384]{2,1,0:T(8,128)(2,1)} %broadcast_in_dim.15), calls=%async_computation.4 | async-start | bytes 786432 | tf_op jit(solution)/shard_map/all_to_all | solution.py:258
  95.0 2.3 %collective-permute-start.10 = (bf16[912,256]{1,0:T(8,128)(2,1)S(1)}, bf16[912,256]{1,0:T(8,128)(2,1)S(1)}, u32[]{:S(2)}, u32[]{:S(2)}) collective-permute-start(bf16[912,256]{1,0:T(8,128)(2,1)S(1)} %collective-permute-done.1.refs_1_), channel_id=1, source_target_pairs={{0,128},{64,448},{128,256},{192,64},{256,384},{320,192},{384,0},{4... | collective-permute-start | bytes 1400840 | tf_op jit(solution)/shard_map/ppermute | solution.py:34
  97.3 3.0 %all-to-all-done.4.mine_ref = bf16[4,128,384]{2,1,0:T(8,128)(2,1)S(1)} async-done(((bf16[4,128,384]{2,1,0:T(8,128)(2,1)}), bf16[4,128,384]{2,1,0:T(8,128)(2,1)S(1)}, u32[]{:S(2)}, u32[]{:S(2)}) %all-to-all-start.4) | async-done | bytes 393248 | tf_op jit(solution)/shard_map/all_to_all | solution.py:258
  100.3 1.9 %collective-permute-start.9 = (bf16[4,128,384]{2,1,0:T(8,128)(2,1)S(1)}, bf16[4,128,384]{2,1,0:T(8,128)(2,1)S(1)}, u32[]{:S(2)}, u32[]{:S(2)}) collective-permute-start(bf16[4,128,384]{2,1,0:T(8,128)(2,1)S(1)} %all-to-all-done.4.mine_ref), channel_id=1, source_target_pairs={{0,1},{1,0},{2,3},{3,2},{4,5},{5,4},{6,7},{7,6},{8,9},{9,8},{10,11... | collective-permute-start | bytes 1179656 | tf_op jit(solution)/shard_map/ppermute | solution.py:38
  102.3 1.9 %collective-permute-start.7 = (bf16[128,768]{1,0:T(8,128)(2,1)S(1)}, bf16[128,768]{1,0:T(8,128)(2,1)S(1)}, u32[]{:S(2)}, u32[]{:S(2)}) collective-permute-start(bf16[128,768]{1,0:T(8,128)(2,1)S(1)} %pad_maximum_fusion.2), channel_id=1, source_target_pairs={{0,2},{2,0},{1,3},{3,1},{4,6},{6,4},{5,7},{7,5},{8,10},{10,8},{9,1... | collective-permute-start | bytes 589832 | tf_op jit(solution)/shard_map/ppermute | solution.py:38
  104.2 4.8 %collective-permute-done.10.refs_3_ = bf16[912,256]{1,0:T(8,128)(2,1)S(1)} collective-permute-done((bf16[912,256]{1,0:T(8,128)(2,1)S(1)}, bf16[912,256]{1,0:T(8,128)(2,1)S(1)}, u32[]{:S(2)}, u32[]{:S(2)}) %collective-permute-start.10) | collective-permute-done | bytes 466976 | tf_op jit(solution)/shard_map/ppermute | solution.py:34
  109.0 2.9 %project_grads.1 = bf16[16,48,256]{2,1,0:T(8,128)(2,1)} custom-call(s32[1]{0:T(128)} %bitcast.8.core_ref, bf16[4,128,384]{2,1,0:T(8,128)(2,1)S(1)} %all-to-all-done.4.mine_ref, bf16[4,128,384]{2,1,0:T(8,128)(2,1)S(1)} %collective-permute-done.9.other_ref, bf16[912,256]{1,0:T(8,128)(2,1)S(1)} %copy-done.2, ...), custom_call_target="tpu_custom_call" | custom-call | flops 358612992 | bytes 4000000 | tf_op jit(solution)/shard_map/project_grads/pallas_call | solution.py:48
  112.0 3.7 %all-to-all-start.5 = ((bf16[16,48,256]{2,1,0:T(8,128)(2,1)}), bf16[16,48,256]{2,1,0:T(8,128)(2,1)S(1)}, u32[]{:S(2)}, u32[]{:S(2)}) async-start(bf16[16,48,256]{2,1,0:T(8,128)(2,1)} %project_grads.1), calls=%async_computation.5 | async-start | bytes 786432 | tf_op jit(solution)/shard_map/all_to_all | solution.py:279
  115.7 1.9 %collective-permute-start.8 = (bf16[256,768]{1,0:T(8,128)(2,1)S(1)}, bf16[256,768]{1,0:T(8,128)(2,1)S(1)}, u32[]{:S(2)}, u32[]{:S(2)}) collective-permute-start(bf16[256,768]{1,0:T(8,128)(2,1)S(1)} %pad_maximum_fusion), channel_id=1, source_target_pairs={{0,1},{1,0},{2,3},{3,2},{4,5},{5,4},{6,7},{7,6},{8,9},{9,8},{10,11... | collective-permute-start | bytes 1179656 | tf_op jit(solution)/shard_map/ppermute | solution.py:38
  117.7 1.7 %collective-permute-done.8.core_ref = bf16[256,768]{1,0:T(8,128)(2,1)S(1)} collective-permute-done((bf16[256,768]{1,0:T(8,128)(2,1)S(1)}, bf16[256,768]{1,0:T(8,128)(2,1)S(1)}, u32[]{:S(2)}, u32[]{:S(2)}) %collective-permute-start.8) | collective-permute-done | bytes 393248 | tf_op jit(solution)/shard_map/ppermute | solution.py:38
  119.4 1.2 feature_grads.1
  120.6 4.8 %all-to-all-done.5.blocks_ref = bf16[16,48,256]{2,1,0:T(8,128)(2,1)S(1)} async-done(((bf16[16,48,256]{2,1,0:T(8,128)(2,1)}), bf16[16,48,256]{2,1,0:T(8,128)(2,1)S(1)}, u32[]{:S(2)}, u32[]{:S(2)}) %all-to-all-start.5) | async-done | bytes 393248 | tf_op jit(solution)/shard_map/all_to_all | solution.py:279
  (43 shorter events, 3.6 us)
Async XLA Ops:
  5.0 9.5 %copy-start.2 = (bf16[912,256]{1,0:T(8,128)(2,1)S(1)}, bf16[912,256]{1,0:T(8,128)(2,1)}, u32[]{:S(2)}) copy-start(bf16[912,256]{1,0:T(8,128)(2,1)} %get-tuple-element.37.refs_0_) | copy-start | bytes 1400836
  5.0 11.4 %copy-start.5 = (s32[4]{0:T(128)S(1)}, s32[4]{0:T(128)}, u32[]{:S(2)}) copy-start(s32[4]{0:T(128)} %constant.81) | copy-start | bytes 52
  5.0 20.5 %all-to-all-start = ((bf16[8,64,768]{2,1,0:T(8,128)(2,1)}), bf16[8,64,768]{2,1,0:T(8,128)(2,1)S(1)}, u32[]{:S(2)}, u32[]{:S(2)}) async-start(bf16[8,64,768]{2,1,0:T(8,128)(2,1)} %get-tuple-element.28), calls=%async_computation | async-start | bytes 1572864 | tf_op jit(solution)/shard_map/all_to_all | solution.py:197
  14.5 22.8 %collective-permute-start.1 = (bf16[912,256]{1,0:T(8,128)(2,1)S(1)}, bf16[912,256]{1,0:T(8,128)(2,1)S(1)}, u32[]{:S(2)}, u32[]{:S(2)}) collective-permute-start(bf16[912,256]{1,0:T(8,128)(2,1)S(1)} %copy-done.2), channel_id=1, source_target_pairs={{0,448},{64,128},{128,64},{192,256},{256,192},{320,384},{384,320},... | collective-permute-start | bytes 1400840 | tf_op jit(solution)/shard_map/ppermute | solution.py:34
  16.6 11.2 %copy-start.4 = (f32[2,128]{1,0:T(2,128)S(1)}, f32[2,128]{1,0:T(2,128)}, u32[]{:S(2)}) copy-start(f32[2,128]{1,0:T(2,128)} %get-tuple-element.30) | copy-start | bytes 3076
  25.9 13.4 %copy-start.3 = (s32[256]{0:T(256)S(1)}, s32[256]{0:T(256)}, u32[]{:S(2)}) copy-start(s32[256]{0:T(256)} %param.12) | copy-start | bytes 3076
  25.9 11.4 %collective-permute-start = (bf16[32,768]{1,0:T(8,128)(2,1)S(1)}, bf16[32,768]{1,0:T(8,128)(2,1)S(1)}, u32[]{:S(2)}, u32[]{:S(2)}) collective-permute-start(bf16[32,768]{1,0:T(8,128)(2,1)S(1)} %get-tuple-element.58), channel_id=1, source_target_pairs={{0,8},{8,16},{16,24},{24,32},{32,40},{40,48},{48,56},{56,64},{64,7... | collective-permute-start | bytes 147464 | tf_op jit(solution)/shard_map/ppermute | solution.py:24
  28.6 20.1 %all-to-all-start.1 = ((bf16[8,32,768]{2,1,0:T(8,128)(2,1)}), bf16[8,32,768]{2,1,0:T(8,128)(2,1)S(1)}, u32[]{:S(2)}, u32[]{:S(2)}) async-start(bf16[8,32,768]{2,1,0:T(8,128)(2,1)} %broadcast_in_dim.14), calls=%async_computation.1 | async-start | bytes 786432 | tf_op jit(solution)/shard_map/all_to_all | solution.py:212
  37.3 11.4 %collective-permute-start.2 = (bf16[64,768]{1,0:T(8,128)(2,1)S(1)}, bf16[64,768]{1,0:T(8,128)(2,1)S(1)}, u32[]{:S(2)}, u32[]{:S(2)}) collective-permute-start(bf16[64,768]{1,0:T(8,128)(2,1)S(1)} %pad_maximum_fusion.3), channel_id=1, source_target_pairs={{0,16},{8,24},{16,32},{24,40},{32,48},{40,56},{48,64},{56,72},{64,... | collective-permute-start | bytes 294920 | tf_op jit(solution)/shard_map/ppermute | solution.py:24
  39.4 29.6 %collective-permute-start.3 = (bf16[912,256]{1,0:T(8,128)(2,1)S(1)}, bf16[912,256]{1,0:T(8,128)(2,1)S(1)}, u32[]{:S(2)}, u32[]{:S(2)}) collective-permute-start(bf16[912,256]{1,0:T(8,128)(2,1)S(1)} %copy-done.2), channel_id=1, source_target_pairs={{0,128},{64,448},{128,256},{192,64},{256,384},{320,192},{384,0},{4... | collective-permute-start | bytes 1400840 | tf_op jit(solution)/shard_map/ppermute | solution.py:34
  49.3 17.7 %collective-permute-start.4 = (bf16[64,768]{1,0:T(8,128)(2,1)S(1)}, bf16[64,768]{1,0:T(8,128)(2,1)S(1)}, u32[]{:S(2)}, u32[]{:S(2)}) collective-permute-start(bf16[64,768]{1,0:T(8,128)(2,1)S(1)} %slice.51), channel_id=1, source_target_pairs={{0,504},{8,0},{16,8},{24,16},{32,24},{40,32},{48,40},{56,48},{64,5... | collective-permute-start | bytes 294920 | tf_op jit(solution)/shard_map/ppermute | solution.py:24
  54.8 19.1 %all-to-all-start.2 = ((bf16[8,32,768]{2,1,0:T(8,128)(2,1)}), bf16[8,32,768]{2,1,0:T(8,128)(2,1)S(1)}, u32[]{:S(2)}, u32[]{:S(2)}) async-start(bf16[8,32,768]{2,1,0:T(8,128)(2,1)} %bitcast.6), calls=%async_computation.2 | async-start | bytes 786432 | tf_op jit(solution)/shard_map/all_to_all | solution.py:229
  67.0 6.9 %collective-permute-start.5 = (bf16[32,768]{1,0:T(8,128)(2,1)S(1)}, bf16[32,768]{1,0:T(8,128)(2,1)S(1)}, u32[]{:S(2)}, u32[]{:S(2)}) collective-permute-start(bf16[32,768]{1,0:T(8,128)(2,1)S(1)} %slice.52), channel_id=1, source_target_pairs={{0,496},{8,504},{16,0},{24,8},{32,16},{40,24},{48,32},{56,40},{64,... | collective-permute-start | bytes 147464 | tf_op jit(solution)/shard_map/ppermute | solution.py:24
  74.9 13.8 %all-to-all-start.3 = ((bf16[8,32,384]{2,1,0:T(8,128)(2,1)}), bf16[8,32,384]{2,1,0:T(8,128)(2,1)S(1)}, u32[]{:S(2)}, u32[]{:S(2)}) async-start(bf16[8,32,384]{2,1,0:T(8,128)(2,1)} %get-tuple-element.39), calls=%async_computation.3 | async-start | bytes 393216 | tf_op jit(solution)/shard_map/all_to_all | solution.py:245
  78.3 8.0 %collective-permute-start.6 = (bf16[64,768]{1,0:T(8,128)(2,1)S(1)}, bf16[64,768]{1,0:T(8,128)(2,1)S(1)}, u32[]{:S(2)}, u32[]{:S(2)}) collective-permute-start(bf16[64,768]{1,0:T(8,128)(2,1)S(1)} %get-tuple-element.41.own_ref), channel_id=1, source_target_pairs={{0,4},{4,0},{1,5},{5,1},{2,6},{6,2},{3,7},{7,3},{8,12},{12,8},{9,1... | collective-permute-start | bytes 294920 | tf_op jit(solution)/shard_map/ppermute | solution.py:38
  89.5 10.8 %all-to-all-start.4 = ((bf16[4,128,384]{2,1,0:T(8,128)(2,1)}), bf16[4,128,384]{2,1,0:T(8,128)(2,1)S(1)}, u32[]{:S(2)}, u32[]{:S(2)}) async-start(bf16[4,128,384]{2,1,0:T(8,128)(2,1)} %broadcast_in_dim.15), calls=%async_computation.4 | async-start | bytes 786432 | tf_op jit(solution)/shard_map/all_to_all | solution.py:258
  95.0 14.0 %collective-permute-start.10 = (bf16[912,256]{1,0:T(8,128)(2,1)S(1)}, bf16[912,256]{1,0:T(8,128)(2,1)S(1)}, u32[]{:S(2)}, u32[]{:S(2)}) collective-permute-start(bf16[912,256]{1,0:T(8,128)(2,1)S(1)} %collective-permute-done.1.refs_1_), channel_id=1, source_target_pairs={{0,128},{64,448},{128,256},{192,64},{256,384},{320,192},{384,0},{4... | collective-permute-start | bytes 1400840 | tf_op jit(solution)/shard_map/ppermute | solution.py:34
  100.3 8.7 %collective-permute-start.9 = (bf16[4,128,384]{2,1,0:T(8,128)(2,1)S(1)}, bf16[4,128,384]{2,1,0:T(8,128)(2,1)S(1)}, u32[]{:S(2)}, u32[]{:S(2)}) collective-permute-start(bf16[4,128,384]{2,1,0:T(8,128)(2,1)S(1)} %all-to-all-done.4.mine_ref), channel_id=1, source_target_pairs={{0,1},{1,0},{2,3},{3,2},{4,5},{5,4},{6,7},{7,6},{8,9},{9,8},{10,11... | collective-permute-start | bytes 1179656 | tf_op jit(solution)/shard_map/ppermute | solution.py:38
  102.3 13.4 %collective-permute-start.7 = (bf16[128,768]{1,0:T(8,128)(2,1)S(1)}, bf16[128,768]{1,0:T(8,128)(2,1)S(1)}, u32[]{:S(2)}, u32[]{:S(2)}) collective-permute-start(bf16[128,768]{1,0:T(8,128)(2,1)S(1)} %pad_maximum_fusion.2), channel_id=1, source_target_pairs={{0,2},{2,0},{1,3},{3,1},{4,6},{6,4},{5,7},{7,5},{8,10},{10,8},{9,1... | collective-permute-start | bytes 589832 | tf_op jit(solution)/shard_map/ppermute | solution.py:38
  112.0 7.4 %copy-start = (bf16[512,768]{1,0:T(8,128)(2,1)S(1)}, bf16[512,768]{1,0:T(8,128)(2,1)}, u32[]{:S(2)}) copy-start(bf16[512,768]{1,0:T(8,128)(2,1)} %txt_proj_ref.3) | copy-start | bytes 2359300
  112.0 7.4 %copy-start.1 = (bf16[400,768]{1,0:T(8,128)(2,1)S(1)}, bf16[400,768]{1,0:T(8,128)(2,1)}, u32[]{:S(2)}) copy-start(bf16[400,768]{1,0:T(8,128)(2,1)} %img_proj_ref.3) | copy-start | bytes 1843204
  112.0 13.4 %all-to-all-start.5 = ((bf16[16,48,256]{2,1,0:T(8,128)(2,1)}), bf16[16,48,256]{2,1,0:T(8,128)(2,1)S(1)}, u32[]{:S(2)}, u32[]{:S(2)}) async-start(bf16[16,48,256]{2,1,0:T(8,128)(2,1)} %project_grads.1), calls=%async_computation.5 | async-start | bytes 786432 | tf_op jit(solution)/shard_map/all_to_all | solution.py:279
  115.7 3.6 %collective-permute-start.8 = (bf16[256,768]{1,0:T(8,128)(2,1)S(1)}, bf16[256,768]{1,0:T(8,128)(2,1)S(1)}, u32[]{:S(2)}, u32[]{:S(2)}) collective-permute-start(bf16[256,768]{1,0:T(8,128)(2,1)S(1)} %pad_maximum_fusion), channel_id=1, source_target_pairs={{0,1},{1,0},{2,3},{3,2},{4,5},{5,4},{6,7},{7,6},{8,9},{9,8},{10,11... | collective-permute-start | bytes 1179656 | tf_op jit(solution)/shard_map/ppermute | solution.py:38
